TPU v7x, 32 devices: a whole 2x2x4 slice. The times are simulated.
32 devices in a mesh: seg: 4 (over x, core), chan: 8 (over z, y).
Axes of the slice: x: 2, y: 2, z: 4, core: 2. Of those that a mesh axis runs over, the one named last changes fastest.
Arguments:
- traces: bfloat16 [32, 1024, 4096], P('seg', 'chan'), may hold values from -6 to 6
- channel_mask: int32 [1024], P('chan'), may hold values 0 or 1
- owner_ids: int32 [8, 64, 1], P('chan'), may hold values from 0 to 7; in each aligned block of 64 rows (0 to 63, 64 to 127, ..., all dimensions but the last counted through in order) at most 16 rows name the same one
- local_bins: int32 [8, 64], P('chan'), may hold values from 0 to 7
Outputs:
- stacks: float32 [64, 2048], P('chan')
Inputs may be any that keep to these rules, and one draw needn't show every extreme that they name: `owner_ids`: among the 64 tiles of one block no owner is named more than 16 times, a bound that some block reaches.
All inputs are finite; a program needn't handle non-finite values. No bound on the sum of `channel_mask` on one device may be relied on, other than what follows from the above.
Results may differ from a plain program's by a relative error of at most 0.0053.
Values may be sent and summed in bfloat16 or wider, within the bound.
No kernel may reach another device: no remote copies, remote signals or barrier semaphores. Data moves between devices by JAX's collectives and lax.ppermute only.
A program may use at most 192 MiB of HBM per device.

v0:
```python
import math

import jax
import jax.numpy as jnp
from jax import lax
from jax.sharding import PartitionSpec as P

NT = 4096
DEC = 2
K0 = 8
HW = 64
R = 4
G = 16
BIN_DEV = 8
NB = 1024
NLAG = 2048


EPSILON = 1e-06


def passed_along(block, axis, distance):
    devices = range(lax.axis_size(axis))
    route = [(i - distance, i) for i in devices if i - distance in devices]
    return lax.ppermute(block, axis, route)


def forward_table():
    samples = jnp.arange(NT, dtype=jnp.int32)
    freqs = K0 + jnp.arange(NB, dtype=jnp.int32)
    phase = samples[:, None] * freqs[None, :] % NT
    angle = phase.astype(jnp.float32) * (2.0 * math.pi / NT)
    return jnp.concatenate([jnp.cos(angle), -jnp.sin(angle)], axis=1).astype(jnp.bfloat16)


def band_table():
    freqs = jnp.arange(NB, dtype=jnp.int32)
    return (jnp.abs(freqs[:, None] - freqs[None, :]) <= HW).astype(jnp.float32)


def inverse_rows(first_bin, bin_count):
    freqs = K0 + first_bin + jnp.arange(bin_count, dtype=jnp.int32)
    delays = (jnp.arange(NLAG, dtype=jnp.int32) - NLAG // 2) * DEC
    phase = jnp.mod(freqs[:, None] * delays[None, :], NT)
    angle = phase.astype(jnp.float32) * (2.0 * math.pi / NT)
    scale = 1.0 / math.sqrt(NB)
    return jnp.concatenate([jnp.cos(angle) * scale, -jnp.sin(angle) * scale], axis=0)


def inverse_table():
    return inverse_rows(0, NB)


def whiten(block, mask_float, table, band):
    segs, chans, length = block.shape
    spectrum = jnp.dot(
        block.reshape(segs * chans, length), table, preferred_element_type=jnp.float32
    )
    half = spectrum.shape[1] // 2
    real_part = spectrum[:, :half]
    imag_part = spectrum[:, half:]
    power = real_part * real_part + imag_part * imag_part
    counts = jnp.sum(band, axis=0)
    level = jnp.sqrt(jnp.dot(power, band, precision=lax.Precision.HIGHEST) / counts + EPSILON)
    weight = jnp.tile(mask_float, segs)[:, None] / level
    result = jnp.concatenate([real_part * weight, imag_part * weight], axis=1)
    return result.astype(jnp.bfloat16).reshape(segs, chans, 2 * half)


def cross(source, source_mask, target, target_mask, total_segs):
    half = source.shape[-1] // 2
    source_float = source.astype(jnp.float32)
    target_float = target.astype(jnp.float32)
    source_real = source_float[..., :half]
    source_imag = source_float[..., half:]
    target_real = target_float[..., :half]
    target_imag = target_float[..., half:]
    real_sum = jnp.sum(source_real * target_real + source_imag * target_imag, axis=0)
    imag_sum = jnp.sum(source_imag * target_real - source_real * target_imag, axis=0)
    chans = real_sum.shape[0]
    real_groups = real_sum.reshape(G, chans // G, half).sum(axis=1)
    imag_groups = imag_sum.reshape(G, chans // G, half).sum(axis=1)
    counts = (source_mask * target_mask).reshape(G, chans // G).sum(axis=1)
    scale = 1.0 / (total_segs * jnp.maximum(counts, 1.0))
    return jnp.concatenate([real_groups, imag_groups], axis=1) * scale[:, None]


def per_device(traces, channel_mask, owner_ids, local_bins):
    seg_count = lax.axis_size("seg")
    chan_count = lax.axis_size("chan")
    total_segs = traces.shape[0] * seg_count
    mask_float = channel_mask.astype(jnp.float32)
    whitened = whiten(traces, mask_float, forward_table(), band_table())
    mask_half = mask_float.astype(jnp.bfloat16)
    pieces = []
    for offset in range(1, R + 1):
        far_spectra, far_mask = passed_along((whitened, mask_half), "chan", -offset)
        pieces.append(
            cross(whitened, mask_float, far_spectra, far_mask.astype(jnp.float32), total_segs)
        )
    tiles = jnp.concatenate(pieces, axis=0)
    tiles = lax.psum(tiles, "seg")
    payload = jnp.dot(tiles, inverse_table(), precision=lax.Precision.HIGHEST)
    width = payload.shape[1]
    tile_count = payload.shape[0]
    capacity = 2 * tile_count // chan_count
    destination = owner_ids.reshape(-1)
    wanted_bins = local_bins.reshape(-1).astype(jnp.float32)
    onehot = (destination[:, None] == jnp.arange(chan_count, dtype=jnp.int32)[None, :]).astype(
        jnp.int32
    )
    earlier = jnp.cumsum(onehot, axis=0) - onehot
    slot_index = jnp.sum(earlier * onehot, axis=1)
    outgoing = (
        jnp.zeros((chan_count, capacity, width), jnp.float32)
        .at[destination, slot_index]
        .set(payload)
    )
    labels = (
        jnp.full((chan_count, capacity), -1.0, jnp.float32)
        .at[destination, slot_index]
        .set(wanted_bins)
    )
    arrived, arrived_labels = (
        lax.all_to_all(outgoing, "chan", split_axis=0, concat_axis=0, tiled=True),
        lax.all_to_all(labels, "chan", split_axis=0, concat_axis=0, tiled=True),
    )
    selector = (
        arrived_labels.reshape(1, -1) == jnp.arange(BIN_DEV, dtype=jnp.float32)[:, None]
    ).astype(jnp.float32)
    stacked = jnp.dot(selector, arrived.reshape(-1, width), precision=lax.Precision.HIGHEST)
    return stacked


def solution(mesh):
    in_specs = (P("seg", "chan", None), P("chan"), P("chan", None, None), P("chan", None))
    out_specs = P("chan", None)
    return jax.shard_map(
        per_device, mesh=mesh, in_specs=in_specs, out_specs=out_specs, check_vma=False
    )
```

profile of v0, /device:TPU:0, one launch (start us, length us, event | category | flops | bytes accessed | tf_op | source)
XLA Modules:
  0.0 838.9 jit_solution(15956323783574124742)
XLA Ops:
  6.8 67.5 %cosine_convert_fusion = (bf16[4096,1024]{1,0:T(8,128)(2,1)S(1)}, bf16[4096,1024]{1,0:T(8,128)(2,1)S(1)}) fusion(s32[1024]{0:T(1024)S(1)} %iota_add_fusion), kind=kLoop, calls=%fused_computation.17 | loop fusion | flops 71303168 | bytes 16781312 | tf_op jit(solution)/shard_map/convert.4
  74.3 22.2 %fusion.17 = f32[1024,2048]{1,0:T(8,128)} fusion(bf16[1024,4096]{1,0:T(8,128)(2,1)} %bitcast.48, bf16[4096,1024]{1,0:T(8,128)(2,1)S(1)} %get-tuple-element.28, bf16[4096,1024]{1,0:T(8,128)(2,1)S(1)} %get-tuple-element.27), kind=kOutput, calls=%fused_computation.31 | convolution fusion | flops 17213423616 | bytes 33554432 | tf_op jit(solution)/shard_map/dot_general | solution.py:56
  96.5 14.5 %multiply_convert_fusion.1 = (bf16[1024,1024]{1,0:T(8,128)(2,1)S(1)}, bf16[1024,1024]{1,0:T(8,128)(2,1)S(1)}) fusion(f32[1024,2048]{1,0:T(8,128)} %fusion.17, f32[1024]{0:T(1024)S(1)} %convert_reduce_fusion, f32[1024]{0:T(1024)S(1)} %broadcast_bitcast_fusion), kind=kOutput, calls=%fused_computation.42 | convolution fusion | flops 12898533376 | bytes 20979712 | tf_op jit(solution)/shard_map/dot_general | solution.py:64
  111.0 5.2 fusion.37
  117.5 1.3 collective-permute-start.2
  118.8 1.3 collective-permute-start.4
  120.1 1.3 collective-permute-start.6
  123.1 88.9 %collective-permute-done.1 = bf16[128]{0:T(256)(128)(2,1)S(1)} collective-permute-done((bf16[128]{0:T(256)(128)(2,1)S(1)}, bf16[128]{0:T(256)(128)(2,1)S(1)}, u32[]{:S(2)}, u32[]{:S(2)}) %collective-permute-start.1) | collective-permute-done | bytes 288 | tf_op jit(solution)/shard_map/ppermute | solution.py:25
  213.3 92.8 %collective-permute-done.3 = bf16[128]{0:T(256)(128)(2,1)S(1)} collective-permute-done((bf16[128]{0:T(256)(128)(2,1)S(1)}, bf16[128]{0:T(256)(128)(2,1)S(1)}, u32[]{:S(2)}, u32[]{:S(2)}) %collective-permute-start.3) | collective-permute-done | bytes 288 | tf_op jit(solution)/shard_map/ppermute | solution.py:25
  308.0 10.2 %scatter_fusion = f32[8,16]{1,0:T(8,128)} fusion(f32[8,16]{1,0:T(8,128)} %broadcast_in_dim.4, s32[64]{0:T(128)S(1)} %fusion.33, f32[64]{0:T(128)S(1)} %convert_bitcast_fusion), kind=kCustom, calls=%fused_computation | custom fusion | bytes 1280 | tf_op jit(solution)/shard_map/scatter | solution.py:122
  318.2 368.5 %all-to-all-start = ((f32[8,1,16]{2,1,0:T(1,128)}), f32[8,1,16]{2,1,0:T(1,128)S(1)}, u32[]{:S(2)}, u32[]{:S(2)}) async-start(f32[8,1,16]{2,1,0:T(1,128)} %bitcast.6), calls=%async_computation | async-start | bytes 8192 | tf_op jit(solution)/shard_map/all_to_all | solution.py:126
  686.8 1.3 collective-permute-start.7
  688.1 5.0 collective-permute-done.7
  694.0 6.5 convert_element_type.69
  700.5 6.5 convert_element_type.72
  706.9 6.5 convert_element_type.74
  713.4 6.5 convert_element_type.76
  719.9 17.5 %add_reduce_fusion.3 = (f32[128,1024]{1,0:T(8,128)}, f32[128,1024]{1,0:T(8,128)}, f32[128,1024]{1,0:T(8,128)S(1)}, f32[128,1024]{1,0:T(8,128)S(1)}, f32[128,1024...) fusion(f32[8,128,2048]{2,1,0:T(8,128)} %convert_element_type.69, ...), kind=kLoop, calls=%fused_computation.40 | loop fusion | flops 32505856 | bytes 46137344 | tf_op jit(solution)/shard_map/reduce_sum | solution.py:78
  737.4 1.5 bitcast_reduce_fusion.6
  740.9 35.6 %cosine_multiply_fusion = (f32[1024,2048]{1,0:T(8,128)}, f32[1024,2048]{1,0:T(8,128)}) fusion(s32[2048]{0:T(1024)S(1)} %add_multiply_fusion, s32[1024]{0:T(1024)S(1)} %iota_add_fusion), kind=kLoop, calls=%fused_computation.30 | loop fusion | flops 35651584 | bytes 16789504 | tf_op jit(solution)/shard_map/mul | solution.py:47
  776.5 13.9 %fusion.7 = f32[64,2048]{1,0:T(8,128)S(1)} fusion(f32[64,2048]{1,0:T(8,128)} %all-reduce.2.cloned.1.call-done, f32[1024,2048]{1,0:T(8,128)} %get-tuple-element.26, f32[1024,2048]{1,0:T(8,128)} %get-tuple-element.25), kind=kOutput, calls=%fused_computation.12 | convolution fusion | flops 3225419776 | bytes 17825792 | tf_op jit(solution)/shard_map/dot_general | solution.py:103
  791.6 11.4 %scatter_fusion.1 = f32[8,16,2048]{2,1,0:T(8,128)} fusion(f32[8,16,2048]{2,1,0:T(8,128)} %broadcast_in_dim.5, s32[64]{0:T(128)S(1)} %fusion.33, f32[64,2048]{1,0:T(8,128)S(1)} %fusion.7), kind=kCustom, calls=%fused_computation.1 | custom fusion | bytes 1573376 | tf_op jit(solution)/shard_map/scatter | solution.py:117
  802.9 4.3 all-to-all-start.1
  808.5 22.5 %all-to-all-done.1 = f32[8,16,2048]{2,1,0:T(8,128)S(1)} async-done(((f32[8,16,2048]{2,1,0:T(8,128)}), f32[8,16,2048]{2,1,0:T(8,128)S(1)}, u32[]{:S(2)}, u32[]{:S(2)}) %all-to-all-start.1) | async-done | bytes 1048608 | tf_op jit(solution)/shard_map/all_to_all | solution.py:125
  (56 shorter events, 12.7 us)
Async XLA Ops:
  6.8 67.5 %copy-start.1 = (s32[128]{0:T(128)S(1)}, s32[128]{0:T(128)}, u32[]{:S(2)}) copy-start(s32[128]{0:T(128)} %param.5) | copy-start | bytes 1540
  111.0 11.7 %copy-start = (s32[1,64,1]{1,2,0:T(1,128)S(1)}, s32[1,64,1]{1,2,0:T(1,128)}, u32[]{:S(2)}) copy-start(s32[1,64,1]{1,2,0:T(1,128)} %param.6) | copy-start | bytes 772
  111.0 102.3 %copy-start.2 = (s32[1,64]{1,0:T(1,128)S(1)}, s32[1,64]{1,0:T(1,128)}, u32[]{:S(2)}) copy-start(s32[1,64]{1,0:T(1,128)} %param.7) | copy-start | bytes 772
  116.3 577.7 %collective-permute-start = (bf16[8,128,2048]{2,1,0:T(8,128)(2,1)}, bf16[8,128,2048]{2,1,0:T(8,128)(2,1)}, u32[]{:S(2)}, u32[]{:S(2)}) collective-permute-start(bf16[8,128,2048]{2,1,0:T(8,128)(2,1)} %get-tuple-element.24), channel_id=1, source_target_pairs={{1,0},{2,1},{3,2},{4,3},{5,4},{6,5},{7,6},{9,8},{10,9},{11,10},{12... | collective-permute-start | bytes 12582920 | tf_op jit(solution)/shard_map/ppermute | solution.py:25
  117.5 582.9 %collective-permute-start.2 = (bf16[8,128,2048]{2,1,0:T(8,128)(2,1)}, bf16[8,128,2048]{2,1,0:T(8,128)(2,1)}, u32[]{:S(2)}, u32[]{:S(2)}) collective-permute-start(bf16[8,128,2048]{2,1,0:T(8,128)(2,1)} %get-tuple-element.24), channel_id=1, source_target_pairs={{2,0},{3,1},{4,2},{5,3},{6,4},{7,5},{10,8},{11,9},{12,10},{13,11},... | collective-permute-start | bytes 12582920 | tf_op jit(solution)/shard_map/ppermute | solution.py:25
  118.8 588.1 %collective-permute-start.4 = (bf16[8,128,2048]{2,1,0:T(8,128)(2,1)}, bf16[8,128,2048]{2,1,0:T(8,128)(2,1)}, u32[]{:S(2)}, u32[]{:S(2)}) collective-permute-start(bf16[8,128,2048]{2,1,0:T(8,128)(2,1)} %get-tuple-element.24), channel_id=1, source_target_pairs={{3,0},{4,1},{5,2},{6,3},{7,4},{11,8},{12,9},{13,10},{14,11},{15,12... | collective-permute-start | bytes 12582920 | tf_op jit(solution)/shard_map/ppermute | solution.py:25
  120.1 593.3 %collective-permute-start.6 = (bf16[8,128,2048]{2,1,0:T(8,128)(2,1)}, bf16[8,128,2048]{2,1,0:T(8,128)(2,1)}, u32[]{:S(2)}, u32[]{:S(2)}) collective-permute-start(bf16[8,128,2048]{2,1,0:T(8,128)(2,1)} %get-tuple-element.24), channel_id=1, source_target_pairs={{4,0},{5,1},{6,2},{7,3},{12,8},{13,9},{14,10},{15,11},{20,16},{21,... | collective-permute-start | bytes 12582920 | tf_op jit(solution)/shard_map/ppermute | solution.py:25
  121.4 90.6 %collective-permute-start.1 = (bf16[128]{0:T(256)(128)(2,1)S(1)}, bf16[128]{0:T(256)(128)(2,1)S(1)}, u32[]{:S(2)}, u32[]{:S(2)}) collective-permute-start(bf16[128]{0:T(256)(128)(2,1)S(1)} %get-tuple-element.33), channel_id=1, source_target_pairs={{1,0},{2,1},{3,2},{4,3},{5,4},{6,5},{7,6},{9,8},{10,9},{11,10},{12... | collective-permute-start | bytes 776 | tf_op jit(solution)/shard_map/ppermute | solution.py:25
  212.0 94.1 %collective-permute-start.3 = (bf16[128]{0:T(256)(128)(2,1)S(1)}, bf16[128]{0:T(256)(128)(2,1)S(1)}, u32[]{:S(2)}, u32[]{:S(2)}) collective-permute-start(bf16[128]{0:T(256)(128)(2,1)S(1)} %get-tuple-element.33), channel_id=1, source_target_pairs={{2,0},{3,1},{4,2},{5,3},{6,4},{7,5},{10,8},{11,9},{12,10},{13,11},... | collective-permute-start | bytes 776 | tf_op jit(solution)/shard_map/ppermute | solution.py:25
  306.1 380.7 %collective-permute-start.5 = (bf16[128]{0:T(256)(128)(2,1)S(1)}, bf16[128]{0:T(256)(128)(2,1)S(1)}, u32[]{:S(2)}, u32[]{:S(2)}) collective-permute-start(bf16[128]{0:T(256)(128)(2,1)S(1)} %get-tuple-element.33), channel_id=1, source_target_pairs={{3,0},{4,1},{5,2},{6,3},{7,4},{11,8},{12,9},{13,10},{14,11},{15,12... | collective-permute-start | bytes 776 | tf_op jit(solution)/shard_map/ppermute | solution.py:25
  318.2 484.8 %all-to-all-start = ((f32[8,1,16]{2,1,0:T(1,128)}), f32[8,1,16]{2,1,0:T(1,128)S(1)}, u32[]{:S(2)}, u32[]{:S(2)}) async-start(f32[8,1,16]{2,1,0:T(1,128)} %bitcast.6), calls=%async_computation | async-start | bytes 8192 | tf_op jit(solution)/shard_map/all_to_all | solution.py:126
  686.7 89.8 %all-reduce.2.cloned.1.call-start = ((), (), s32[]{:S(2)}) async-start(), calls=%async_computation.2 | async-start | bytes 1048576 | tf_op jit(solution)/shard_map/psum | solution.py:102
  686.8 6.3 collective-permute-start.7
  802.9 28.1 %all-to-all-start.1 = ((f32[8,16,2048]{2,1,0:T(8,128)}), f32[8,16,2048]{2,1,0:T(8,128)S(1)}, u32[]{:S(2)}, u32[]{:S(2)}) async-start(f32[8,16,2048]{2,1,0:T(8,128)} %scatter_fusion.1), calls=%async_computation.1 | async-start | bytes 2097152 | tf_op jit(solution)/shard_map/all_to_all | solution.py:125
Sparse Core Ops, SparseCore 0:
  741.0 32.8 all-reduce.1
where the time goes:
time: 840 us; the launch traced here: 839 us
  starting transfers between devices  383 us (46%)
  waiting for transfers between devices  209 us (25%)
  other arithmetic  157 us (19%)
  matrix products  51.7 us (6%)
  local copies, waits for them, and re-layouts  24.2 us (3%)
  between operations  13.7 us (2%)
    all_to_all x1, starting transfers between devices, per_device(): lax.all_to_all(labels, 'chan', split_axis=0, concat_axis=0, tiled=True)  369 us
    ppermute x8, waiting for transfers between devices, passed_along(): return lax.ppermute(block, axis, route)  187 us
    another operation x1, other arithmetic  67.5 us
    mul x1, other arithmetic, inverse_rows(): jnp.cos(angle) * scale  35.6 us
    convert_element_type x4, other arithmetic, cross(): target_float = target.astype(jnp.float32)  25.9 us
    all_to_all x1, waiting for transfers between devices, per_device(): lax.all_to_all(outgoing, 'chan', split_axis=0, concat_axis=0, tiled=True)  22.5 us
    dot_general x1, matrix products, whiten(): jnp.dot(block.reshape(segs * chans, length), table, preferred_element_typ...  22.2 us
    reduce_sum x1, other arithmetic, cross(): jnp.sum(source_real * target_real + source_imag * target_imag, axis=0)  17.5 us
  transfers between devices with their start and end apart: 11, of which 4 were waited for; matrix products, arithmetic and copies ran while one was open for 15% of the time, Pallas kernels for 0%

commit v1 on v0

v1 whole, which is shorter than its diff:
```python
import functools
import math

import jax
import jax.numpy as jnp
import ml_dtypes
import numpy as np
from jax import lax
from jax.experimental import pallas as pl
from jax.experimental.pallas import tpu as pltpu
from jax.sharding import PartitionSpec as P

NT = 4096
DEC = 2
K0 = 8
HW = 64
R = 4
G = 16
BIN_DEV = 8
NB = 1024
NLAG = 2048
EPSILON = 1e-06

LANES = 128
SLICES = NB // LANES
FOLD = 4
CLASS = NB // FOLD
QUARTER = NT // FOLD
LAGQ = NLAG // FOLD
VMEM = 56 * 1024 * 1024


ORDER = np.arange(NB).reshape(CLASS, FOLD).T.reshape(-1)


def forward_tables():
    samples = np.arange(NT // 2, dtype=np.int64)
    freqs = K0 + ORDER.astype(np.int64)
    phase = samples[:, None] * freqs[None, :] % NT
    angle = (phase.astype(np.float32) * np.float32(2.0 * math.pi / NT)).astype(np.float64)
    cos = np.cos(angle).astype(np.float32).astype(ml_dtypes.bfloat16)
    sin = (-np.sin(angle)).astype(np.float32).astype(ml_dtypes.bfloat16)

    def part(which, rows):
        columns = slice(which * CLASS, (which + 1) * CLASS)
        return [cos[:rows, columns], sin[:rows, columns]]

    zero = np.concatenate(part(0, QUARTER), axis=1)
    two = np.concatenate(part(2, QUARTER), axis=1)
    odd = np.concatenate(part(1, 2 * QUARTER) + part(3, 2 * QUARTER), axis=1)
    return zero, two, odd


def band_tables():
    band = np.abs(ORDER[:, None] - ORDER[None, :]) <= HW
    counts = band.sum(axis=0).astype(np.float32)
    return band.astype(ml_dtypes.bfloat16), (1.0 / counts)[None, :].astype(np.float32)


def inverse_tables():
    freqs = K0 + ORDER.astype(np.int64)
    delays = (np.arange(2 * LAGQ, dtype=np.int64) - NLAG // 2) * DEC
    phase = np.mod(freqs[:, None] * delays[None, :], NT)
    angle = phase.astype(np.float64) * (2.0 * math.pi / NT)
    scale = 1.0 / math.sqrt(NB)
    real = (np.cos(angle) * scale).reshape(SLICES, 1, LANES, 2 * LAGQ)
    imag = (-np.sin(angle) * scale).reshape(SLICES, 1, LANES, 2 * LAGQ)
    rows = np.concatenate([real, imag], axis=1).reshape(FOLD, 2 * CLASS, 2 * LAGQ)
    zero = rows[0][:, :LAGQ]
    two = rows[2][:, :LAGQ]
    odd = np.concatenate([rows[1], rows[3]], axis=0)
    return [table.astype(np.float32).astype(ml_dtypes.bfloat16) for table in (zero, two, odd)]


def spectra_kernel(x_ref, mask_ref, zero_ref, two_ref, odd_ref, band_ref, inverse_ref, out_ref, hold):
    f32, bf16 = jnp.float32, jnp.bfloat16
    x = [x_ref[:, m * QUARTER:(m + 1) * QUARTER].astype(f32) for m in range(FOLD)]
    even, odd = x[0] + x[2], x[1] + x[3]
    first = jnp.dot((even + odd).astype(bf16), zero_ref[...], preferred_element_type=f32)
    third = jnp.dot((even - odd).astype(bf16), two_ref[...], preferred_element_type=f32)
    others = jnp.dot((x[0] - x[2]).astype(bf16), odd_ref[:QUARTER], preferred_element_type=f32)
    others += jnp.dot((x[1] - x[3]).astype(bf16), odd_ref[QUARTER:], preferred_element_type=f32)
    parts = [first, others[:, :2 * CLASS], third, others[:, 2 * CLASS:]]
    power = [part[:, :CLASS] * part[:, :CLASS] + part[:, CLASS:] * part[:, CLASS:] for part in parts]
    power = jnp.concatenate(power, axis=1).astype(bf16)
    mean = jnp.dot(power, band_ref[...], preferred_element_type=f32) * inverse_ref[...]
    weight = mask_ref[...] * lax.rsqrt(mean + EPSILON)
    rows = x_ref.shape[0]
    per_group = LANES // G
    for piece in range(SLICES):
        part, start = parts[piece // 2], (piece % 2) * LANES
        scale = weight[:, piece * LANES:(piece + 1) * LANES]
        hold[0] = part[:, start:start + LANES] * scale
        hold[1] = part[:, CLASS + start:CLASS + start + LANES] * scale
        for seg in range(rows // LANES):
            for j in range(per_group):
                at = seg * LANES + j * G
                for half in range(2):
                    taken = hold[half, pl.ds(seg * LANES + j, G, stride=per_group), :]
                    out_ref[piece, at:at + G, half * LANES:(half + 1) * LANES] = taken.astype(bf16)


def spectra(traces, mask_column, first_row, rows, block):
    tables = forward_tables() + band_tables()
    whole = [pl.BlockSpec(table.shape, lambda i: (0, 0)) for table in tables]
    skip = first_row // block
    return pl.pallas_call(
        spectra_kernel,
        grid=(rows // block,),
        in_specs=[
            pl.BlockSpec((block, NT), lambda i: (i + skip, 0)),
            pl.BlockSpec((block, 1), lambda i: (0, 0)),
        ] + whole,
        out_specs=pl.BlockSpec((SLICES, block, 2 * LANES), lambda i: (0, i, 0)),
        out_shape=jax.ShapeDtypeStruct((SLICES, rows, 2 * LANES), jnp.bfloat16),
        scratch_shapes=[pltpu.VMEM((2, block, LANES), jnp.float32)],
        compiler_params=pltpu.CompilerParams(vmem_limit_bytes=VMEM),
        cost_estimate=pl.CostEstimate(
            flops=8 * rows * NB * NB, bytes_accessed=rows * NT * 3 + 8 * NB * NB, transcendentals=rows * NB
        ),
        name="spectra",
    )(traces, mask_column, *[jnp.asarray(table) for table in tables])


def cross_kernel(blocks, steps, wide_ref, selector_ref, out_ref, tiles):
    f32 = jnp.float32
    tiles[...] = jnp.zeros_like(tiles)
    for source in range(0, blocks, 2):
        pairs = [
            (b, b + d) for b in (source, source + 1) for d in range(1, R + 1) if b + d < blocks and b < blocks
        ]
        if not pairs:
            continue
        needed = sorted({b for pair in pairs for b in pair})

        def body(step, sums):
            at = pl.ds(pl.multiple_of(step * G, G), G)
            real = {b: wide_ref[b, at, :LANES].astype(f32) for b in needed}
            imag = {b: wide_ref[b, at, LANES:].astype(f32) for b in needed}
            new = []
            for (a, b), (re, im) in zip(pairs, sums):
                re = re + (real[a] * real[b] + imag[a] * imag[b])
                im = im + (imag[a] * real[b] - real[a] * imag[b])
                new.append((re, im))
            return tuple(new)

        zero = jnp.zeros((G, LANES), f32)
        sums = lax.fori_loop(0, steps, body, tuple((zero, zero) for _ in pairs))
        for (a, b), (re, im) in zip(pairs, sums):
            row = a * R * G + (b - a - 1) * G
            tiles[row:row + G, :LANES] = re
            tiles[row:row + G, LANES:] = im
    stacked = jnp.dot(
        selector_ref[...], tiles[...], precision=lax.Precision.HIGHEST, preferred_element_type=f32
    ).astype(out_ref.dtype)
    for copy in range(out_ref.shape[0]):
        out_ref[copy] = stacked


def cross_stacks(wide, selector, copies):
    blocks, rows, width = wide.shape
    return pl.pallas_call(
        functools.partial(cross_kernel, blocks, rows // G),
        out_shape=jax.ShapeDtypeStruct((copies, selector.shape[0], width), jnp.bfloat16),
        scratch_shapes=[pltpu.VMEM((blocks * R * G, width), jnp.float32)],
        compiler_params=pltpu.CompilerParams(vmem_limit_bytes=VMEM),
        name="cross",
    )(wide, selector)


def lags_kernel(stacks_ref, zero_ref, two_ref, odd_ref, out_ref):
    f32, bf16 = jnp.float32, jnp.bfloat16
    copies = stacks_ref.shape[0] // SLICES
    pieces = []
    for piece in range(SLICES):
        total = stacks_ref[piece].astype(f32)
        for copy in range(1, copies):
            total += stacks_ref[copy * SLICES + piece].astype(f32)
        pieces.append(total)

    def product(values, table):
        high = values.astype(bf16)
        low = (values - high.astype(f32)).astype(bf16)
        both = jnp.dot(jnp.concatenate([high, low], axis=0), table, preferred_element_type=f32)
        return both[:BIN_DEV] + both[BIN_DEV:]

    zero = product(jnp.concatenate(pieces[0:2], axis=1), zero_ref[...])
    two = product(jnp.concatenate(pieces[4:6], axis=1), two_ref[...])
    odd = product(jnp.concatenate(pieces[2:4] + pieces[6:8], axis=1), odd_ref[...])
    plus, minus = zero + two, zero - two
    out_ref[:, :LAGQ] = plus + odd[:, :LAGQ]
    out_ref[:, LAGQ:2 * LAGQ] = minus + odd[:, LAGQ:]
    out_ref[:, 2 * LAGQ:3 * LAGQ] = plus - odd[:, :LAGQ]
    out_ref[:, 3 * LAGQ:] = minus - odd[:, LAGQ:]


def lags(stacks):
    tables = [jnp.asarray(table) for table in inverse_tables()]
    return pl.pallas_call(
        lags_kernel,
        out_shape=jax.ShapeDtypeStruct((BIN_DEV, NLAG), jnp.float32),
        compiler_params=pltpu.CompilerParams(vmem_limit_bytes=VMEM),
        name="lags",
    )(stacks, *tables)


def selector_of(channel_mask, owner_ids, local_bins, total_segs, blocks):
    own = jnp.concatenate([channel_mask, owner_ids.reshape(-1) * BIN_DEV + local_bins.reshape(-1)])
    every = lax.all_gather(own, "chan", axis=0, tiled=False)
    chans = channel_mask.shape[0]
    masks = every[:, :chans].astype(jnp.float32).reshape(blocks, G, chans // G)
    labels = every[:, chans:].reshape(-1)
    padded = jnp.concatenate([masks, jnp.zeros((R,) + masks.shape[1:], jnp.float32)], axis=0)
    counts = jnp.stack(
        [jnp.sum(masks * padded[d:d + blocks], axis=2) for d in range(1, R + 1)], axis=1
    ).reshape(-1)
    scale = 1.0 / (total_segs * jnp.maximum(counts, 1.0))
    bins = jnp.arange(blocks * BIN_DEV, dtype=labels.dtype)
    return jnp.where(labels[None, :] == bins[:, None], scale[None, :], 0.0)


def per_device(traces, channel_mask, owner_ids, local_bins):
    seg_count = lax.axis_size("seg")
    chan_count = lax.axis_size("chan")
    segs, chans, length = traces.shape
    total_segs = segs * seg_count
    rows = segs * chans
    block = 2 * chans
    narrow = SLICES * LANES // chan_count
    splits = LANES // narrow
    selector = selector_of(channel_mask, owner_ids, local_bins, total_segs, chan_count)
    mask_column = jnp.tile(channel_mask.astype(jnp.float32), 2)[:, None]
    outgoing = spectra(traces.reshape(rows, length), mask_column, 0, rows, block)
    if splits > 1:
        outgoing = outgoing.reshape(SLICES, rows, 2, splits, narrow).transpose(0, 3, 1, 2, 4)
        outgoing = outgoing.reshape(chan_count, rows, 2 * narrow)
    wide = lax.all_to_all(outgoing, "chan", split_axis=0, concat_axis=0, tiled=True)
    if splits > 1:
        wide = wide.reshape(chan_count, rows, 2, narrow)
        wide = jnp.pad(wide, ((0, 0), (0, 0), (0, 0), (0, LANES - narrow)))
        wide = wide.reshape(chan_count, rows, 2 * LANES)
    stacks = cross_stacks(wide, selector, seg_count)
    stacks = stacks.reshape(seg_count * chan_count, BIN_DEV, 2 * LANES)
    if splits > 1:
        stacks = stacks.reshape(-1, BIN_DEV, 2, LANES)[..., :narrow].reshape(-1, BIN_DEV, 2 * narrow)
    stacks = lax.all_to_all(stacks, ("seg", "chan"), split_axis=0, concat_axis=0, tiled=True)
    if splits > 1:
        stacks = stacks.reshape(seg_count, SLICES, splits, BIN_DEV, 2, narrow).transpose(0, 1, 3, 4, 2, 5)
        stacks = stacks.reshape(seg_count * SLICES, BIN_DEV, 2 * LANES)
    return lags(stacks)


def solution(mesh):
    in_specs = (P("seg", "chan", None), P("chan"), P("chan", None, None), P("chan", None))
    out_specs = P("chan", None)
    return jax.shard_map(
        per_device, mesh=mesh, in_specs=in_specs, out_specs=out_specs, check_vma=False
    )
```

time: 840 us -> 145 us (0.17)
  starting transfers between devices: 383 us -> 7.43 us
  waiting for transfers between devices: 209 us -> 0.01 us
  other arithmetic: 157 us -> 1.62 us
  blocking collectives: 0 us -> 104 us
  matrix products: 51.7 us -> 0 us
  Pallas kernels: 0 us -> 29.1 us
  local copies, waits for them, and re-layouts: 24.2 us -> 1.73 us
  between operations: 13.7 us -> 0.75 us
    all_to_all x1 -> x0, starting transfers between devices: 369 us -> none  [per_device(): lax.all_to_all(labels, 'chan', split_axis=0, concat_axis=0, tiled=True)]
    ppermute x8 -> x0, waiting for transfers between devices: 187 us -> none  [passed_along(): return lax.ppermute(block, axis, route)]
    unnamed x0 -> x1, blocking collectives: none -> 92.1 us
    another operation x2 -> x0, other arithmetic: 67.6 us -> none
    dot_general x4 -> x0, matrix products: 51.7 us -> none  [the longest x1 22.2 us: whiten(): jnp.dot(block.reshape(segs * chans, length), table, preferred_element_typ...]
    mul x7 -> x0, other arithmetic: 36 us -> none  [the longest x1 35.6 us: inverse_rows(): jnp.cos(angle) * scale]
    convert_element_type x8 -> x2, other arithmetic: 31.2 us -> 0.66 us  [the longest x1 0.66 us: per_device(): mask_column = jnp.tile(channel_mask.astype(jnp.float32), 2)[:, None]]
    pallas_call x0 -> x3, Pallas kernels: none -> 29.1 us  [the longest x1 17.1 us: spectra(): pl.pallas_call(spectra_kernel, grid=(rows // block,), in_specs=[pl.BlockS...]
  transfers between devices with their start and end apart: 11 -> 1, of which waited for: 4 -> 0; matrix products, arithmetic and copies ran while one was open for 15% -> 1% of each run, Pallas kernels for 0% -> 0%
where the time goes in v1:
time: 145 us; the launch traced here: 144 us
  blocking collectives  104 us (72%)
  Pallas kernels  29.1 us (20%)
  starting transfers between devices  7.43 us (5%)
  local copies, waits for them, and re-layouts  1.73 us (1%)
  other arithmetic  1.62 us (1%)
    unnamed x1, blocking collectives  92.1 us
    pallas_call x1, Pallas kernels, spectra(): pl.pallas_call(spectra_kernel, grid=(rows // block,), in_specs=[pl.BlockS...  17.1 us
    all_to_all x1, blocking collectives, per_device(): lax.all_to_all(stacks, ('seg', 'chan'), split_axis=0, concat_axis=0, tile...  11.5 us
    pallas_call x1, Pallas kernels, cross_stacks(): pl.pallas_call(functools.partial(cross_kernel, blocks, rows // G), out_sh...  8.91 us
    all_to_all x1, starting transfers between devices, per_device(): lax.all_to_all(outgoing, 'chan', split_axis=0, concat_axis=0, tiled=True)  7.43 us
    pallas_call x1, Pallas kernels, lags(): pl.pallas_call(lags_kernel, out_shape=jax.ShapeDtypeStruct((BIN_DEV, NLAG...  3.12 us
  transfers between devices with their start and end apart: 1, of which 0 were waited for; matrix products, arithmetic and copies ran while one was open for 1% of the time, Pallas kernels for 0%

profile of v1, /device:TPU:0, one launch (start us, length us, event | category | flops | bytes accessed | tf_op | source)
XLA Modules:
  0.0 144.3 jit_solution(16652605001524651195)
XLA Ops:
  0.0 0.7 convert_element_type.6
  0.7 0.8 copy.13.mask_ref
  1.4 17.1 %spectra.1 = bf16[8,1024,256]{2,1,0:T(8,128)(2,1)} custom-call(bf16[1024,4096]{1,0:T(8,128)(2,1)} %bitcast.18, f32[256,1]{1,0:T(8,128)} %copy.13.mask_ref, bf16[1024,512]{1,0:T(8,128)(2,1)} %constant.11.clone.zero_ref, bf16[1024,512]{1,0:T(8,128)(2,1)} %constant.26.clone.two_ref, bf16[2048,1024]{1,0:T(8,128)(2,1)} %constant.27.clone.odd_ref, ...), custom_call_target="tpu_custom_call" | custom-call | flops 8589934592 | bytes 20971520 | tf_op jit(solution)/shard_map/spectra/pallas_call | solution.py:107
  18.6 0.0 copy-start.3
  18.6 0.0 copy-start.1
  18.6 0.0 copy-start
  18.6 7.4 %all-to-all-start = ((bf16[8,1024,256]{2,1,0:T(8,128)(2,1)}), bf16[8,1024,256]{2,1,0:T(8,128)(2,1)}, u32[]{:S(2)}, u32[]{:S(2)}) async-start(bf16[8,1024,256]{2,1,0:T(8,128)(2,1)} %spectra.1), calls=%async_computation | async-start | bytes 8388608 | tf_op jit(solution)/shard_map/all_to_all | solution.py:237
  26.0 0.0 copy-done.3
  26.0 0.6 dynamic-slice
  27.3 0.0 copy-done.1
  27.3 0.0 copy-done.2
  27.3 0.0 copy-done
  27.3 0.1 add_dynamic-update-slice_fusion
  27.4 92.1 %all-reduce.1 = s32[1536]{0:T(1024)S(1)} all-reduce(s32[1536]{0:T(1024)S(1)} %add_dynamic-update-slice_fusion), channel_id=2, replica_groups=mesh['seg'=4,'chan'=8] {'chan'}, use_global_device_ids=true, to_apply=%add.1 | all-reduce | flops 1536 | bytes 12288
  119.6 0.1 reshape.35
  119.7 0.1 reshape.33
  119.7 0.1 fusion.2
  119.9 0.1 div.11
  120.0 0.1 eq.15
  120.1 0.7 fusion.selector_ref
  120.8 0.0 all-to-all-done.wide_ref
  120.8 8.9 %cross.1 = bf16[4,64,256]{2,1,0:T(8,128)(2,1)} custom-call(bf16[8,1024,256]{2,1,0:T(8,128)(2,1)} %all-to-all-done.wide_ref, f32[64,512]{1,0:T(8,128)} %fusion.selector_ref), custom_call_target="tpu_custom_call" | custom-call | tf_op jit(solution)/shard_map/cross/pallas_call | solution.py:162
  129.7 11.5 %all_to_all.10.stacks_ref = bf16[32,8,256]{2,1,0:T(8,128)(2,1)} all-to-all(bf16[32,8,256]{2,1,0:T(8,128)(2,1)} %bitcast.12), channel_id=1, replica_groups=mesh['seg'=4,'chan'=8] {'seg','chan'}, dimensions={0} | all-to-all | bytes 262144 | tf_op jit(solution)/shard_map/all_to_all | solution.py:246
  141.2 3.1 %lags.1 = f32[8,2048]{1,0:T(8,128)} custom-call(bf16[32,8,256]{2,1,0:T(8,128)(2,1)} %all_to_all.10.stacks_ref, bf16[512,512]{1,0:T(8,128)(2,1)} %constant.30.clone.zero_ref, bf16[512,512]{1,0:T(8,128)(2,1)} %constant.31.clone.two_ref, bf16[1024,1024]{1,0:T(8,128)(2,1)} %constant.32.clone.odd_ref), custom_call_target="tpu_custom_call" | custom-call | tf_op jit(solution)/shard_map/lags/pallas_call | solution.py:199
  (8 shorter events, 0.0 us)
Async XLA Ops:
  18.6 7.5 %copy-start.3 = (u32[32]{0:T(128)S(1)}, u32[32]{0:T(128)}, u32[]{:S(2)}) copy-start(u32[32]{0:T(128)} %constant.39) | copy-start | bytes 388
  18.6 8.7 %copy-start.1 = (s32[1,64]{1,0:T(1,128)S(1)}, s32[1,64]{1,0:T(1,128)}, u32[]{:S(2)}) copy-start(s32[1,64]{1,0:T(1,128)} %param.15) | copy-start | bytes 772
  18.6 8.7 %copy-start.2 = (s32[1,64,1]{1,2,0:T(1,128)S(1)}, s32[1,64,1]{1,2,0:T(1,128)}, u32[]{:S(2)}) copy-start(s32[1,64,1]{1,2,0:T(1,128)} %param.14) | copy-start | bytes 772
  18.6 8.7 %copy-start = (s32[128]{0:T(128)S(1)}, s32[128]{0:T(128)}, u32[]{:S(2)}) copy-start(s32[128]{0:T(128)} %param.13) | copy-start | bytes 1540
  18.6 102.2 %all-to-all-start = ((bf16[8,1024,256]{2,1,0:T(8,128)(2,1)}), bf16[8,1024,256]{2,1,0:T(8,128)(2,1)}, u32[]{:S(2)}, u32[]{:S(2)}) async-start(bf16[8,1024,256]{2,1,0:T(8,128)(2,1)} %spectra.1), calls=%async_computation | async-start | bytes 8388608 | tf_op jit(solution)/shard_map/all_to_all | solution.py:237

commit v2 on v1

v2 whole, which is shorter than its diff:
```python
import functools
import math

import jax
import jax.numpy as jnp
import ml_dtypes
import numpy as np
from jax import lax
from jax.experimental import pallas as pl
from jax.experimental.pallas import tpu as pltpu
from jax.sharding import PartitionSpec as P

NT = 4096
DEC = 2
K0 = 8
HW = 64
R = 4
G = 16
BIN_DEV = 8
NB = 1024
NLAG = 2048
EPSILON = 1e-06

LANES = 128
SLICES = NB // LANES
FOLD = 4
CLASS = NB // FOLD
QUARTER = NT // FOLD
LAGQ = NLAG // FOLD
VMEM = 32 * 1024 * 1024
BLOCK = 256
META = 16

SENT = (4, 3, 5, 2, 6, 1, 7)


ORDER = np.arange(NB).reshape(CLASS, FOLD).T.reshape(-1)


def forward_tables():
    samples = np.arange(NT // 2, dtype=np.int64)
    freqs = K0 + ORDER.astype(np.int64)
    phase = samples[:, None] * freqs[None, :] % NT
    angle = (phase.astype(np.float32) * np.float32(2.0 * math.pi / NT)).astype(np.float64)
    cos = np.cos(angle).astype(np.float32).astype(ml_dtypes.bfloat16)
    sin = (-np.sin(angle)).astype(np.float32).astype(ml_dtypes.bfloat16)

    def part(which, rows):
        columns = slice(which * CLASS, (which + 1) * CLASS)
        return [cos[rows, columns], sin[rows, columns]]

    low, high = slice(0, QUARTER), slice(QUARTER, 2 * QUARTER)
    band = (np.abs(ORDER[:, None] - ORDER[None, :]) <= HW).astype(ml_dtypes.bfloat16)
    table = np.concatenate(
        [
            np.concatenate(part(0, low) + part(2, low), axis=1),
            np.concatenate(part(1, low) + part(3, low), axis=1),
            np.concatenate(part(1, high) + part(3, high), axis=1),
            band,
        ],
        axis=0,
    )
    counts = band.astype(np.float32).sum(axis=0)
    return table, (1.0 / counts)[None, :].astype(np.float32)


def inverse_tables():
    freqs = K0 + ORDER.astype(np.int64)
    delays = (np.arange(2 * LAGQ, dtype=np.int64) - NLAG // 2) * DEC
    phase = np.mod(freqs[:, None] * delays[None, :], NT)
    angle = phase.astype(np.float64) * (2.0 * math.pi / NT)
    scale = 1.0 / math.sqrt(NB)
    real = (np.cos(angle) * scale).reshape(SLICES, 1, LANES, 2 * LAGQ)
    imag = (-np.sin(angle) * scale).reshape(SLICES, 1, LANES, 2 * LAGQ)
    rows = np.concatenate([real, imag], axis=1).reshape(FOLD, 2 * CLASS, 2 * LAGQ)
    zero = rows[0][:, :LAGQ]
    two = rows[2][:, :LAGQ]
    odd = np.concatenate([rows[1], rows[3]], axis=0)
    return [table.astype(np.float32).astype(ml_dtypes.bfloat16) for table in (zero, two, odd)]


def two_terms(values):
    high = values.astype(jnp.bfloat16)
    low = (values - high.astype(jnp.float32)).astype(jnp.bfloat16)
    return high, low


def two_term_dot(values_ref, table):
    rows = values_ref.shape[0] // 2
    both = jnp.dot(values_ref[...], table, preferred_element_type=jnp.float32)
    return both[:rows] + both[rows:]


def spectra_kernel(relative, with_meta, *refs):
    f32, bf16 = jnp.float32, jnp.bfloat16
    refs = list(refs)
    order_ref = refs.pop(0) if relative else None
    x_ref, mask_ref, owner_ref, bins_ref, table_ref, inverse_ref = refs[:6]
    out_refs = refs[6:-7]
    u, v, a, b, early, others, hold = refs[-7:]
    part = pl.program_id(1)
    rows = x_ref.shape[0]

    @pl.when(part == 0)
    def fold():
        x = [x_ref[:, m * QUARTER:(m + 1) * QUARTER].astype(f32) for m in range(FOLD)]
        even, odd = x[0] + x[2], x[1] + x[3]
        u[:rows], u[rows:] = two_terms(even + odd)
        v[:rows], v[rows:] = two_terms(even - odd)
        a[:rows], a[rows:] = two_terms(x[0] - x[2])
        b[:rows], b[rows:] = two_terms(x[1] - x[3])
        early[:, :2 * CLASS] = two_term_dot(u, table_ref[:, :2 * CLASS])
        early[:, 2 * CLASS:] = two_term_dot(v, table_ref[:, 2 * CLASS:])

    @pl.when(part == 1)
    def first_half():
        others[...] = two_term_dot(a, table_ref[...])

    @pl.when(part == 2)
    def second_half():
        others[...] += two_term_dot(b, table_ref[...])

    @pl.when(part == 3)
    def whiten():
        holders = [(early, 0), (others, 0), (early, 2 * CLASS), (others, 2 * CLASS)]
        power = []
        for ref, start in holders:
            real, imag = ref[:, start:start + CLASS], ref[:, start + CLASS:start + 2 * CLASS]
            power.append((real * real + imag * imag).astype(bf16))
        power = jnp.concatenate(power, axis=1)
        mean = jnp.dot(power, table_ref[...], preferred_element_type=f32) * inverse_ref[...]
        shape = (LANES, LANES)
        diagonal = lax.broadcasted_iota(jnp.int32, shape, 0) == lax.broadcasted_iota(jnp.int32, shape, 1)
        mask = jnp.where(diagonal, jnp.broadcast_to(mask_ref[...], shape), 0).astype(f32)
        mask = jnp.sum(mask, axis=1, keepdims=True)
        weight = jnp.concatenate([mask] * (rows // LANES), axis=0) * lax.rsqrt(mean + EPSILON)
        per_group = LANES // G
        target = refs[-8] if relative else out_refs[0]
        for piece in range(SLICES):
            ref, start = holders[piece // 2]
            start += (piece % 2) * LANES
            scale = weight[:, piece * LANES:(piece + 1) * LANES]
            hold[0] = ref[:, start:start + LANES] * scale
            hold[1] = ref[:, CLASS + start:CLASS + start + LANES] * scale
            for seg in range(rows // LANES):
                for j in range(per_group):
                    at = seg * LANES + j * G
                    for half in range(2):
                        taken = hold[half, pl.ds(seg * LANES + j, G, stride=per_group), :]
                        target[piece, at:at + G, half * LANES:(half + 1) * LANES] = taken.astype(bf16)
        if with_meta:
            tiles = owner_ref.shape[1]
            labels = (owner_ref[...] * BIN_DEV + bins_ref[...]).astype(f32)
            for piece in range(SLICES):
                at = pl.ds(rows, META)
                target[piece, at, :] = jnp.zeros((META, 2 * LANES), bf16)
                target[piece, at, :LANES] = jnp.broadcast_to(mask_ref[...].astype(f32), (META, LANES)).astype(bf16)
                target[piece, at, LANES:LANES + tiles] = jnp.broadcast_to(labels, (META, tiles)).astype(bf16)
        if relative:
            for slot in range(SLICES):
                out_refs[slot][...] = target[order_ref[slot]]


def spectra(traces, mask, owners, bins, first_row, rows, order=None, with_meta=False):
    table, inverse = forward_tables()
    block, relative = BLOCK, order is not None
    skip = first_row // block
    whole = lambda shape: pl.BlockSpec(shape, lambda i, p, *_: (0, 0))
    in_specs = [
        pl.BlockSpec((block, NT), lambda i, p, *_: (i + skip, 0)),
        whole(mask.shape),
        whole(owners.shape),
        whole(bins.shape),
        pl.BlockSpec((QUARTER, NB), lambda i, p, *_: (p, 0)),
        whole(inverse.shape),
    ]
    f32, bf16 = jnp.float32, jnp.bfloat16
    scratch = [pltpu.VMEM((2 * block, QUARTER), bf16)] * 4
    scratch += [pltpu.VMEM((block, 4 * CLASS), f32)] * 2 + [pltpu.VMEM((2, block, LANES), f32)]
    if relative:
        scratch = [pltpu.VMEM((SLICES, block, 2 * LANES), bf16)] + scratch
        out_specs = [pl.BlockSpec((block, 2 * LANES), lambda i, p, *_: (i, 0))] * SLICES
        out_shape = [jax.ShapeDtypeStruct((rows, 2 * LANES), bf16)] * SLICES
    else:
        extra = META if with_meta else 0
        out_specs = [pl.BlockSpec((SLICES, block + extra, 2 * LANES), lambda i, p, *_: (0, i, 0))]
        out_shape = [jax.ShapeDtypeStruct((SLICES, rows + extra, 2 * LANES), bf16)]
    result = pl.pallas_call(
        functools.partial(spectra_kernel, relative, with_meta),
        grid_spec=pltpu.PrefetchScalarGridSpec(
            num_scalar_prefetch=1 if relative else 0,
            grid=(rows // block, 4),
            in_specs=in_specs,
            out_specs=out_specs,
            scratch_shapes=scratch,
        ),
        out_shape=out_shape,
        compiler_params=pltpu.CompilerParams(vmem_limit_bytes=VMEM),
        cost_estimate=pl.CostEstimate(
            flops=14 * rows * NB * NB, bytes_accessed=rows * NT * 3 + 8 * NB * NB, transcendentals=rows * NB
        ),
        name="spectra",
    )(*([order] if relative else []), traces, mask, owners, bins, jnp.asarray(table), inverse)
    return result if relative else result[0]


def pair_sums(block_refs, pairs, steps, tiles):
    f32 = jnp.float32
    done = 0
    groups, current = [], []
    for pair in pairs:
        members = {m for p in current + [pair] for m in p}
        if current and 4 * (len(current) + 1) + 4 * len(members) > 60:
            groups.append(current)
            current = []
        current = current + [pair]
    groups.append(current)
    for group in groups:
        needed = sorted({m for pair in group for m in pair})

        def body(step, sums):
            at = pl.ds(pl.multiple_of(step * G, G), G)
            real = {m: block_refs[m][at, :LANES].astype(f32) for m in needed}
            imag = {m: block_refs[m][at, LANES:].astype(f32) for m in needed}
            new = []
            for (p, q), (re, im) in zip(group, sums):
                re = re + (real[p] * real[q] + imag[p] * imag[q])
                im = im + (imag[p] * real[q] - real[p] * imag[q])
                new.append((re, im))
            return tuple(new)

        zero = jnp.zeros((G, LANES), f32)
        sums = lax.fori_loop(0, steps, body, tuple((zero, zero) for _ in group), unroll=2)
        for re, im in sums:
            tiles[done:done + G, :LANES] = re
            tiles[done:done + G, LANES:] = im
            done += G


def cross_kernel(split, pairs, steps, has_before, *refs):
    f32 = jnp.float32
    refs = list(refs)
    before_ref = refs.pop(-3) if has_before else None
    *block_refs, scale_ref, onehot_ref, out_ref, tiles = refs
    if split:
        block_refs = [block_refs[0].at[m] for m in range(block_refs[0].shape[0])]
    pair_sums(block_refs, pairs, steps, tiles)
    high, low = two_terms(tiles[...] * scale_ref[...])
    stacked = jnp.dot(onehot_ref[...], high, preferred_element_type=f32)
    stacked += jnp.dot(onehot_ref[...], low, preferred_element_type=f32)
    if has_before:
        stacked += before_ref[...]
    if len(out_ref.shape) == 2:
        out_ref[...] = stacked
    else:
        for copy in range(out_ref.shape[0]):
            out_ref[copy] = stacked.astype(out_ref.dtype)


def cross(blocks, pairs, rows, scale, onehot, before=None, copies=None):
    bins = onehot.shape[0]
    shape = (bins, 2 * LANES)
    split = not isinstance(blocks, (list, tuple))
    inputs = ([blocks] if split else list(blocks)) + [scale, onehot]
    if before is not None:
        inputs.append(before)
    if copies is None:
        out_shape = jax.ShapeDtypeStruct(shape, jnp.float32)
    else:
        out_shape = jax.ShapeDtypeStruct((copies,) + shape, jnp.bfloat16)
    moved = sum(4 * rows * LANES for _ in range(len(pairs)))
    return pl.pallas_call(
        functools.partial(cross_kernel, split, pairs, rows // G, before is not None),
        out_shape=out_shape,
        scratch_shapes=[pltpu.VMEM((len(pairs) * G, 2 * LANES), jnp.float32)],
        compiler_params=pltpu.CompilerParams(vmem_limit_bytes=VMEM),
        cost_estimate=pl.CostEstimate(
            flops=8 * rows * LANES * len(pairs), bytes_accessed=moved, transcendentals=0
        ),
        name="cross",
    )(*inputs)

def lags_kernel(stacks_ref, zero_ref, two_ref, odd_ref, out_ref):
    f32 = jnp.float32
    copies = stacks_ref.shape[0] // SLICES
    pieces = []
    for piece in range(SLICES):
        total = stacks_ref[piece].astype(f32)
        for copy in range(1, copies):
            total += stacks_ref[copy * SLICES + piece].astype(f32)
        pieces.append(total)

    def product(values, table):
        both = jnp.dot(jnp.concatenate(two_terms(values), axis=0), table, preferred_element_type=f32)
        return both[:BIN_DEV] + both[BIN_DEV:]

    zero = product(jnp.concatenate(pieces[0:2], axis=1), zero_ref[...])
    two = product(jnp.concatenate(pieces[4:6], axis=1), two_ref[...])
    odd = product(jnp.concatenate(pieces[2:4] + pieces[6:8], axis=1), odd_ref[...])
    plus, minus = zero + two, zero - two
    out_ref[:, :LAGQ] = plus + odd[:, :LAGQ]
    out_ref[:, LAGQ:2 * LAGQ] = minus + odd[:, LAGQ:]
    out_ref[:, 2 * LAGQ:3 * LAGQ] = plus - odd[:, :LAGQ]
    out_ref[:, 3 * LAGQ:] = minus - odd[:, LAGQ:]


def lags(stacks):
    tables = [jnp.asarray(table) for table in inverse_tables()]
    return pl.pallas_call(
        lags_kernel,
        out_shape=jax.ShapeDtypeStruct((BIN_DEV, NLAG), jnp.float32),
        compiler_params=pltpu.CompilerParams(vmem_limit_bytes=VMEM // 2),
        name="lags",
    )(stacks, *tables)


def weights_of(masks, labels, low, far, sign, total_segs):
    blocks = masks.shape[0]
    valid = (far >= 1) & (far <= R) & (low + far < blocks)
    far = jnp.where(valid, far, 1)
    other = jnp.minimum(low + far, blocks - 1)
    groups = masks.reshape(blocks, G, -1)
    counts = jnp.sum(groups[low] * groups[other], axis=2)
    scale = jnp.where(valid[:, None], 1.0 / (total_segs * jnp.maximum(counts, 1.0)), 0.0)
    chosen = labels.reshape(blocks, R, G)[low, far - 1].reshape(-1)
    half = jnp.repeat(jnp.stack([jnp.ones_like(sign), sign], axis=1), LANES, axis=1)
    wide = (scale[:, :, None] * half[:, None, :]).reshape(-1, 2 * LANES)
    bins = jnp.arange(blocks * BIN_DEV, dtype=jnp.float32)
    return wide, (chosen[None, :] == bins[:, None]).astype(jnp.bfloat16)


def fixed_pairs(blocks):
    return [(b, b + d) for b in range(blocks) for d in range(1, R + 1) if b + d < blocks]


def fixed_weights(masks, labels, total_segs):
    pairs = np.array(fixed_pairs(masks.shape[0]))
    low, far = jnp.asarray(pairs[:, 0]), jnp.asarray(pairs[:, 1] - pairs[:, 0])
    return weights_of(masks, labels, low, far, jnp.ones((len(pairs),), jnp.float32), total_segs)


def slot_weights(masks, labels, pairs, total_segs):
    blocks = masks.shape[0]
    here = lax.axis_index("chan")
    slots = jnp.asarray(np.array(pairs))
    held = (here - slots) % blocks
    low, high = jnp.min(held, axis=1), jnp.max(held, axis=1)
    sign = jnp.where(held[:, 0] < held[:, 1], 1.0, -1.0)
    return weights_of(masks, labels, low, high - low, sign, total_segs)


def sent_along(x, mask, owners, bins, total_segs):
    seg_count = lax.axis_size("seg")
    count = lax.axis_size("chan")
    rows, chans = x.shape[0], mask.shape[1]
    early = BLOCK
    late = rows - early
    first = spectra(x, mask, owners, bins, 0, early, with_meta=True)
    first = lax.all_to_all(first, "chan", split_axis=0, concat_axis=0, tiled=True)
    order = (lax.axis_index("chan") + jnp.arange(count, dtype=jnp.int32)) % count
    second = spectra(x, mask, owners, bins, early, late, order=order)
    slots = {0: second[0]}
    for shift in SENT:
        slots[shift] = lax.ppermute(second[shift], "chan", [(i, (i + shift) % count) for i in range(count)])

    meta = first[:, early, :].astype(jnp.float32)
    masks, labels = meta[:, :chans], meta[:, LANES:LANES + owners.shape[1]]
    stacks = cross(first, fixed_pairs(count), early, *fixed_weights(masks, labels, total_segs))
    known = (0,) + SENT[:-1]
    pairs = [(known[i], known[j]) for i in range(len(known)) for j in range(i + 1, len(known))]
    at = {slot: i for i, slot in enumerate(known)}
    stacks = cross(
        [slots[slot] for slot in known],
        [(at[p], at[q]) for p, q in pairs],
        late,
        *slot_weights(masks, labels, pairs, total_segs),
        before=stacks,
    )
    known = (0,) + SENT
    pairs = [(slot, SENT[-1]) for slot in known[:-1]]
    return cross(
        [slots[slot] for slot in known],
        [(i, len(known) - 1) for i in range(len(known) - 1)],
        late,
        *slot_weights(masks, labels, pairs, total_segs),
        before=stacks,
        copies=seg_count,
    )


def sent_at_once(x, mask, owners, bins, total_segs):
    seg_count = lax.axis_size("seg")
    count = lax.axis_size("chan")
    rows, chans = x.shape[0], mask.shape[1]
    narrow = NB // count
    splits = LANES // narrow
    own = jnp.concatenate([mask, owners * BIN_DEV + bins], axis=1)
    every = lax.all_gather(own, "chan", axis=0, tiled=True).astype(jnp.float32)
    masks, labels = every[:, :chans], every[:, chans:]
    outgoing = spectra(x, mask, owners, bins, 0, rows)
    outgoing = outgoing.reshape(SLICES, rows, 2, splits, narrow).transpose(0, 3, 1, 2, 4)
    outgoing = outgoing.reshape(count, rows, 2 * narrow)
    wide = lax.all_to_all(outgoing, "chan", split_axis=0, concat_axis=0, tiled=True)
    wide = jnp.pad(wide.reshape(count, rows, 2, narrow), ((0, 0), (0, 0), (0, 0), (0, LANES - narrow)))
    wide = wide.reshape(count, rows, 2 * LANES)
    stacks = cross(wide, fixed_pairs(count), rows, *fixed_weights(masks, labels, total_segs), copies=seg_count)
    return stacks.reshape(-1, 2, LANES)[..., :narrow]


def per_device(traces, channel_mask, owner_ids, local_bins):
    seg_count = lax.axis_size("seg")
    count = lax.axis_size("chan")
    segs, chans, length = traces.shape
    x = traces.reshape(segs * chans, length)
    mask = channel_mask.reshape(1, chans)
    owners = owner_ids.reshape(1, -1)
    if count == SLICES:
        stacks = sent_along(x, mask, owners, local_bins, segs * seg_count)
        stacks = stacks.reshape(seg_count * count, BIN_DEV, 2 * LANES)
        stacks = lax.all_to_all(stacks, ("seg", "chan"), split_axis=0, concat_axis=0, tiled=True)
    else:
        narrow = NB // count
        stacks = sent_at_once(x, mask, owners, local_bins, segs * seg_count)
        stacks = stacks.reshape(seg_count * count, BIN_DEV, 2 * narrow)
        stacks = lax.all_to_all(stacks, ("seg", "chan"), split_axis=0, concat_axis=0, tiled=True)
        stacks = stacks.reshape(seg_count, SLICES, count // SLICES, BIN_DEV, 2, narrow)
        stacks = stacks.transpose(0, 1, 3, 4, 2, 5).reshape(seg_count * SLICES, BIN_DEV, 2 * LANES)
    return lags(stacks)


def solution(mesh):
    in_specs = (P("seg", "chan", None), P("chan"), P("chan", None, None), P("chan", None))
    out_specs = P("chan", None)
    return jax.shard_map(
        per_device, mesh=mesh, in_specs=in_specs, out_specs=out_specs, check_vma=False
    )
```

time: 145 us -> 140 us (0.966)
  blocking collectives: 104 us -> 13.7 us
  local copies, waits for them, and re-layouts: 1.73 us -> 39 us
  waiting for transfers between devices: 0.01 us -> 19.8 us
  starting transfers between devices: 7.43 us -> 22.8 us
  other arithmetic: 1.62 us -> 11.5 us
  Pallas kernels: 29.1 us -> 31.8 us
    unnamed x1 -> x0, blocking collectives: 92.1 us -> none
    ppermute x0 -> x7, waiting for transfers between devices: none -> 19.8 us  [sent_along(): lax.ppermute(second[shift], 'chan', [(i, (i + shift) % count) for i in ra...]
    unnamed x10 -> x53, local copies, waits for them, and re-layouts: 0.6 us -> 19.6 us
    ppermute x0 -> x7, starting transfers between devices: none -> 15.3 us  [sent_along(): lax.ppermute(second[shift], 'chan', [(i, (i + shift) % count) for i in ra...]
    gather x0 -> x9, local copies, waits for them, and re-layouts: none -> 11.4 us  [the longest x6 7.69 us: weights_of(): counts = jnp.sum(groups[low] * groups[other], axis=2)]
    pallas_call x2 -> x5, Pallas kernels: 26 us -> 30.6 us  [the longest x2 24.4 us: spectra(): pl.pallas_call(functools.partial(spectra_kernel, relative, with_meta), gr...]
    reduce_sum x1 -> x3, other arithmetic: 0.14 us -> 3.18 us  [weights_of(): counts = jnp.sum(groups[low] * groups[other], axis=2)]
    eq x1 -> x3, local copies, waits for them, and re-layouts: 0.08 us -> 2.82 us  [weights_of(): return (wide, (chosen[None, :] == bins[:, None]).astype(jnp.bfloat16))]
  transfers between devices with their start and end apart: 1 -> 8, of which waited for: 0 -> 2; matrix products, arithmetic and copies ran while one was open for 1% -> 23% of each run, Pallas kernels for 0% -> 16%
where the time goes in v2:
time: 140 us; the launch traced here: 139 us
  local copies, waits for them, and re-layouts  39 us (28%)
  Pallas kernels  31.8 us (23%)
  starting transfers between devices  22.8 us (16%)
  waiting for transfers between devices  19.8 us (14%)
  blocking collectives  13.7 us (10%)
  other arithmetic  11.5 us (8%)
    pallas_call x2, Pallas kernels, spectra(): pl.pallas_call(functools.partial(spectra_kernel, relative, with_meta), gr...  24.4 us
    ppermute x7, waiting for transfers between devices, sent_along(): lax.ppermute(second[shift], 'chan', [(i, (i + shift) % count) for i in ra...  19.8 us
    unnamed x53, local copies, waits for them, and re-layouts  19.6 us
    ppermute x7, starting transfers between devices, sent_along(): lax.ppermute(second[shift], 'chan', [(i, (i + shift) % count) for i in ra...  15.3 us
    all_to_all x1, blocking collectives, per_device(): lax.all_to_all(stacks, ('seg', 'chan'), split_axis=0, concat_axis=0, tile...  13.7 us
    gather x6, local copies, waits for them, and re-layouts, weights_of(): counts = jnp.sum(groups[low] * groups[other], axis=2)  7.69 us
    all_to_all x1, starting transfers between devices, sent_along(): lax.all_to_all(first, 'chan', split_axis=0, concat_axis=0, tiled=True)  7.43 us
    pallas_call x3, Pallas kernels, cross(): pl.pallas_call(functools.partial(cross_kernel, split, pairs, rows // G, b...  6.22 us
  transfers between devices with their start and end apart: 8, of which 2 were waited for; matrix products, arithmetic and copies ran while one was open for 23% of the time, Pallas kernels for 16%

profile of v2, /device:TPU:0, one launch (start us, length us, event | category | flops | bytes accessed | tf_op | source)
XLA Modules:
  0.0 138.9 jit_solution(2533302391550249598)
XLA Ops:
  0.0 3.4 %copy-done = bf16[8,128,4096]{2,1,0:T(8,128)(2,1)S(1)} copy-done((bf16[8,128,4096]{2,1,0:T(8,128)(2,1)S(1)}, bf16[8,128,4096]{2,1,0:T(8,128)(2,1)}, u32[]{:S(2)}) %copy-start) | copy-done | bytes 8388632
  3.4 3.4 %copy-done.2 = bf16[4096,1024]{1,0:T(8,128)(2,1)S(1)} copy-done((bf16[4096,1024]{1,0:T(8,128)(2,1)S(1)}, bf16[4096,1024]{1,0:T(8,128)(2,1)}, u32[]{:S(2)}) %copy-start.2) | copy-done | bytes 8388632
  9.4 6.4 %spectra.3 = bf16[8,272,256]{2,1,0:T(8,128)(2,1)} custom-call(bf16[1024,4096]{1,0:T(8,128)(2,1)S(1)} %bitcast.75, s32[1,128]{1,0:T(1,128)S(1)} %bitcast.78, s32[1,64]{1,0:T(1,128)S(1)} %bitcast.80, s32[1,64]{1,0:T(1,128)S(1)} %copy-done.13, bf16[4096,1024]{1,0:T(8,128)(2,1)S(1)} %copy-done.2, f32[1,1024]{1,0:T(1,128)S(1)} %copy-done.7), custom_call_target="tpu_custom_call" | custom-call | flops 3758096384 | bytes 11534336 | tf_op jit(solution)/shard_map/spectra/pallas_call | solution.py:188
  15.8 7.4 %all-to-all-start = ((bf16[8,272,256]{2,1,0:T(8,128)(2,1)}), bf16[8,272,256]{2,1,0:T(8,128)(2,1)S(1)}, u32[]{:S(2)}, u32[]{:S(2)}) async-start(bf16[8,272,256]{2,1,0:T(8,128)(2,1)} %spectra.3), calls=%async_computation | async-start | bytes 2228224 | tf_op jit(solution)/shard_map/all_to_all | solution.py:359
  23.3 3.4 %copy-done.1 = bf16[8,128,4096]{2,1,0:T(8,128)(2,1)S(1)} copy-done((bf16[8,128,4096]{2,1,0:T(8,128)(2,1)S(1)}, bf16[8,128,4096]{2,1,0:T(8,128)(2,1)}, u32[]{:S(2)}) %copy-start.1) | copy-done | bytes 8388632
  26.7 3.4 %copy-done.3 = bf16[4096,1024]{1,0:T(8,128)(2,1)S(1)} copy-done((bf16[4096,1024]{1,0:T(8,128)(2,1)S(1)}, bf16[4096,1024]{1,0:T(8,128)(2,1)}, u32[]{:S(2)}) %copy-start.3) | copy-done | bytes 8388632
  30.1 18.0 %spectra.2 = (bf16[768,256]{1,0:T(8,128)(2,1)S(1)}, bf16[768,256]{1,0:T(8,128)(2,1)S(1)}, bf16[768,256]{1,0:T(8,128)(2,1)}, bf16[768,256]{1,0:T(8,128)(2,1)}, bf...) custom-call(s32[8]{0:T(128)S(1)} %and_select_fusion.2.refs_0_, ...), custom_call_target="tpu_custom_call" | custom-call | flops 11274289152 | bytes 17825792 | tf_op jit(solution)/shard_map/spectra/pallas_call | solution.py:188
  49.6 2.9 %collective-permute-start = (bf16[768,256]{1,0:T(8,128)(2,1)}, bf16[768,256]{1,0:T(8,128)(2,1)S(1)}, u32[]{:S(2)}, u32[]{:S(2)}) collective-permute-start(bf16[768,256]{1,0:T(8,128)(2,1)} %get-tuple-element.14), channel_id=1, source_target_pairs={{0,4},{1,5},{2,6},{3,7},{4,0},{5,1},{6,2},{7,3},{8,12},{9,13},{10,... | collective-permute-start | bytes 1179656 | tf_op jit(solution)/shard_map/ppermute | solution.py:364
  52.5 2.4 %collective-permute-start.1 = (bf16[768,256]{1,0:T(8,128)(2,1)}, bf16[768,256]{1,0:T(8,128)(2,1)S(1)}, u32[]{:S(2)}, u32[]{:S(2)}) collective-permute-start(bf16[768,256]{1,0:T(8,128)(2,1)} %get-tuple-element.15), channel_id=1, source_target_pairs={{0,3},{1,4},{2,5},{3,6},{4,7},{5,0},{6,1},{7,2},{8,11},{9,12},{10,... | collective-permute-start | bytes 1179656 | tf_op jit(solution)/shard_map/ppermute | solution.py:364
  54.9 1.5 %collective-permute-start.2 = (bf16[768,256]{1,0:T(8,128)(2,1)}, bf16[768,256]{1,0:T(8,128)(2,1)S(1)}, u32[]{:S(2)}, u32[]{:S(2)}) collective-permute-start(bf16[768,256]{1,0:T(8,128)(2,1)} %get-tuple-element.16), channel_id=1, source_target_pairs={{0,5},{1,6},{2,7},{3,0},{4,1},{5,2},{6,3},{7,4},{8,13},{9,14},{10,... | collective-permute-start | bytes 1179656 | tf_op jit(solution)/shard_map/ppermute | solution.py:364
  56.3 1.5 %collective-permute-start.3 = (bf16[768,256]{1,0:T(8,128)(2,1)}, bf16[768,256]{1,0:T(8,128)(2,1)S(1)}, u32[]{:S(2)}, u32[]{:S(2)}) collective-permute-start(bf16[768,256]{1,0:T(8,128)(2,1)} %get-tuple-element.17), channel_id=1, source_target_pairs={{0,2},{1,3},{2,4},{3,5},{4,6},{5,7},{6,0},{7,1},{8,10},{9,11},{10,... | collective-permute-start | bytes 1179656 | tf_op jit(solution)/shard_map/ppermute | solution.py:364
  57.8 2.4 %collective-permute-start.4 = (bf16[768,256]{1,0:T(8,128)(2,1)}, bf16[768,256]{1,0:T(8,128)(2,1)S(1)}, u32[]{:S(2)}, u32[]{:S(2)}) collective-permute-start(bf16[768,256]{1,0:T(8,128)(2,1)} %get-tuple-element.18), channel_id=1, source_target_pairs={{0,6},{1,7},{2,0},{3,1},{4,2},{5,3},{6,4},{7,5},{8,14},{9,15},{10,... | collective-permute-start | bytes 1179656 | tf_op jit(solution)/shard_map/ppermute | solution.py:364
  66.3 1.4 gather_fusion.3
  76.9 1.3 select_n.189
  79.0 1.5 %gather_fusion.8 = f32[22,16]{1,0:T(8,128)} fusion(f32[8,4,16]{2,1,0:T(4,128)S(1)} %reshape.285, s32[22]{0:T(128)} %constant.187), kind=kCustom, calls=%fused_computation.8 | custom fusion | bytes 2992 | tf_op jit(solution)/shard_map/gather | solution.py:325
  80.5 1.4 eq.59
  81.9 1.5 %gather_fusion.5 = f32[21,16]{1,0:T(8,128)} fusion(f32[8,4,16]{2,1,0:T(4,128)S(1)} %reshape.285, s32[21]{0:T(128)} %get-tuple-element.27), kind=kCustom, calls=%fused_computation.5 | custom fusion | bytes 2856 | tf_op jit(solution)/shard_map/gather | solution.py:325
  83.3 1.4 eq.55
  91.5 4.8 %collective-permute-done.refs_1_ = bf16[768,256]{1,0:T(8,128)(2,1)S(1)} collective-permute-done((bf16[768,256]{1,0:T(8,128)(2,1)}, bf16[768,256]{1,0:T(8,128)(2,1)S(1)}, u32[]{:S(2)}, u32[]{:S(2)}) %collective-permute-start) | collective-permute-done | bytes 393248 | tf_op jit(solution)/shard_map/ppermute | solution.py:364
  99.2 4.8 %collective-permute-start.6 = (bf16[768,256]{1,0:T(8,128)(2,1)S(1)}, bf16[768,256]{1,0:T(8,128)(2,1)S(1)}, u32[]{:S(2)}, u32[]{:S(2)}) collective-permute-start(bf16[768,256]{1,0:T(8,128)(2,1)S(1)} %copy-done.16), channel_id=1, source_target_pairs={{0,7},{1,0},{2,1},{3,2},{4,3},{5,4},{6,5},{7,6},{8,15},{9,8},{10,9... | collective-permute-start | bytes 1179656 | tf_op jit(solution)/shard_map/ppermute | solution.py:364
  104.0 14.9 %collective-permute-done.5.refs_6_ = bf16[768,256]{1,0:T(8,128)(2,1)S(1)} collective-permute-done((bf16[768,256]{1,0:T(8,128)(2,1)}, bf16[768,256]{1,0:T(8,128)(2,1)S(1)}, u32[]{:S(2)}, u32[]{:S(2)}) %collective-permute-start.5) | collective-permute-done | bytes 393248 | tf_op jit(solution)/shard_map/ppermute | solution.py:364
  119.0 3.4 %cross.4.refs_10_ = f32[64,256]{1,0:T(8,128)S(1)} custom-call(bf16[768,256]{1,0:T(8,128)(2,1)S(1)} %get-tuple-element.13.refs_0_, bf16[768,256]{1,0:T(8,128)(2,1)S(1)} %collective-permute-done.refs_1_, bf16[768,256]{1,0:T(8,128)(2,1)S(1)} %collective-permute-done.1.refs_2_, bf16[768,256]{1,0:T(8,128)(2,1)S(1)} %collective-permute-done.2.refs_3_, ...), custom_call_target="tpu_custom_call" | custom-call | flops 16515072 | bytes 8257536 | tf_op jit(solution)/shard_map/cross/pallas_call | solution.py:272
  122.5 1.5 %cross.5 = bf16[4,64,256]{2,1,0:T(8,128)(2,1)S(1)} custom-call(bf16[768,256]{1,0:T(8,128)(2,1)S(1)} %get-tuple-element.13.refs_0_, bf16[768,256]{1,0:T(8,128)(2,1)S(1)} %collective-permute-done.refs_1_, bf16[768,256]{1,0:T(8,128)(2,1)S(1)} %collective-permute-done.1.refs_2_, bf16[768,256]{1,0:T(8,128)(2,1)S(1)} %collective-permute-done.2.refs_3_, ...), custom_call_target="tpu_custom_call" | custom-call | flops 5505024 | bytes 2752512 | tf_op jit(solution)/shard_map/cross/pallas_call | solution.py:272
  124.0 13.7 %all_to_all.10.stacks_ref = bf16[32,8,256]{2,1,0:T(8,128)(2,1)S(1)} all-to-all(bf16[32,8,256]{2,1,0:T(8,128)(2,1)S(1)} %bitcast.77), channel_id=1, replica_groups=mesh['seg'=4,'chan'=8] {'seg','chan'}, dimensions={0} | all-to-all | bytes 262144 | tf_op jit(solution)/shard_map/all_to_all | solution.py:420
  (100 shorter events, 31.0 us)
Async XLA Ops:
  0.0 3.4 %copy-start = (bf16[8,128,4096]{2,1,0:T(8,128)(2,1)S(1)}, bf16[8,128,4096]{2,1,0:T(8,128)(2,1)}, u32[]{:S(2)}) copy-start(bf16[8,128,4096]{2,1,0:T(8,128)(2,1)} %param.15) | copy-start | bytes 25165828
  3.4 3.4 %copy-start.2 = (bf16[4096,1024]{1,0:T(8,128)(2,1)S(1)}, bf16[4096,1024]{1,0:T(8,128)(2,1)}, u32[]{:S(2)}) copy-start(bf16[4096,1024]{1,0:T(8,128)(2,1)} %constant.54.clone.refs_5_.refs_4_) | copy-start | bytes 25165828
  15.8 7.5 %copy-start.8 = (f32[1,1024]{1,0:T(1,128)S(1)}, f32[1,1024]{1,0:T(1,128)}, u32[]{:S(2)}) copy-start(f32[1,1024]{1,0:T(1,128)} %constant.55.clone.refs_6_.refs_5_) | copy-start | bytes 12292
  15.8 7.5 %copy-start.10 = (s32[128]{0:T(128)S(1)}, s32[128]{0:T(128)}, u32[]{:S(2)}) copy-start(s32[128]{0:T(128)} %param.16) | copy-start | bytes 1540
  15.8 7.5 %copy-start.12 = (s32[1,64,1]{1,2,0:T(1,128)S(1)}, s32[1,64,1]{1,2,0:T(1,128)}, u32[]{:S(2)}) copy-start(s32[1,64,1]{1,2,0:T(1,128)} %param.17) | copy-start | bytes 772
  15.8 7.5 %copy-start.14 = (s32[1,64]{1,0:T(1,128)S(1)}, s32[1,64]{1,0:T(1,128)}, u32[]{:S(2)}) copy-start(s32[1,64]{1,0:T(1,128)} %refs_3_.1) | copy-start | bytes 772
  15.8 49.8 %all-to-all-start = ((bf16[8,272,256]{2,1,0:T(8,128)(2,1)}), bf16[8,272,256]{2,1,0:T(8,128)(2,1)S(1)}, u32[]{:S(2)}, u32[]{:S(2)}) async-start(bf16[8,272,256]{2,1,0:T(8,128)(2,1)} %spectra.3), calls=%async_computation | async-start | bytes 2228224 | tf_op jit(solution)/shard_map/all_to_all | solution.py:359
  23.3 3.4 %copy-start.1 = (bf16[8,128,4096]{2,1,0:T(8,128)(2,1)S(1)}, bf16[8,128,4096]{2,1,0:T(8,128)(2,1)}, u32[]{:S(2)}) copy-start(bf16[8,128,4096]{2,1,0:T(8,128)(2,1)} %param.15) | copy-start | bytes 25165828
  30.0 30.1 %copy-start.19 = (s32[21,2]{1,0:T(8,128)S(1)}, s32[21,2]{1,0:T(8,128)}, u32[]{:S(2)}) copy-start(s32[21,2]{1,0:T(8,128)} %constant.114) | copy-start | bytes 508
  30.0 31.1 %copy-start.21 = (s32[7,2]{1,0:T(8,128)S(1)}, s32[7,2]{1,0:T(8,128)}, u32[]{:S(2)}) copy-start(s32[7,2]{1,0:T(8,128)} %constant.113) | copy-start | bytes 172
  30.0 32.1 %copy-start.23 = (s32[22]{0:T(128)S(1)}, s32[22]{0:T(128)}, u32[]{:S(2)}) copy-start(s32[22]{0:T(128)} %constant.178) | copy-start | bytes 268
  30.0 32.1 %copy-start.22 = (s32[22]{0:T(128)S(1)}, s32[22]{0:T(128)}, u32[]{:S(2)}) copy-start(s32[22]{0:T(128)} %constant.179) | copy-start | bytes 268
  49.6 46.8 %collective-permute-start = (bf16[768,256]{1,0:T(8,128)(2,1)}, bf16[768,256]{1,0:T(8,128)(2,1)S(1)}, u32[]{:S(2)}, u32[]{:S(2)}) collective-permute-start(bf16[768,256]{1,0:T(8,128)(2,1)} %get-tuple-element.14), channel_id=1, source_target_pairs={{0,4},{1,5},{2,6},{3,7},{4,0},{5,1},{6,2},{7,3},{8,12},{9,13},{10,... | collective-permute-start | bytes 1179656 | tf_op jit(solution)/shard_map/ppermute | solution.py:364
  52.5 46.6 %collective-permute-start.1 = (bf16[768,256]{1,0:T(8,128)(2,1)}, bf16[768,256]{1,0:T(8,128)(2,1)S(1)}, u32[]{:S(2)}, u32[]{:S(2)}) collective-permute-start(bf16[768,256]{1,0:T(8,128)(2,1)} %get-tuple-element.15), channel_id=1, source_target_pairs={{0,3},{1,4},{2,5},{3,6},{4,7},{5,0},{6,1},{7,2},{8,11},{9,12},{10,... | collective-permute-start | bytes 1179656 | tf_op jit(solution)/shard_map/ppermute | solution.py:364
  54.9 49.1 %collective-permute-start.2 = (bf16[768,256]{1,0:T(8,128)(2,1)}, bf16[768,256]{1,0:T(8,128)(2,1)S(1)}, u32[]{:S(2)}, u32[]{:S(2)}) collective-permute-start(bf16[768,256]{1,0:T(8,128)(2,1)} %get-tuple-element.16), channel_id=1, source_target_pairs={{0,5},{1,6},{2,7},{3,0},{4,1},{5,2},{6,3},{7,4},{8,13},{9,14},{10,... | collective-permute-start | bytes 1179656 | tf_op jit(solution)/shard_map/ppermute | solution.py:364
  56.3 47.6 %collective-permute-start.3 = (bf16[768,256]{1,0:T(8,128)(2,1)}, bf16[768,256]{1,0:T(8,128)(2,1)S(1)}, u32[]{:S(2)}, u32[]{:S(2)}) collective-permute-start(bf16[768,256]{1,0:T(8,128)(2,1)} %get-tuple-element.17), channel_id=1, source_target_pairs={{0,2},{1,3},{2,4},{3,5},{4,6},{5,7},{6,0},{7,1},{8,10},{9,11},{10,... | collective-permute-start | bytes 1179656 | tf_op jit(solution)/shard_map/ppermute | solution.py:364
  57.8 46.2 %collective-permute-start.4 = (bf16[768,256]{1,0:T(8,128)(2,1)}, bf16[768,256]{1,0:T(8,128)(2,1)S(1)}, u32[]{:S(2)}, u32[]{:S(2)}) collective-permute-start(bf16[768,256]{1,0:T(8,128)(2,1)} %get-tuple-element.18), channel_id=1, source_target_pairs={{0,6},{1,7},{2,0},{3,1},{4,2},{5,3},{6,4},{7,5},{8,14},{9,15},{10,... | collective-permute-start | bytes 1179656 | tf_op jit(solution)/shard_map/ppermute | solution.py:364
  87.3 16.6 %copy-start.20 = (f32[336]{0:T(512)S(1)}, f32[336]{0:T(512)}, u32[]{:S(2)}) copy-start(f32[336]{0:T(512)} %eq.55) | copy-start | bytes 4036
  89.8 9.3 %copy-start.16 = (bf16[768,256]{1,0:T(8,128)(2,1)S(1)}, bf16[768,256]{1,0:T(8,128)(2,1)}, u32[]{:S(2)}) copy-start(bf16[768,256]{1,0:T(8,128)(2,1)} %copy-done.15) | copy-start | bytes 1179652
  96.4 22.6 %collective-permute-start.5 = (bf16[768,256]{1,0:T(8,128)(2,1)}, bf16[768,256]{1,0:T(8,128)(2,1)S(1)}, u32[]{:S(2)}, u32[]{:S(2)}) collective-permute-start(bf16[768,256]{1,0:T(8,128)(2,1)} %copy-done.17), channel_id=1, source_target_pairs={{0,1},{1,2},{2,3},{3,4},{4,5},{5,6},{6,7},{7,0},{8,9},{9,10},{10,1... | collective-permute-start | bytes 1179656 | tf_op jit(solution)/shard_map/ppermute | solution.py:364
  99.2 23.3 %collective-permute-start.6 = (bf16[768,256]{1,0:T(8,128)(2,1)S(1)}, bf16[768,256]{1,0:T(8,128)(2,1)S(1)}, u32[]{:S(2)}, u32[]{:S(2)}) collective-permute-start(bf16[768,256]{1,0:T(8,128)(2,1)S(1)} %copy-done.16), channel_id=1, source_target_pairs={{0,7},{1,0},{2,1},{3,2},{4,3},{5,4},{6,5},{7,6},{8,15},{9,8},{10,9... | collective-permute-start | bytes 1179656 | tf_op jit(solution)/shard_map/ppermute | solution.py:364
  122.4 15.3 %copy-start.4 = (bf16[1024,1024]{1,0:T(8,128)(2,1)S(1)}, bf16[1024,1024]{1,0:T(8,128)(2,1)}, u32[]{:S(2)}) copy-start(bf16[1024,1024]{1,0:T(8,128)(2,1)} %constant.106.clone.odd_ref) | copy-start | bytes 6291460
  122.4 15.3 %copy-start.5 = (bf16[512,512]{1,0:T(8,128)(2,1)S(1)}, bf16[512,512]{1,0:T(8,128)(2,1)}, u32[]{:S(2)}) copy-start(bf16[512,512]{1,0:T(8,128)(2,1)} %constant.104.clone.zero_ref) | copy-start | bytes 1572868
  122.4 15.3 %copy-start.6 = (bf16[512,512]{1,0:T(8,128)(2,1)S(1)}, bf16[512,512]{1,0:T(8,128)(2,1)}, u32[]{:S(2)}) copy-start(bf16[512,512]{1,0:T(8,128)(2,1)} %constant.105.clone.two_ref) | copy-start | bytes 1572868
  (8 other events, 8.1 us)

commit v3 on v2

--- a/solution.py
+++ b/solution.py
@@ -27,11 +27,13 @@
 CLASS = NB // FOLD
 QUARTER = NT // FOLD
 LAGQ = NLAG // FOLD
-VMEM = 32 * 1024 * 1024
+VMEM = 58 * 1024 * 1024
+VMEM_SMALL = 20 * 1024 * 1024
 BLOCK = 256
 META = 16
 
-SENT = (4, 3, 5, 2, 6, 1, 7)
+SENT = (1, 7, 4, 3, 5, 2, 6)
+LATEST = 2
 
 
 ORDER = np.arange(NB).reshape(CLASS, FOLD).T.reshape(-1)
@@ -60,8 +62,7 @@
         ],
         axis=0,
     )
-    counts = band.astype(np.float32).sum(axis=0)
-    return table, (1.0 / counts)[None, :].astype(np.float32)
+    return table
 
 
 def inverse_tables():
@@ -94,9 +95,9 @@
 def spectra_kernel(relative, with_meta, *refs):
     f32, bf16 = jnp.float32, jnp.bfloat16
     refs = list(refs)
-    order_ref = refs.pop(0) if relative else None
-    x_ref, mask_ref, owner_ref, bins_ref, table_ref, inverse_ref = refs[:6]
-    out_refs = refs[6:-7]
+    here_ref = refs.pop(0) if relative else None
+    x_ref, mask_ref, owner_ref, bins_ref, table_ref = refs[:5]
+    out_refs = refs[5:-7]
     u, v, a, b, early, others, hold = refs[-7:]
     part = pl.program_id(1)
     rows = x_ref.shape[0]
@@ -128,7 +129,10 @@
             real, imag = ref[:, start:start + CLASS], ref[:, start + CLASS:start + 2 * CLASS]
             power.append((real * real + imag * imag).astype(bf16))
         power = jnp.concatenate(power, axis=1)
-        mean = jnp.dot(power, table_ref[...], preferred_element_type=f32) * inverse_ref[...]
+        lane = lax.broadcasted_iota(jnp.int32, (1, NB), 1)
+        bin_ = (lane % CLASS) * FOLD + lane // CLASS
+        within = jnp.minimum(bin_ + HW, NB - 1) - jnp.maximum(bin_ - HW, 0) + 1
+        mean = jnp.dot(power, table_ref[...], preferred_element_type=f32) * (1.0 / within.astype(f32))
         shape = (LANES, LANES)
         diagonal = lax.broadcasted_iota(jnp.int32, shape, 0) == lax.broadcasted_iota(jnp.int32, shape, 1)
         mask = jnp.where(diagonal, jnp.broadcast_to(mask_ref[...], shape), 0).astype(f32)
@@ -158,12 +162,11 @@
                 target[piece, at, LANES:LANES + tiles] = jnp.broadcast_to(labels, (META, tiles)).astype(bf16)
         if relative:
             for slot in range(SLICES):
-                out_refs[slot][...] = target[order_ref[slot]]
-
-
-def spectra(traces, mask, owners, bins, first_row, rows, order=None, with_meta=False):
-    table, inverse = forward_tables()
-    block, relative = BLOCK, order is not None
+                out_refs[slot][...] = target[lax.rem(here_ref[0] + slot, SLICES)]
+
+
+def spectra(traces, mask, owners, bins, first_row, rows, here=None, with_meta=False):
+    block, relative = BLOCK, here is not None
     skip = first_row // block
     whole = lambda shape: pl.BlockSpec(shape, lambda i, p, *_: (0, 0))
     in_specs = [
@@ -172,7 +175,6 @@
         whole(owners.shape),
         whole(bins.shape),
         pl.BlockSpec((QUARTER, NB), lambda i, p, *_: (p, 0)),
-        whole(inverse.shape),
     ]
     f32, bf16 = jnp.float32, jnp.bfloat16
     scratch = [pltpu.VMEM((2 * block, QUARTER), bf16)] * 4
@@ -200,7 +202,7 @@
             flops=14 * rows * NB * NB, bytes_accessed=rows * NT * 3 + 8 * NB * NB, transcendentals=rows * NB
         ),
         name="spectra",
-    )(*([order] if relative else []), traces, mask, owners, bins, jnp.asarray(table), inverse)
+    )(*([here] if relative else []), traces, mask, owners, bins, jnp.asarray(forward_tables()))
     return result if relative else result[0]
 
 
@@ -241,13 +243,22 @@
     f32 = jnp.float32
     refs = list(refs)
     before_ref = refs.pop(-3) if has_before else None
-    *block_refs, scale_ref, onehot_ref, out_ref, tiles = refs
+    *block_refs, rows_ref, out_ref, tiles = refs
     if split:
         block_refs = [block_refs[0].at[m] for m in range(block_refs[0].shape[0])]
     pair_sums(block_refs, pairs, steps, tiles)
-    high, low = two_terms(tiles[...] * scale_ref[...])
-    stacked = jnp.dot(onehot_ref[...], high, preferred_element_type=f32)
-    stacked += jnp.dot(onehot_ref[...], low, preferred_element_type=f32)
+    bins, count = out_ref.shape[-2], tiles.shape[0]
+    wanted = rows_ref[0:1, :] == lax.broadcasted_iota(jnp.int32, (bins, count), 0).astype(f32)
+    high, low = two_terms(tiles[...])
+    stacked = []
+    for half in range(2):
+        weights = jnp.where(wanted, jnp.broadcast_to(rows_ref[half + 1:half + 2, :], (bins, count)), 0.0)
+        weights = jnp.concatenate(two_terms(weights), axis=0)
+        at = slice(half * LANES, (half + 1) * LANES)
+        both = jnp.dot(weights, high[:, at], preferred_element_type=f32)
+        both = both[:bins] + both[bins:]
+        stacked.append(both + jnp.dot(weights[:bins], low[:, at], preferred_element_type=f32))
+    stacked = jnp.concatenate(stacked, axis=1)
     if has_before:
         stacked += before_ref[...]
     if len(out_ref.shape) == 2:
@@ -257,28 +268,77 @@
             out_ref[copy] = stacked.astype(out_ref.dtype)
 
 
-def cross(blocks, pairs, rows, scale, onehot, before=None, copies=None):
-    bins = onehot.shape[0]
+def cross(blocks, pairs, steps, bins, weights, before=None, copies=None):
     shape = (bins, 2 * LANES)
     split = not isinstance(blocks, (list, tuple))
-    inputs = ([blocks] if split else list(blocks)) + [scale, onehot]
+    inputs = ([blocks] if split else list(blocks)) + [weights]
     if before is not None:
         inputs.append(before)
     if copies is None:
         out_shape = jax.ShapeDtypeStruct(shape, jnp.float32)
     else:
         out_shape = jax.ShapeDtypeStruct((copies,) + shape, jnp.bfloat16)
-    moved = sum(4 * rows * LANES for _ in range(len(pairs)))
     return pl.pallas_call(
-        functools.partial(cross_kernel, split, pairs, rows // G, before is not None),
+        functools.partial(cross_kernel, split, pairs, steps, before is not None),
         out_shape=out_shape,
         scratch_shapes=[pltpu.VMEM((len(pairs) * G, 2 * LANES), jnp.float32)],
-        compiler_params=pltpu.CompilerParams(vmem_limit_bytes=VMEM),
+        compiler_params=pltpu.CompilerParams(vmem_limit_bytes=VMEM_SMALL if copies is None or not split else VMEM),
         cost_estimate=pl.CostEstimate(
-            flops=8 * rows * LANES * len(pairs), bytes_accessed=moved, transcendentals=0
+            flops=8 * G * steps * LANES * len(pairs), bytes_accessed=4 * G * steps * LANES * len(pairs), transcendentals=0
         ),
         name="cross",
     )(*inputs)
+
+
+def weights_kernel(blocks, total_segs, here_ref, meta_ref, *refs):
+    f32, bf16 = jnp.float32, jnp.bfloat16
+    meta = jnp.concatenate([meta_ref[b, 0:1, :] for b in range(blocks)], axis=0)
+    masks, labels = meta[:, :LANES], meta[:, LANES:]
+    empty = jnp.zeros((R, LANES), bf16)
+    padded = jnp.concatenate([masks.astype(f32), empty.astype(f32)], axis=0)
+    half = len(refs) // 2
+    for ends_ref, out_ref in zip(refs[:half], refs[half:]):
+        lanes = out_ref.shape[1]
+        first, second = ends_ref[0:1, :], ends_ref[1:2, :]
+        slots = first < 0
+        held = [jnp.where(slots, lax.rem(here_ref[0] + end + 2 * blocks, blocks), end) for end in (first, second)]
+        low, far = jnp.minimum(held[0], held[1]), jnp.abs(held[0] - held[1])
+        sign = jnp.where(held[0] < held[1], 1.0, -1.0)
+        block = lax.broadcasted_iota(jnp.int32, (blocks, lanes), 0)
+        group = lax.broadcasted_iota(jnp.int32, (LANES, lanes), 1) % G
+        place = lax.broadcasted_iota(jnp.int32, (LANES, lanes), 0)
+        chosen = (place == (far - 1) * G + group).astype(f32).astype(bf16)
+        label = jnp.dot(labels, chosen, preferred_element_type=f32)
+        label = jnp.sum(jnp.where(block == low, label, 0.0), axis=0, keepdims=True)
+        member = (place // (LANES // G) == group).astype(f32).astype(bf16)
+        count = jnp.zeros((1, lanes), f32)
+        for d in range(1, R + 1):
+            both = (padded[:blocks] * padded[d:d + blocks]).astype(bf16)
+            of_block = jnp.dot(both, member, preferred_element_type=f32)
+            count += jnp.sum(jnp.where((block == low) & (far == d), of_block, 0.0), axis=0, keepdims=True)
+        scale = jnp.where(far <= R, 1.0 / (total_segs * jnp.maximum(count, 1.0)), 0.0)
+        out_ref[...] = jnp.concatenate([label, scale, scale * sign, jnp.zeros((5, lanes), f32)], axis=0)
+
+
+def pair_weights(here, meta, at, total_segs, pair_lists):
+    blocks = meta.shape[0]
+    ends = [jnp.asarray(np.repeat(np.array(pairs, np.int32).T, G, axis=1)) for pairs in pair_lists]
+    whole = lambda shape: pl.BlockSpec(shape, lambda i, *_: (0, 0))
+    shapes = [(8, G * len(pairs)) for pairs in pair_lists]
+    return pl.pallas_call(
+        functools.partial(weights_kernel, blocks, total_segs),
+        grid_spec=pltpu.PrefetchScalarGridSpec(
+            num_scalar_prefetch=1,
+            grid=(1,),
+            in_specs=[pl.BlockSpec((blocks, META, 2 * LANES), lambda i, *_: (0, at // META, 0))]
+            + [whole(end.shape) for end in ends],
+            out_specs=[whole(shape) for shape in shapes],
+        ),
+        out_shape=[jax.ShapeDtypeStruct(shape, jnp.float32) for shape in shapes],
+        compiler_params=pltpu.CompilerParams(vmem_limit_bytes=VMEM_SMALL),
+        name="weights",
+    )(here, meta, *ends)
+
 
 def lags_kernel(stacks_ref, zero_ref, two_ref, odd_ref, out_ref):
     f32 = jnp.float32
@@ -309,83 +369,40 @@
     return pl.pallas_call(
         lags_kernel,
         out_shape=jax.ShapeDtypeStruct((BIN_DEV, NLAG), jnp.float32),
-        compiler_params=pltpu.CompilerParams(vmem_limit_bytes=VMEM // 2),
+        compiler_params=pltpu.CompilerParams(vmem_limit_bytes=VMEM_SMALL),
         name="lags",
     )(stacks, *tables)
 
 
-def weights_of(masks, labels, low, far, sign, total_segs):
-    blocks = masks.shape[0]
-    valid = (far >= 1) & (far <= R) & (low + far < blocks)
-    far = jnp.where(valid, far, 1)
-    other = jnp.minimum(low + far, blocks - 1)
-    groups = masks.reshape(blocks, G, -1)
-    counts = jnp.sum(groups[low] * groups[other], axis=2)
-    scale = jnp.where(valid[:, None], 1.0 / (total_segs * jnp.maximum(counts, 1.0)), 0.0)
-    chosen = labels.reshape(blocks, R, G)[low, far - 1].reshape(-1)
-    half = jnp.repeat(jnp.stack([jnp.ones_like(sign), sign], axis=1), LANES, axis=1)
-    wide = (scale[:, :, None] * half[:, None, :]).reshape(-1, 2 * LANES)
-    bins = jnp.arange(blocks * BIN_DEV, dtype=jnp.float32)
-    return wide, (chosen[None, :] == bins[:, None]).astype(jnp.bfloat16)
-
-
 def fixed_pairs(blocks):
     return [(b, b + d) for b in range(blocks) for d in range(1, R + 1) if b + d < blocks]
-
-
-def fixed_weights(masks, labels, total_segs):
-    pairs = np.array(fixed_pairs(masks.shape[0]))
-    low, far = jnp.asarray(pairs[:, 0]), jnp.asarray(pairs[:, 1] - pairs[:, 0])
-    return weights_of(masks, labels, low, far, jnp.ones((len(pairs),), jnp.float32), total_segs)
-
-
-def slot_weights(masks, labels, pairs, total_segs):
-    blocks = masks.shape[0]
-    here = lax.axis_index("chan")
-    slots = jnp.asarray(np.array(pairs))
-    held = (here - slots) % blocks
-    low, high = jnp.min(held, axis=1), jnp.max(held, axis=1)
-    sign = jnp.where(held[:, 0] < held[:, 1], 1.0, -1.0)
-    return weights_of(masks, labels, low, high - low, sign, total_segs)
 
 
 def sent_along(x, mask, owners, bins, total_segs):
     seg_count = lax.axis_size("seg")
     count = lax.axis_size("chan")
-    rows, chans = x.shape[0], mask.shape[1]
     early = BLOCK
-    late = rows - early
+    late = x.shape[0] - early
+    here = lax.axis_index("chan").astype(jnp.int32).reshape(1)
     first = spectra(x, mask, owners, bins, 0, early, with_meta=True)
     first = lax.all_to_all(first, "chan", split_axis=0, concat_axis=0, tiled=True)
-    order = (lax.axis_index("chan") + jnp.arange(count, dtype=jnp.int32)) % count
-    second = spectra(x, mask, owners, bins, early, late, order=order)
+    second = spectra(x, mask, owners, bins, early, late, here=here)
     slots = {0: second[0]}
     for shift in SENT:
         slots[shift] = lax.ppermute(second[shift], "chan", [(i, (i + shift) % count) for i in range(count)])
 
-    meta = first[:, early, :].astype(jnp.float32)
-    masks, labels = meta[:, :chans], meta[:, LANES:LANES + owners.shape[1]]
-    stacks = cross(first, fixed_pairs(count), early, *fixed_weights(masks, labels, total_segs))
-    known = (0,) + SENT[:-1]
-    pairs = [(known[i], known[j]) for i in range(len(known)) for j in range(i + 1, len(known))]
-    at = {slot: i for i, slot in enumerate(known)}
-    stacks = cross(
-        [slots[slot] for slot in known],
-        [(at[p], at[q]) for p, q in pairs],
-        late,
-        *slot_weights(masks, labels, pairs, total_segs),
-        before=stacks,
-    )
+    fixed = fixed_pairs(count)
     known = (0,) + SENT
-    pairs = [(slot, SENT[-1]) for slot in known[:-1]]
-    return cross(
-        [slots[slot] for slot in known],
-        [(i, len(known) - 1) for i in range(len(known) - 1)],
-        late,
-        *slot_weights(masks, labels, pairs, total_segs),
-        before=stacks,
-        copies=seg_count,
-    )
+    before = len(known) - LATEST
+    soon = [(i, j) for j in range(1, before) for i in range(j)]
+    last = [(i, j) for j in range(before, len(known)) for i in range(j)]
+    as_slots = lambda pairs: [(-known[i] - count, -known[j] - count) for i, j in pairs]
+    weights = pair_weights(here, first, early, total_segs, [fixed, as_slots(soon), as_slots(last)])
+    rows = count * BIN_DEV
+    stacks = cross(first, fixed, early // G, rows, weights[0])
+    held = [slots[slot] for slot in known]
+    stacks = cross(held[:before], soon, late // G, rows, weights[1], before=stacks)
+    return cross(held, last, late // G, rows, weights[2], before=stacks, copies=seg_count)
 
 
 def sent_at_once(x, mask, owners, bins, total_segs):
@@ -394,16 +411,20 @@
     rows, chans = x.shape[0], mask.shape[1]
     narrow = NB // count
     splits = LANES // narrow
+    here = lax.axis_index("chan").astype(jnp.int32).reshape(1)
     own = jnp.concatenate([mask, owners * BIN_DEV + bins], axis=1)
-    every = lax.all_gather(own, "chan", axis=0, tiled=True).astype(jnp.float32)
-    masks, labels = every[:, :chans], every[:, chans:]
+    every = lax.all_gather(own, "chan", axis=0, tiled=True).astype(jnp.bfloat16)
+    every = jnp.pad(every, ((0, 0), (0, 2 * LANES - every.shape[1])))
+    every = jnp.broadcast_to(every[:, None, :], (count, META, 2 * LANES))
+    fixed = fixed_pairs(count)
+    weights = pair_weights(here, every, 0, total_segs, [fixed])
     outgoing = spectra(x, mask, owners, bins, 0, rows)
     outgoing = outgoing.reshape(SLICES, rows, 2, splits, narrow).transpose(0, 3, 1, 2, 4)
     outgoing = outgoing.reshape(count, rows, 2 * narrow)
     wide = lax.all_to_all(outgoing, "chan", split_axis=0, concat_axis=0, tiled=True)
     wide = jnp.pad(wide.reshape(count, rows, 2, narrow), ((0, 0), (0, 0), (0, 0), (0, LANES - narrow)))
     wide = wide.reshape(count, rows, 2 * LANES)
-    stacks = cross(wide, fixed_pairs(count), rows, *fixed_weights(masks, labels, total_segs), copies=seg_count)
+    stacks = cross(wide, fixed, rows // G, count * BIN_DEV, weights[0], copies=seg_count)
     return stacks.reshape(-1, 2, LANES)[..., :narrow]
 
 

time: 140 us -> 128 us (0.914)
  local copies, waits for them, and re-layouts: 39 us -> 0.04 us
  waiting for transfers between devices: 19.8 us -> 52.7 us
  other arithmetic: 11.5 us -> 0 us
  Pallas kernels: 31.8 us -> 40.5 us
  starting transfers between devices: 22.8 us -> 19 us
  blocking collectives: 13.7 us -> 15.7 us
    ppermute x7, waiting for transfers between devices: 19.8 us -> 52.7 us  [sent_along(): lax.ppermute(second[shift], 'chan', [(i, (i + shift) % count) for i in ra...]
    unnamed x53 -> x14, local copies, waits for them, and re-layouts: 19.6 us -> 0.04 us
    gather x9 -> x0, local copies, waits for them, and re-layouts: 11.4 us -> none  [the longest x6 7.69 us: weights_of(): counts = jnp.sum(groups[low] * groups[other], axis=2)]
    pallas_call x2, Pallas kernels: 24.4 us -> 31.6 us  [spectra(): pl.pallas_call(functools.partial(spectra_kernel, relative, with_meta), gr...]
    ppermute x7, starting transfers between devices: 15.3 us -> 11.7 us  [sent_along(): lax.ppermute(second[shift], 'chan', [(i, (i + shift) % count) for i in ra...]
    reduce_sum x3 -> x0, other arithmetic: 3.18 us -> none  [weights_of(): counts = jnp.sum(groups[low] * groups[other], axis=2)]
    eq x3 -> x0, local copies, waits for them, and re-layouts: 2.82 us -> none  [weights_of(): return (wide, (chosen[None, :] == bins[:, None]).astype(jnp.bfloat16))]
    select_n x3 -> x0, local copies, waits for them, and re-layouts: 2.1 us -> none  [weights_of(): jnp.where(valid[:, None], 1.0 / (total_segs * jnp.maximum(counts, 1.0)),...]
  transfers between devices with their start and end apart: 8 -> 8, of which waited for: 2 -> 4; matrix products, arithmetic and copies ran while one was open for 23% -> 0% of each run, Pallas kernels for 16% -> 21%
where the time goes in v3:
time: 128 us
  waiting for transfers between devices  52.7 us (41%)
  Pallas kernels  40.5 us (32%)
  starting transfers between devices  19 us (15%)
  blocking collectives  15.7 us (12%)
    ppermute x7, waiting for transfers between devices, sent_along(): lax.ppermute(second[shift], 'chan', [(i, (i + shift) % count) for i in ra...  52.7 us
    pallas_call x2, Pallas kernels, spectra(): pl.pallas_call(functools.partial(spectra_kernel, relative, with_meta), gr...  31.6 us
    all_to_all x1, blocking collectives, per_device(): lax.all_to_all(stacks, ('seg', 'chan'), split_axis=0, concat_axis=0, tile...  15.7 us
    ppermute x7, starting transfers between devices, sent_along(): lax.ppermute(second[shift], 'chan', [(i, (i + shift) % count) for i in ra...  11.7 us
    pallas_call x3, Pallas kernels, cross(): pl.pallas_call(functools.partial(cross_kernel, split, pairs, steps, befor...  7.5 us
    all_to_all x1, starting transfers between devices, sent_along(): lax.all_to_all(first, 'chan', split_axis=0, concat_axis=0, tiled=True)  7.29 us
  transfers between devices with their start and end apart: 8, of which 4 were waited for; matrix products, arithmetic and copies ran while one was open for 0% of the time, Pallas kernels for 21%

profile of v3, /device:TPU:0, one launch (start us, length us, event | category | flops | bytes accessed | tf_op | source)
XLA Modules:
  0.0 128.0 jit_solution(14981563509933220574)
XLA Ops:
  0.0 9.0 %spectra.3 = bf16[8,272,256]{2,1,0:T(8,128)(2,1)} custom-call(bf16[1024,4096]{1,0:T(8,128)(2,1)} %bitcast.6, s32[1,128]{1,0:T(1,128)} %bitcast.8, s32[1,64]{1,0:T(1,128)} %bitcast.10, s32[1,64]{1,0:T(1,128)} %refs_3_.1, bf16[4096,1024]{1,0:T(8,128)(2,1)} %constant.18.clone.refs_5_.refs_4_), custom_call_target="tpu_custom_call" | custom-call | flops 3758096384 | bytes 11534336 | tf_op jit(solution)/shard_map/spectra/pallas_call | solution.py:190
  9.0 7.3 %all-to-all-start = ((bf16[8,272,256]{2,1,0:T(8,128)(2,1)}), bf16[8,272,256]{2,1,0:T(8,128)(2,1)S(1)}, u32[]{:S(2)}, u32[]{:S(2)}) async-start(bf16[8,272,256]{2,1,0:T(8,128)(2,1)} %spectra.3), calls=%async_computation | async-start | bytes 2228224 | tf_op jit(solution)/shard_map/all_to_all | solution.py:388
  16.3 0.0 copy-start.5
  16.3 0.0 copy-start.6
  16.3 22.6 %spectra.2 = (bf16[768,256]{1,0:T(8,128)(2,1)}, bf16[768,256]{1,0:T(8,128)(2,1)}, bf16[768,256]{1,0:T(8,128)(2,1)}, bf16[768,256]{1,0:T(8,128)(2,1)}, bf16[768,2...) custom-call(s32[1]{0:T(128)} %bitcast.refs_0_.here_ref, ...), custom_call_target="tpu_custom_call" | custom-call | flops 11274289152 | bytes 17825792 | tf_op jit(solution)/shard_map/spectra/pallas_call | solution.py:190
  38.9 2.0 %collective-permute-start = (bf16[768,256]{1,0:T(8,128)(2,1)}, bf16[768,256]{1,0:T(8,128)(2,1)S(1)}, u32[]{:S(2)}, u32[]{:S(2)}) collective-permute-start(bf16[768,256]{1,0:T(8,128)(2,1)} %get-tuple-element.17), channel_id=1, source_target_pairs={{0,1},{1,2},{2,3},{3,4},{4,5},{5,6},{6,7},{7,0},{8,9},{9,10},{10,1... | collective-permute-start | bytes 1179656 | tf_op jit(solution)/shard_map/ppermute | solution.py:392
  40.9 2.8 %collective-permute-start.1 = (bf16[768,256]{1,0:T(8,128)(2,1)}, bf16[768,256]{1,0:T(8,128)(2,1)S(1)}, u32[]{:S(2)}, u32[]{:S(2)}) collective-permute-start(bf16[768,256]{1,0:T(8,128)(2,1)} %get-tuple-element.18), channel_id=1, source_target_pairs={{0,7},{1,0},{2,1},{3,2},{4,3},{5,4},{6,5},{7,6},{8,15},{9,8},{10,9... | collective-permute-start | bytes 1179656 | tf_op jit(solution)/shard_map/ppermute | solution.py:392
  43.7 1.1 collective-permute-start.2
  44.8 1.5 %collective-permute-start.3 = (bf16[768,256]{1,0:T(8,128)(2,1)}, bf16[768,256]{1,0:T(8,128)(2,1)S(1)}, u32[]{:S(2)}, u32[]{:S(2)}) collective-permute-start(bf16[768,256]{1,0:T(8,128)(2,1)} %get-tuple-element.20), channel_id=1, source_target_pairs={{0,3},{1,4},{2,5},{3,6},{4,7},{5,0},{6,1},{7,2},{8,11},{9,12},{10,... | collective-permute-start | bytes 1179656 | tf_op jit(solution)/shard_map/ppermute | solution.py:392
  46.2 2.4 %collective-permute-start.4 = (bf16[768,256]{1,0:T(8,128)(2,1)}, bf16[768,256]{1,0:T(8,128)(2,1)S(1)}, u32[]{:S(2)}, u32[]{:S(2)}) collective-permute-start(bf16[768,256]{1,0:T(8,128)(2,1)} %get-tuple-element.21), channel_id=1, source_target_pairs={{0,5},{1,6},{2,7},{3,0},{4,1},{5,2},{6,3},{7,4},{8,13},{9,14},{10,... | collective-permute-start | bytes 1179656 | tf_op jit(solution)/shard_map/ppermute | solution.py:392
  48.6 9.1 %collective-permute-done.refs_1_ = bf16[768,256]{1,0:T(8,128)(2,1)S(1)} collective-permute-done((bf16[768,256]{1,0:T(8,128)(2,1)}, bf16[768,256]{1,0:T(8,128)(2,1)S(1)}, u32[]{:S(2)}, u32[]{:S(2)}) %collective-permute-start) | collective-permute-done | bytes 393248 | tf_op jit(solution)/shard_map/ppermute | solution.py:392
  57.6 0.8 collective-permute-start.5
  58.4 9.6 %collective-permute-done.1.refs_2_ = bf16[768,256]{1,0:T(8,128)(2,1)S(1)} collective-permute-done((bf16[768,256]{1,0:T(8,128)(2,1)}, bf16[768,256]{1,0:T(8,128)(2,1)S(1)}, u32[]{:S(2)}, u32[]{:S(2)}) %collective-permute-start.1) | collective-permute-done | bytes 393248 | tf_op jit(solution)/shard_map/ppermute | solution.py:392
  68.0 1.2 collective-permute-start.6
  69.2 0.3 weights.1
  69.5 1.3 %cross.3.refs_7_ = f32[64,256]{1,0:T(8,128)S(1)} custom-call(bf16[8,272,256]{2,1,0:T(8,128)(2,1)S(1)} %all-to-all-done.meta_ref.refs_0_, f32[8,352]{1,0:T(8,128)S(1)} %get-tuple-element.26.refs_1_), custom_call_target="tpu_custom_call" | custom-call | flops 5767168 | bytes 2883584 | tf_op jit(solution)/shard_map/cross/pallas_call | solution.py:281
  70.8 26.4 %collective-permute-done.2.refs_3_ = bf16[768,256]{1,0:T(8,128)(2,1)S(1)} collective-permute-done((bf16[768,256]{1,0:T(8,128)(2,1)}, bf16[768,256]{1,0:T(8,128)(2,1)S(1)}, u32[]{:S(2)}, u32[]{:S(2)}) %collective-permute-start.2) | collective-permute-done | bytes 393248 | tf_op jit(solution)/shard_map/ppermute | solution.py:392
  97.2 2.4 %cross.4.refs_9_ = f32[64,256]{1,0:T(8,128)S(1)} custom-call(bf16[768,256]{1,0:T(8,128)(2,1)S(1)} %copy-done.1, bf16[768,256]{1,0:T(8,128)(2,1)S(1)} %collective-permute-done.refs_1_, bf16[768,256]{1,0:T(8,128)(2,1)S(1)} %collective-permute-done.1.refs_2_, bf16[768,256]{1,0:T(8,128)(2,1)S(1)} %collective-permute-done.2.refs_3_, ...), custom_call_target="tpu_custom_call" | custom-call | flops 11796480 | bytes 5898240 | tf_op jit(solution)/shard_map/cross/pallas_call | solution.py:281
  99.7 0.0 copy-start
  99.7 0.0 copy-start.2
  99.7 7.7 %collective-permute-done.6.refs_7_ = bf16[768,256]{1,0:T(8,128)(2,1)} collective-permute-done((bf16[768,256]{1,0:T(8,128)(2,1)}, bf16[768,256]{1,0:T(8,128)(2,1)}, u32[]{:S(2)}, u32[]{:S(2)}) %collective-permute-start.6) | collective-permute-done | bytes 393248 | tf_op jit(solution)/shard_map/ppermute | solution.py:392
  107.4 3.7 %cross.5 = bf16[4,64,256]{2,1,0:T(8,128)(2,1)S(1)} custom-call(bf16[768,256]{1,0:T(8,128)(2,1)S(1)} %copy-done.1, bf16[768,256]{1,0:T(8,128)(2,1)S(1)} %collective-permute-done.refs_1_, bf16[768,256]{1,0:T(8,128)(2,1)S(1)} %collective-permute-done.1.refs_2_, bf16[768,256]{1,0:T(8,128)(2,1)S(1)} %collective-permute-done.2.refs_3_, ...), custom_call_target="tpu_custom_call" | custom-call | flops 10223616 | bytes 5111808 | tf_op jit(solution)/shard_map/cross/pallas_call | solution.py:281
  111.1 15.7 %all_to_all.10.stacks_ref = bf16[32,8,256]{2,1,0:T(8,128)(2,1)S(1)} all-to-all(bf16[32,8,256]{2,1,0:T(8,128)(2,1)S(1)} %bitcast.5), channel_id=1, replica_groups=mesh['seg'=4,'chan'=8] {'seg','chan'}, dimensions={0} | all-to-all | bytes 262144 | tf_op jit(solution)/shard_map/all_to_all | solution.py:441
  126.8 1.2 lags.1
  (14 shorter events, 0.0 us)
Async XLA Ops:
  9.0 60.2 %all-to-all-start = ((bf16[8,272,256]{2,1,0:T(8,128)(2,1)}), bf16[8,272,256]{2,1,0:T(8,128)(2,1)S(1)}, u32[]{:S(2)}, u32[]{:S(2)}) async-start(bf16[8,272,256]{2,1,0:T(8,128)(2,1)} %spectra.3), calls=%async_computation | async-start | bytes 2228224 | tf_op jit(solution)/shard_map/all_to_all | solution.py:388
  16.3 52.9 %copy-start.4 = (s32[2,352]{1,0:T(2,128)S(1)}, s32[2,352]{1,0:T(2,128)}, u32[]{:S(2)}) copy-start(s32[2,352]{1,0:T(2,128)} %constant.19.clone.refs_0_) | copy-start | bytes 8452
  16.3 52.9 %copy-start.5 = (s32[2,208]{1,0:T(2,128)S(1)}, s32[2,208]{1,0:T(2,128)}, u32[]{:S(2)}) copy-start(s32[2,208]{1,0:T(2,128)} %constant.21.clone.refs_2_) | copy-start | bytes 4996
  16.3 52.9 %copy-start.6 = (s32[2,240]{1,0:T(2,128)S(1)}, s32[2,240]{1,0:T(2,128)}, u32[]{:S(2)}) copy-start(s32[2,240]{1,0:T(2,128)} %constant.20.clone.refs_1_) | copy-start | bytes 5764
  38.9 58.4 %copy-start.1 = (bf16[768,256]{1,0:T(8,128)(2,1)S(1)}, bf16[768,256]{1,0:T(8,128)(2,1)}, u32[]{:S(2)}) copy-start(bf16[768,256]{1,0:T(8,128)(2,1)} %get-tuple-element.16.refs_0_) | copy-start | bytes 1179652
  38.9 18.8 %collective-permute-start = (bf16[768,256]{1,0:T(8,128)(2,1)}, bf16[768,256]{1,0:T(8,128)(2,1)S(1)}, u32[]{:S(2)}, u32[]{:S(2)}) collective-permute-start(bf16[768,256]{1,0:T(8,128)(2,1)} %get-tuple-element.17), channel_id=1, source_target_pairs={{0,1},{1,2},{2,3},{3,4},{4,5},{5,6},{6,7},{7,0},{8,9},{9,10},{10,1... | collective-permute-start | bytes 1179656 | tf_op jit(solution)/shard_map/ppermute | solution.py:392
  40.9 27.1 %collective-permute-start.1 = (bf16[768,256]{1,0:T(8,128)(2,1)}, bf16[768,256]{1,0:T(8,128)(2,1)S(1)}, u32[]{:S(2)}, u32[]{:S(2)}) collective-permute-start(bf16[768,256]{1,0:T(8,128)(2,1)} %get-tuple-element.18), channel_id=1, source_target_pairs={{0,7},{1,0},{2,1},{3,2},{4,3},{5,4},{6,5},{7,6},{8,15},{9,8},{10,9... | collective-permute-start | bytes 1179656 | tf_op jit(solution)/shard_map/ppermute | solution.py:392
  43.7 53.5 %collective-permute-start.2 = (bf16[768,256]{1,0:T(8,128)(2,1)}, bf16[768,256]{1,0:T(8,128)(2,1)S(1)}, u32[]{:S(2)}, u32[]{:S(2)}) collective-permute-start(bf16[768,256]{1,0:T(8,128)(2,1)} %get-tuple-element.19), channel_id=1, source_target_pairs={{0,4},{1,5},{2,6},{3,7},{4,0},{5,1},{6,2},{7,3},{8,12},{9,13},{10,... | collective-permute-start | bytes 1179656 | tf_op jit(solution)/shard_map/ppermute | solution.py:392
  44.8 52.5 %collective-permute-start.3 = (bf16[768,256]{1,0:T(8,128)(2,1)}, bf16[768,256]{1,0:T(8,128)(2,1)S(1)}, u32[]{:S(2)}, u32[]{:S(2)}) collective-permute-start(bf16[768,256]{1,0:T(8,128)(2,1)} %get-tuple-element.20), channel_id=1, source_target_pairs={{0,3},{1,4},{2,5},{3,6},{4,7},{5,0},{6,1},{7,2},{8,11},{9,12},{10,... | collective-permute-start | bytes 1179656 | tf_op jit(solution)/shard_map/ppermute | solution.py:392
  46.2 51.0 %collective-permute-start.4 = (bf16[768,256]{1,0:T(8,128)(2,1)}, bf16[768,256]{1,0:T(8,128)(2,1)S(1)}, u32[]{:S(2)}, u32[]{:S(2)}) collective-permute-start(bf16[768,256]{1,0:T(8,128)(2,1)} %get-tuple-element.21), channel_id=1, source_target_pairs={{0,5},{1,6},{2,7},{3,0},{4,1},{5,2},{6,3},{7,4},{8,13},{9,14},{10,... | collective-permute-start | bytes 1179656 | tf_op jit(solution)/shard_map/ppermute | solution.py:392
  57.6 42.0 %collective-permute-start.5 = (bf16[768,256]{1,0:T(8,128)(2,1)}, bf16[768,256]{1,0:T(8,128)(2,1)}, u32[]{:S(2)}, u32[]{:S(2)}) collective-permute-start(bf16[768,256]{1,0:T(8,128)(2,1)} %get-tuple-element.22), channel_id=1, source_target_pairs={{0,2},{1,3},{2,4},{3,5},{4,6},{5,7},{6,0},{7,1},{8,10},{9,11},{10,... | collective-permute-start | bytes 1179656 | tf_op jit(solution)/shard_map/ppermute | solution.py:392
  68.0 39.4 %collective-permute-start.6 = (bf16[768,256]{1,0:T(8,128)(2,1)}, bf16[768,256]{1,0:T(8,128)(2,1)}, u32[]{:S(2)}, u32[]{:S(2)}) collective-permute-start(bf16[768,256]{1,0:T(8,128)(2,1)} %get-tuple-element.23), channel_id=1, source_target_pairs={{0,6},{1,7},{2,0},{3,1},{4,2},{5,3},{6,4},{7,5},{8,14},{9,15},{10,... | collective-permute-start | bytes 1179656 | tf_op jit(solution)/shard_map/ppermute | solution.py:392
  99.7 27.2 %copy-start = (bf16[1024,1024]{1,0:T(8,128)(2,1)S(1)}, bf16[1024,1024]{1,0:T(8,128)(2,1)}, u32[]{:S(2)}) copy-start(bf16[1024,1024]{1,0:T(8,128)(2,1)} %constant.24.clone.odd_ref) | copy-start | bytes 6291460
  99.7 27.2 %copy-start.2 = (bf16[512,512]{1,0:T(8,128)(2,1)S(1)}, bf16[512,512]{1,0:T(8,128)(2,1)}, u32[]{:S(2)}) copy-start(bf16[512,512]{1,0:T(8,128)(2,1)} %constant.23.clone.two_ref) | copy-start | bytes 1572868
  99.7 27.1 %copy-start.3 = (bf16[512,512]{1,0:T(8,128)(2,1)S(1)}, bf16[512,512]{1,0:T(8,128)(2,1)}, u32[]{:S(2)}) copy-start(bf16[512,512]{1,0:T(8,128)(2,1)} %constant.22.clone.zero_ref) | copy-start | bytes 1572868

commit v4 on v3

--- a/solution.py
+++ b/solution.py
@@ -33,7 +33,7 @@
 META = 16
 
 SENT = (1, 7, 4, 3, 5, 2, 6)
-LATEST = 2
+STAGES = (6, 7, 8)
 
 
 ORDER = np.arange(NB).reshape(CLASS, FOLD).T.reshape(-1)
@@ -96,102 +96,106 @@
     f32, bf16 = jnp.float32, jnp.bfloat16
     refs = list(refs)
     here_ref = refs.pop(0) if relative else None
-    x_ref, mask_ref, owner_ref, bins_ref, table_ref = refs[:5]
-    out_refs = refs[5:-7]
-    u, v, a, b, early, others, hold = refs[-7:]
-    part = pl.program_id(1)
+    x_ref, mask_ref, owner_ref, bins_ref, source_ref = refs[:5]
+    out_refs = refs[5:-9]
+    table_ref, arrived, u, v, a, b, early, others, hold = refs[-9:]
+    target = refs[-10] if relative else out_refs[0]
+    first = pl.program_id(0) == 0
     rows = x_ref.shape[0]
-
-    @pl.when(part == 0)
-    def fold():
-        x = [x_ref[:, m * QUARTER:(m + 1) * QUARTER].astype(f32) for m in range(FOLD)]
-        even, odd = x[0] + x[2], x[1] + x[3]
-        u[:rows], u[rows:] = two_terms(even + odd)
-        v[:rows], v[rows:] = two_terms(even - odd)
-        a[:rows], a[rows:] = two_terms(x[0] - x[2])
-        b[:rows], b[rows:] = two_terms(x[1] - x[3])
-        early[:, :2 * CLASS] = two_term_dot(u, table_ref[:, :2 * CLASS])
-        early[:, 2 * CLASS:] = two_term_dot(v, table_ref[:, 2 * CLASS:])
-
-    @pl.when(part == 1)
-    def first_half():
-        others[...] = two_term_dot(a, table_ref[...])
-
-    @pl.when(part == 2)
-    def second_half():
-        others[...] += two_term_dot(b, table_ref[...])
-
-    @pl.when(part == 3)
-    def whiten():
-        holders = [(early, 0), (others, 0), (early, 2 * CLASS), (others, 2 * CLASS)]
-        power = []
-        for ref, start in holders:
-            real, imag = ref[:, start:start + CLASS], ref[:, start + CLASS:start + 2 * CLASS]
-            power.append((real * real + imag * imag).astype(bf16))
-        power = jnp.concatenate(power, axis=1)
-        lane = lax.broadcasted_iota(jnp.int32, (1, NB), 1)
-        bin_ = (lane % CLASS) * FOLD + lane // CLASS
-        within = jnp.minimum(bin_ + HW, NB - 1) - jnp.maximum(bin_ - HW, 0) + 1
-        mean = jnp.dot(power, table_ref[...], preferred_element_type=f32) * (1.0 / within.astype(f32))
-        shape = (LANES, LANES)
-        diagonal = lax.broadcasted_iota(jnp.int32, shape, 0) == lax.broadcasted_iota(jnp.int32, shape, 1)
-        mask = jnp.where(diagonal, jnp.broadcast_to(mask_ref[...], shape), 0).astype(f32)
-        mask = jnp.sum(mask, axis=1, keepdims=True)
-        weight = jnp.concatenate([mask] * (rows // LANES), axis=0) * lax.rsqrt(mean + EPSILON)
-        per_group = LANES // G
-        target = refs[-8] if relative else out_refs[0]
+    copies = [
+        pltpu.make_async_copy(source_ref.at[part], table_ref.at[part], arrived.at[part]) for part in range(FOLD)
+    ]
+
+    @pl.when(first)
+    def start():
+        for copy in copies:
+            copy.start()
+
+    x = [x_ref[:, m * QUARTER:(m + 1) * QUARTER].astype(f32) for m in range(FOLD)]
+    even, odd = x[0] + x[2], x[1] + x[3]
+    u[:rows], u[rows:] = two_terms(even + odd)
+    v[:rows], v[rows:] = two_terms(even - odd)
+    a[:rows], a[rows:] = two_terms(x[0] - x[2])
+    b[:rows], b[rows:] = two_terms(x[1] - x[3])
+
+    pl.when(first)(copies[0].wait)
+    early[:, :2 * CLASS] = two_term_dot(u, table_ref[0, :, :2 * CLASS])
+    early[:, 2 * CLASS:] = two_term_dot(v, table_ref[0, :, 2 * CLASS:])
+    pl.when(first)(copies[1].wait)
+    others[...] = two_term_dot(a, table_ref[1])
+    pl.when(first)(copies[2].wait)
+    others[...] += two_term_dot(b, table_ref[2])
+    pl.when(first)(copies[3].wait)
+
+    holders = [(early, 0), (others, 0), (early, 2 * CLASS), (others, 2 * CLASS)]
+    power = []
+    for ref, start in holders:
+        real, imag = ref[:, start:start + CLASS], ref[:, start + CLASS:start + 2 * CLASS]
+        power.append((real * real + imag * imag).astype(bf16))
+    power = jnp.concatenate(power, axis=1)
+    lane = lax.broadcasted_iota(jnp.int32, (1, NB), 1)
+    bin_ = (lane % CLASS) * FOLD + lane // CLASS
+    within = jnp.minimum(bin_ + HW, NB - 1) - jnp.maximum(bin_ - HW, 0) + 1
+    mean = jnp.dot(power, table_ref[3], preferred_element_type=f32) * (1.0 / within.astype(f32))
+    shape = (LANES, LANES)
+    diagonal = lax.broadcasted_iota(jnp.int32, shape, 0) == lax.broadcasted_iota(jnp.int32, shape, 1)
+    mask = jnp.where(diagonal, jnp.broadcast_to(mask_ref[...], shape), 0).astype(f32)
+    mask = jnp.sum(mask, axis=1, keepdims=True)
+    weight = jnp.concatenate([mask] * (rows // LANES), axis=0) * lax.rsqrt(mean + EPSILON)
+    per_group = LANES // G
+    for piece in range(SLICES):
+        ref, start = holders[piece // 2]
+        start += (piece % 2) * LANES
+        scale = weight[:, piece * LANES:(piece + 1) * LANES]
+        hold[0] = ref[:, start:start + LANES] * scale
+        hold[1] = ref[:, CLASS + start:CLASS + start + LANES] * scale
+        for seg in range(rows // LANES):
+            for j in range(per_group):
+                at = seg * LANES + j * G
+                for half in range(2):
+                    taken = hold[half, pl.ds(seg * LANES + j, G, stride=per_group), :]
+                    target[piece, at:at + G, half * LANES:(half + 1) * LANES] = taken.astype(bf16)
+    if with_meta:
+        tiles = owner_ref.shape[1]
+        labels = (owner_ref[...] * BIN_DEV + bins_ref[...]).astype(f32)
         for piece in range(SLICES):
-            ref, start = holders[piece // 2]
-            start += (piece % 2) * LANES
-            scale = weight[:, piece * LANES:(piece + 1) * LANES]
-            hold[0] = ref[:, start:start + LANES] * scale
-            hold[1] = ref[:, CLASS + start:CLASS + start + LANES] * scale
-            for seg in range(rows // LANES):
-                for j in range(per_group):
-                    at = seg * LANES + j * G
-                    for half in range(2):
-                        taken = hold[half, pl.ds(seg * LANES + j, G, stride=per_group), :]
-                        target[piece, at:at + G, half * LANES:(half + 1) * LANES] = taken.astype(bf16)
-        if with_meta:
-            tiles = owner_ref.shape[1]
-            labels = (owner_ref[...] * BIN_DEV + bins_ref[...]).astype(f32)
-            for piece in range(SLICES):
-                at = pl.ds(rows, META)
-                target[piece, at, :] = jnp.zeros((META, 2 * LANES), bf16)
-                target[piece, at, :LANES] = jnp.broadcast_to(mask_ref[...].astype(f32), (META, LANES)).astype(bf16)
-                target[piece, at, LANES:LANES + tiles] = jnp.broadcast_to(labels, (META, tiles)).astype(bf16)
-        if relative:
-            for slot in range(SLICES):
-                out_refs[slot][...] = target[lax.rem(here_ref[0] + slot, SLICES)]
+            at = pl.ds(rows, META)
+            target[piece, at, :] = jnp.zeros((META, 2 * LANES), bf16)
+            target[piece, at, :LANES] = jnp.broadcast_to(mask_ref[...].astype(f32), (META, LANES)).astype(bf16)
+            target[piece, at, LANES:LANES + tiles] = jnp.broadcast_to(labels, (META, tiles)).astype(bf16)
+    if relative:
+        for slot in range(SLICES):
+            out_refs[slot][...] = target[lax.rem(here_ref[0] + slot, SLICES)]
 
 
 def spectra(traces, mask, owners, bins, first_row, rows, here=None, with_meta=False):
     block, relative = BLOCK, here is not None
     skip = first_row // block
-    whole = lambda shape: pl.BlockSpec(shape, lambda i, p, *_: (0, 0))
+    whole = lambda shape: pl.BlockSpec(shape, lambda i, *_: (0, 0))
     in_specs = [
-        pl.BlockSpec((block, NT), lambda i, p, *_: (i + skip, 0)),
+        pl.BlockSpec((block, NT), lambda i, *_: (i + skip, 0)),
         whole(mask.shape),
         whole(owners.shape),
         whole(bins.shape),
-        pl.BlockSpec((QUARTER, NB), lambda i, p, *_: (p, 0)),
+        pl.BlockSpec(memory_space=pl.ANY),
     ]
     f32, bf16 = jnp.float32, jnp.bfloat16
-    scratch = [pltpu.VMEM((2 * block, QUARTER), bf16)] * 4
+    scratch = [pltpu.VMEM((FOLD, QUARTER, NB), bf16), pltpu.SemaphoreType.DMA((FOLD,))]
+    scratch += [pltpu.VMEM((2 * block, QUARTER), bf16)] * 4
     scratch += [pltpu.VMEM((block, 4 * CLASS), f32)] * 2 + [pltpu.VMEM((2, block, LANES), f32)]
     if relative:
         scratch = [pltpu.VMEM((SLICES, block, 2 * LANES), bf16)] + scratch
-        out_specs = [pl.BlockSpec((block, 2 * LANES), lambda i, p, *_: (i, 0))] * SLICES
+        out_specs = [pl.BlockSpec((block, 2 * LANES), lambda i, *_: (i, 0))] * SLICES
         out_shape = [jax.ShapeDtypeStruct((rows, 2 * LANES), bf16)] * SLICES
     else:
         extra = META if with_meta else 0
-        out_specs = [pl.BlockSpec((SLICES, block + extra, 2 * LANES), lambda i, p, *_: (0, i, 0))]
+        out_specs = [pl.BlockSpec((SLICES, block + extra, 2 * LANES), lambda i, *_: (0, i, 0))]
         out_shape = [jax.ShapeDtypeStruct((SLICES, rows + extra, 2 * LANES), bf16)]
     result = pl.pallas_call(
         functools.partial(spectra_kernel, relative, with_meta),
         grid_spec=pltpu.PrefetchScalarGridSpec(
             num_scalar_prefetch=1 if relative else 0,
-            grid=(rows // block, 4),
+            grid=(rows // block,),
             in_specs=in_specs,
             out_specs=out_specs,
             scratch_shapes=scratch,
@@ -202,7 +206,7 @@
             flops=14 * rows * NB * NB, bytes_accessed=rows * NT * 3 + 8 * NB * NB, transcendentals=rows * NB
         ),
         name="spectra",
-    )(*([here] if relative else []), traces, mask, owners, bins, jnp.asarray(forward_tables()))
+    )(*([here] if relative else []), traces, mask, owners, bins, jnp.asarray(forward_tables()).reshape(FOLD, QUARTER, NB))
     return result if relative else result[0]
 
 
@@ -393,16 +397,18 @@
 
     fixed = fixed_pairs(count)
     known = (0,) + SENT
-    before = len(known) - LATEST
-    soon = [(i, j) for j in range(1, before) for i in range(j)]
-    last = [(i, j) for j in range(before, len(known)) for i in range(j)]
+    stages = [
+        [(i, j) for j in range(start, end) for i in range(j)] for start, end in zip((1,) + STAGES, STAGES)
+    ]
     as_slots = lambda pairs: [(-known[i] - count, -known[j] - count) for i, j in pairs]
-    weights = pair_weights(here, first, early, total_segs, [fixed, as_slots(soon), as_slots(last)])
+    weights = pair_weights(here, first, early, total_segs, [fixed] + [as_slots(pairs) for pairs in stages])
     rows = count * BIN_DEV
     stacks = cross(first, fixed, early // G, rows, weights[0])
     held = [slots[slot] for slot in known]
-    stacks = cross(held[:before], soon, late // G, rows, weights[1], before=stacks)
-    return cross(held, last, late // G, rows, weights[2], before=stacks, copies=seg_count)
+    for end, pairs, weight in zip(STAGES, stages, weights[1:]):
+        copies = seg_count if end == len(known) else None
+        stacks = cross(held[:end], pairs, late // G, rows, weight, before=stacks, copies=copies)
+    return stacks
 
 
 def sent_at_once(x, mask, owners, bins, total_segs):

time: 128 us -> 129 us (level)
  blocking collectives: 15.7 us -> 18.2 us
  waiting for transfers between devices: 52.7 us -> 50.8 us
    all_to_all x1, blocking collectives: 15.7 us -> 18.2 us  [per_device(): lax.all_to_all(stacks, ('seg', 'chan'), split_axis=0, concat_axis=0, tile...]
    ppermute x7, waiting for transfers between devices: 52.7 us -> 50.8 us  [sent_along(): lax.ppermute(second[shift], 'chan', [(i, (i + shift) % count) for i in ra...]
    pallas_call x3 -> x4, Pallas kernels: 7.5 us -> 8.58 us  [cross(): pl.pallas_call(functools.partial(cross_kernel, split, pairs, steps, befor...]
  transfers between devices with their start and end apart: 8 -> 8, of which waited for: 4 -> 4; matrix products, arithmetic and copies ran while one was open for 0% -> 0% of each run, Pallas kernels for 21% -> 22%
where the time goes in v4:
time: 129 us
  waiting for transfers between devices  50.8 us (39%)
  Pallas kernels  41.1 us (32%)
  starting transfers between devices  18.6 us (14%)
  blocking collectives  18.2 us (14%)
    ppermute x7, waiting for transfers between devices, sent_along(): lax.ppermute(second[shift], 'chan', [(i, (i + shift) % count) for i in ra...  50.8 us
    pallas_call x2, Pallas kernels, spectra(): pl.pallas_call(functools.partial(spectra_kernel, relative, with_meta), gr...  31 us
    all_to_all x1, blocking collectives, per_device(): lax.all_to_all(stacks, ('seg', 'chan'), split_axis=0, concat_axis=0, tile...  18.2 us
    ppermute x7, starting transfers between devices, sent_along(): lax.ppermute(second[shift], 'chan', [(i, (i + shift) % count) for i in ra...  11.3 us
    pallas_call x4, Pallas kernels, cross(): pl.pallas_call(functools.partial(cross_kernel, split, pairs, steps, befor...  8.58 us
    all_to_all x1, starting transfers between devices, sent_along(): lax.all_to_all(first, 'chan', split_axis=0, concat_axis=0, tiled=True)  7.3 us
  transfers between devices with their start and end apart: 8, of which 4 were waited for; matrix products, arithmetic and copies ran while one was open for 0% of the time, Pallas kernels for 22%

profile of v4, /device:TPU:0, one launch (start us, length us, event | category | flops | bytes accessed | tf_op | source)
XLA Modules:
  0.0 128.8 jit_solution(9962596437393013965)
XLA Ops:
  0.0 9.3 %spectra.3 = bf16[8,272,256]{2,1,0:T(8,128)(2,1)} custom-call(bf16[1024,4096]{1,0:T(8,128)(2,1)} %bitcast.6, s32[1,128]{1,0:T(1,128)} %bitcast.8, s32[1,64]{1,0:T(1,128)} %bitcast.10, s32[1,64]{1,0:T(1,128)} %refs_3_.2, bf16[4,1024,1024]{2,1,0:T(8,128)(2,1)} %constant.30.refs_5_.refs_4_), custom_call_target="tpu_custom_call" | custom-call | flops 3758096384 | bytes 11534336 | tf_op jit(solution)/shard_map/spectra/pallas_call | solution.py:194
  9.3 7.3 %all-to-all-start = ((bf16[8,272,256]{2,1,0:T(8,128)(2,1)}), bf16[8,272,256]{2,1,0:T(8,128)(2,1)S(1)}, u32[]{:S(2)}, u32[]{:S(2)}) async-start(bf16[8,272,256]{2,1,0:T(8,128)(2,1)} %spectra.3), calls=%async_computation | async-start | bytes 2228224 | tf_op jit(solution)/shard_map/all_to_all | solution.py:392
  16.6 0.0 copy-start.5
  16.6 0.0 copy-start.7
  16.6 21.7 %spectra.2 = (bf16[768,256]{1,0:T(8,128)(2,1)}, bf16[768,256]{1,0:T(8,128)(2,1)}, bf16[768,256]{1,0:T(8,128)(2,1)}, bf16[768,256]{1,0:T(8,128)(2,1)}, bf16[768,2...) custom-call(s32[1]{0:T(128)} %bitcast.refs_0_.here_ref, ...), custom_call_target="tpu_custom_call" | custom-call | flops 11274289152 | bytes 17825792 | tf_op jit(solution)/shard_map/spectra/pallas_call | solution.py:194
  38.4 2.1 %collective-permute-start = (bf16[768,256]{1,0:T(8,128)(2,1)}, bf16[768,256]{1,0:T(8,128)(2,1)S(1)}, u32[]{:S(2)}, u32[]{:S(2)}) collective-permute-start(bf16[768,256]{1,0:T(8,128)(2,1)} %get-tuple-element.18), channel_id=1, source_target_pairs={{0,1},{1,2},{2,3},{3,4},{4,5},{5,6},{6,7},{7,0},{8,9},{9,10},{10,1... | collective-permute-start | bytes 1179656 | tf_op jit(solution)/shard_map/ppermute | solution.py:396
  40.5 2.8 %collective-permute-start.1 = (bf16[768,256]{1,0:T(8,128)(2,1)}, bf16[768,256]{1,0:T(8,128)(2,1)S(1)}, u32[]{:S(2)}, u32[]{:S(2)}) collective-permute-start(bf16[768,256]{1,0:T(8,128)(2,1)} %get-tuple-element.19), channel_id=1, source_target_pairs={{0,7},{1,0},{2,1},{3,2},{4,3},{5,4},{6,5},{7,6},{8,15},{9,8},{10,9... | collective-permute-start | bytes 1179656 | tf_op jit(solution)/shard_map/ppermute | solution.py:396
  43.2 1.1 collective-permute-start.2
  44.3 1.5 %collective-permute-start.3 = (bf16[768,256]{1,0:T(8,128)(2,1)}, bf16[768,256]{1,0:T(8,128)(2,1)S(1)}, u32[]{:S(2)}, u32[]{:S(2)}) collective-permute-start(bf16[768,256]{1,0:T(8,128)(2,1)} %get-tuple-element.21), channel_id=1, source_target_pairs={{0,3},{1,4},{2,5},{3,6},{4,7},{5,0},{6,1},{7,2},{8,11},{9,12},{10,... | collective-permute-start | bytes 1179656 | tf_op jit(solution)/shard_map/ppermute | solution.py:396
  45.8 2.4 %collective-permute-start.4 = (bf16[768,256]{1,0:T(8,128)(2,1)}, bf16[768,256]{1,0:T(8,128)(2,1)S(1)}, u32[]{:S(2)}, u32[]{:S(2)}) collective-permute-start(bf16[768,256]{1,0:T(8,128)(2,1)} %get-tuple-element.22), channel_id=1, source_target_pairs={{0,5},{1,6},{2,7},{3,0},{4,1},{5,2},{6,3},{7,4},{8,13},{9,14},{10,... | collective-permute-start | bytes 1179656 | tf_op jit(solution)/shard_map/ppermute | solution.py:396
  48.1 9.5 %collective-permute-done.refs_1_ = bf16[768,256]{1,0:T(8,128)(2,1)S(1)} collective-permute-done((bf16[768,256]{1,0:T(8,128)(2,1)}, bf16[768,256]{1,0:T(8,128)(2,1)S(1)}, u32[]{:S(2)}, u32[]{:S(2)}) %collective-permute-start) | collective-permute-done | bytes 393248 | tf_op jit(solution)/shard_map/ppermute | solution.py:396
  57.6 0.4 collective-permute-start.5
  58.0 9.6 %collective-permute-done.1.refs_2_ = bf16[768,256]{1,0:T(8,128)(2,1)S(1)} collective-permute-done((bf16[768,256]{1,0:T(8,128)(2,1)}, bf16[768,256]{1,0:T(8,128)(2,1)S(1)}, u32[]{:S(2)}, u32[]{:S(2)}) %collective-permute-start.1) | collective-permute-done | bytes 393248 | tf_op jit(solution)/shard_map/ppermute | solution.py:396
  67.5 1.2 collective-permute-start.6
  68.7 0.3 weights.1
  69.0 1.3 %cross.4.refs_7_ = f32[64,256]{1,0:T(8,128)S(1)} custom-call(bf16[8,272,256]{2,1,0:T(8,128)(2,1)S(1)} %all-to-all-done.meta_ref.refs_0_, f32[8,352]{1,0:T(8,128)S(1)} %get-tuple-element.28.refs_1_), custom_call_target="tpu_custom_call" | custom-call | flops 5767168 | bytes 2883584 | tf_op jit(solution)/shard_map/cross/pallas_call | solution.py:285
  70.4 26.4 %collective-permute-done.2.refs_3_ = bf16[768,256]{1,0:T(8,128)(2,1)S(1)} collective-permute-done((bf16[768,256]{1,0:T(8,128)(2,1)}, bf16[768,256]{1,0:T(8,128)(2,1)S(1)}, u32[]{:S(2)}, u32[]{:S(2)}) %collective-permute-start.2) | collective-permute-done | bytes 393248 | tf_op jit(solution)/shard_map/ppermute | solution.py:396
  96.8 2.4 %cross.5.refs_8_ = f32[64,256]{1,0:T(8,128)S(1)} custom-call(bf16[768,256]{1,0:T(8,128)(2,1)S(1)} %copy-done, bf16[768,256]{1,0:T(8,128)(2,1)S(1)} %collective-permute-done.refs_1_, bf16[768,256]{1,0:T(8,128)(2,1)S(1)} %collective-permute-done.1.refs_2_, bf16[768,256]{1,0:T(8,128)(2,1)S(1)} %collective-permute-done.2.refs_3_, ...), custom_call_target="tpu_custom_call" | custom-call | flops 11796480 | bytes 5898240 | tf_op jit(solution)/shard_map/cross/pallas_call | solution.py:285
  99.2 2.2 %cross.6.refs_9_ = f32[64,256]{1,0:T(8,128)S(1)} custom-call(bf16[768,256]{1,0:T(8,128)(2,1)S(1)} %copy-done, bf16[768,256]{1,0:T(8,128)(2,1)S(1)} %collective-permute-done.refs_1_, bf16[768,256]{1,0:T(8,128)(2,1)S(1)} %collective-permute-done.1.refs_2_, bf16[768,256]{1,0:T(8,128)(2,1)S(1)} %collective-permute-done.2.refs_3_, ...), custom_call_target="tpu_custom_call" | custom-call | flops 4718592 | bytes 2359296 | tf_op jit(solution)/shard_map/cross/pallas_call | solution.py:285
  101.4 0.0 copy-start.1
  101.5 5.4 %collective-permute-done.6.refs_7_ = bf16[768,256]{1,0:T(8,128)(2,1)} collective-permute-done((bf16[768,256]{1,0:T(8,128)(2,1)}, bf16[768,256]{1,0:T(8,128)(2,1)}, u32[]{:S(2)}, u32[]{:S(2)}) %collective-permute-start.6) | collective-permute-done | bytes 393248 | tf_op jit(solution)/shard_map/ppermute | solution.py:396
  106.9 2.6 %cross.7 = bf16[4,64,256]{2,1,0:T(8,128)(2,1)S(1)} custom-call(bf16[768,256]{1,0:T(8,128)(2,1)S(1)} %copy-done, bf16[768,256]{1,0:T(8,128)(2,1)S(1)} %collective-permute-done.refs_1_, bf16[768,256]{1,0:T(8,128)(2,1)S(1)} %collective-permute-done.1.refs_2_, bf16[768,256]{1,0:T(8,128)(2,1)S(1)} %collective-permute-done.2.refs_3_, ...), custom_call_target="tpu_custom_call" | custom-call | flops 5505024 | bytes 2752512 | tf_op jit(solution)/shard_map/cross/pallas_call | solution.py:285
  109.5 18.2 %all_to_all.10.stacks_ref = bf16[32,8,256]{2,1,0:T(8,128)(2,1)S(1)} all-to-all(bf16[32,8,256]{2,1,0:T(8,128)(2,1)S(1)} %bitcast.5), channel_id=1, replica_groups=mesh['seg'=4,'chan'=8] {'seg','chan'}, dimensions={0} | all-to-all | bytes 262144 | tf_op jit(solution)/shard_map/all_to_all | solution.py:447
  127.7 1.2 lags.1
  (17 shorter events, 0.0 us)
Async XLA Ops:
  9.3 59.4 %all-to-all-start = ((bf16[8,272,256]{2,1,0:T(8,128)(2,1)}), bf16[8,272,256]{2,1,0:T(8,128)(2,1)S(1)}, u32[]{:S(2)}, u32[]{:S(2)}) async-start(bf16[8,272,256]{2,1,0:T(8,128)(2,1)} %spectra.3), calls=%async_computation | async-start | bytes 2228224 | tf_op jit(solution)/shard_map/all_to_all | solution.py:392
  16.6 52.1 %copy-start.4 = (s32[2,352]{1,0:T(2,128)S(1)}, s32[2,352]{1,0:T(2,128)}, u32[]{:S(2)}) copy-start(s32[2,352]{1,0:T(2,128)} %constant.21.clone.refs_0_) | copy-start | bytes 8452
  16.6 52.1 %copy-start.5 = (s32[2,240]{1,0:T(2,128)S(1)}, s32[2,240]{1,0:T(2,128)}, u32[]{:S(2)}) copy-start(s32[2,240]{1,0:T(2,128)} %constant.22.clone.refs_1_) | copy-start | bytes 5764
  16.6 52.1 %copy-start.6 = (s32[2,112]{1,0:T(2,128)S(1)}, s32[2,112]{1,0:T(2,128)}, u32[]{:S(2)}) copy-start(s32[2,112]{1,0:T(2,128)} %constant.24.clone.refs_3_) | copy-start | bytes 2692
  16.6 52.1 %copy-start.7 = (s32[2,96]{1,0:T(2,128)S(1)}, s32[2,96]{1,0:T(2,128)}, u32[]{:S(2)}) copy-start(s32[2,96]{1,0:T(2,128)} %constant.23.clone.refs_2_) | copy-start | bytes 2308
  38.4 58.4 %copy-start = (bf16[768,256]{1,0:T(8,128)(2,1)S(1)}, bf16[768,256]{1,0:T(8,128)(2,1)}, u32[]{:S(2)}) copy-start(bf16[768,256]{1,0:T(8,128)(2,1)} %get-tuple-element.17.refs_0_) | copy-start | bytes 1179652
  38.4 19.2 %collective-permute-start = (bf16[768,256]{1,0:T(8,128)(2,1)}, bf16[768,256]{1,0:T(8,128)(2,1)S(1)}, u32[]{:S(2)}, u32[]{:S(2)}) collective-permute-start(bf16[768,256]{1,0:T(8,128)(2,1)} %get-tuple-element.18), channel_id=1, source_target_pairs={{0,1},{1,2},{2,3},{3,4},{4,5},{5,6},{6,7},{7,0},{8,9},{9,10},{10,1... | collective-permute-start | bytes 1179656 | tf_op jit(solution)/shard_map/ppermute | solution.py:396
  40.5 27.1 %collective-permute-start.1 = (bf16[768,256]{1,0:T(8,128)(2,1)}, bf16[768,256]{1,0:T(8,128)(2,1)S(1)}, u32[]{:S(2)}, u32[]{:S(2)}) collective-permute-start(bf16[768,256]{1,0:T(8,128)(2,1)} %get-tuple-element.19), channel_id=1, source_target_pairs={{0,7},{1,0},{2,1},{3,2},{4,3},{5,4},{6,5},{7,6},{8,15},{9,8},{10,9... | collective-permute-start | bytes 1179656 | tf_op jit(solution)/shard_map/ppermute | solution.py:396
  43.2 53.5 %collective-permute-start.2 = (bf16[768,256]{1,0:T(8,128)(2,1)}, bf16[768,256]{1,0:T(8,128)(2,1)S(1)}, u32[]{:S(2)}, u32[]{:S(2)}) collective-permute-start(bf16[768,256]{1,0:T(8,128)(2,1)} %get-tuple-element.20), channel_id=1, source_target_pairs={{0,4},{1,5},{2,6},{3,7},{4,0},{5,1},{6,2},{7,3},{8,12},{9,13},{10,... | collective-permute-start | bytes 1179656 | tf_op jit(solution)/shard_map/ppermute | solution.py:396
  44.3 52.5 %collective-permute-start.3 = (bf16[768,256]{1,0:T(8,128)(2,1)}, bf16[768,256]{1,0:T(8,128)(2,1)S(1)}, u32[]{:S(2)}, u32[]{:S(2)}) collective-permute-start(bf16[768,256]{1,0:T(8,128)(2,1)} %get-tuple-element.21), channel_id=1, source_target_pairs={{0,3},{1,4},{2,5},{3,6},{4,7},{5,0},{6,1},{7,2},{8,11},{9,12},{10,... | collective-permute-start | bytes 1179656 | tf_op jit(solution)/shard_map/ppermute | solution.py:396
  45.8 51.0 %collective-permute-start.4 = (bf16[768,256]{1,0:T(8,128)(2,1)}, bf16[768,256]{1,0:T(8,128)(2,1)S(1)}, u32[]{:S(2)}, u32[]{:S(2)}) collective-permute-start(bf16[768,256]{1,0:T(8,128)(2,1)} %get-tuple-element.22), channel_id=1, source_target_pairs={{0,5},{1,6},{2,7},{3,0},{4,1},{5,2},{6,3},{7,4},{8,13},{9,14},{10,... | collective-permute-start | bytes 1179656 | tf_op jit(solution)/shard_map/ppermute | solution.py:396
  57.6 41.6 %collective-permute-start.5 = (bf16[768,256]{1,0:T(8,128)(2,1)}, bf16[768,256]{1,0:T(8,128)(2,1)}, u32[]{:S(2)}, u32[]{:S(2)}) collective-permute-start(bf16[768,256]{1,0:T(8,128)(2,1)} %get-tuple-element.23), channel_id=1, source_target_pairs={{0,2},{1,3},{2,4},{3,5},{4,6},{5,7},{6,0},{7,1},{8,10},{9,11},{10,... | collective-permute-start | bytes 1179656 | tf_op jit(solution)/shard_map/ppermute | solution.py:396
  67.5 39.4 %collective-permute-start.6 = (bf16[768,256]{1,0:T(8,128)(2,1)}, bf16[768,256]{1,0:T(8,128)(2,1)}, u32[]{:S(2)}, u32[]{:S(2)}) collective-permute-start(bf16[768,256]{1,0:T(8,128)(2,1)} %get-tuple-element.24), channel_id=1, source_target_pairs={{0,6},{1,7},{2,0},{3,1},{4,2},{5,3},{6,4},{7,5},{8,14},{9,15},{10,... | collective-permute-start | bytes 1179656 | tf_op jit(solution)/shard_map/ppermute | solution.py:396
  101.4 26.2 %copy-start.1 = (bf16[1024,1024]{1,0:T(8,128)(2,1)S(1)}, bf16[1024,1024]{1,0:T(8,128)(2,1)}, u32[]{:S(2)}) copy-start(bf16[1024,1024]{1,0:T(8,128)(2,1)} %constant.27.clone.odd_ref) | copy-start | bytes 6291460
  101.5 26.2 %copy-start.2 = (bf16[512,512]{1,0:T(8,128)(2,1)S(1)}, bf16[512,512]{1,0:T(8,128)(2,1)}, u32[]{:S(2)}) copy-start(bf16[512,512]{1,0:T(8,128)(2,1)} %constant.26.clone.two_ref) | copy-start | bytes 1572868
  101.5 26.2 %copy-start.3 = (bf16[512,512]{1,0:T(8,128)(2,1)S(1)}, bf16[512,512]{1,0:T(8,128)(2,1)}, u32[]{:S(2)}) copy-start(bf16[512,512]{1,0:T(8,128)(2,1)} %constant.25.clone.zero_ref) | copy-start | bytes 1572868

commit v5 on v4

--- a/solution.py
+++ b/solution.py
@@ -24,8 +24,7 @@
 LANES = 128
 SLICES = NB // LANES
 FOLD = 4
-CLASS = NB // FOLD
-QUARTER = NT // FOLD
+PART = LANES // FOLD
 LAGQ = NLAG // FOLD
 VMEM = 58 * 1024 * 1024
 VMEM_SMALL = 20 * 1024 * 1024
@@ -33,51 +32,39 @@
 META = 16
 
 SENT = (1, 7, 4, 3, 5, 2, 6)
-STAGES = (6, 7, 8)
-
-
-ORDER = np.arange(NB).reshape(CLASS, FOLD).T.reshape(-1)
-
-
-def forward_tables():
-    samples = np.arange(NT // 2, dtype=np.int64)
+STAGES = (6, 8)
+
+WITHIN = np.arange(LANES).reshape(PART, FOLD).T.reshape(-1)
+ORDER = (np.arange(SLICES)[:, None] * LANES + WITHIN[None, :]).reshape(-1)
+
+
+def forward_table():
+    samples = np.arange(NT, dtype=np.int64)
     freqs = K0 + ORDER.astype(np.int64)
     phase = samples[:, None] * freqs[None, :] % NT
-    angle = (phase.astype(np.float32) * np.float32(2.0 * math.pi / NT)).astype(np.float64)
-    cos = np.cos(angle).astype(np.float32).astype(ml_dtypes.bfloat16)
-    sin = (-np.sin(angle)).astype(np.float32).astype(ml_dtypes.bfloat16)
-
-    def part(which, rows):
-        columns = slice(which * CLASS, (which + 1) * CLASS)
-        return [cos[rows, columns], sin[rows, columns]]
-
-    low, high = slice(0, QUARTER), slice(QUARTER, 2 * QUARTER)
-    band = (np.abs(ORDER[:, None] - ORDER[None, :]) <= HW).astype(ml_dtypes.bfloat16)
-    table = np.concatenate(
-        [
-            np.concatenate(part(0, low) + part(2, low), axis=1),
-            np.concatenate(part(1, low) + part(3, low), axis=1),
-            np.concatenate(part(1, high) + part(3, high), axis=1),
-            band,
-        ],
-        axis=0,
-    )
-    return table
+    angle = np.arange(NT).astype(np.float32) * np.float32(2.0 * math.pi / NT)
+    cos = np.cos(angle.astype(np.float64)).astype(np.float32).astype(ml_dtypes.bfloat16)
+    sin = (-np.sin(angle.astype(np.float64))).astype(np.float32).astype(ml_dtypes.bfloat16)
+    both = [table[phase].reshape(NT, SLICES, 1, LANES) for table in (cos, sin)]
+    return np.concatenate(both, axis=2).reshape(NT, SLICES, 2 * LANES).transpose(1, 0, 2)
+
+
+def band_table():
+    around = (np.arange(3)[:, None] * LANES + WITHIN[None, :]).reshape(-1)
+    return (np.abs(around[:, None] - (LANES + WITHIN)[None, :]) <= HW).astype(ml_dtypes.bfloat16)
 
 
 def inverse_tables():
     freqs = K0 + ORDER.astype(np.int64)
     delays = (np.arange(2 * LAGQ, dtype=np.int64) - NLAG // 2) * DEC
     phase = np.mod(freqs[:, None] * delays[None, :], NT)
-    angle = phase.astype(np.float64) * (2.0 * math.pi / NT)
+    angle = np.arange(NT).astype(np.float64) * (2.0 * math.pi / NT)
     scale = 1.0 / math.sqrt(NB)
-    real = (np.cos(angle) * scale).reshape(SLICES, 1, LANES, 2 * LAGQ)
-    imag = (-np.sin(angle) * scale).reshape(SLICES, 1, LANES, 2 * LAGQ)
-    rows = np.concatenate([real, imag], axis=1).reshape(FOLD, 2 * CLASS, 2 * LAGQ)
-    zero = rows[0][:, :LAGQ]
-    two = rows[2][:, :LAGQ]
-    odd = np.concatenate([rows[1], rows[3]], axis=0)
-    return [table.astype(np.float32).astype(ml_dtypes.bfloat16) for table in (zero, two, odd)]
+    real = (np.cos(angle) * scale).astype(np.float32).astype(ml_dtypes.bfloat16)[phase]
+    imag = (-np.sin(angle) * scale).astype(np.float32).astype(ml_dtypes.bfloat16)[phase]
+    parts = [table.reshape(SLICES, FOLD, PART, 2 * LAGQ).transpose(1, 0, 2, 3) for table in (real, imag)]
+    rows = np.stack(parts, axis=1).reshape(FOLD, 2 * SLICES * PART, 2 * LAGQ)
+    return rows[0][:, :LAGQ], rows[2][:, :LAGQ], np.concatenate([rows[1], rows[3]], axis=0)
 
 
 def two_terms(values):
@@ -86,75 +73,78 @@
     return high, low
 
 
-def two_term_dot(values_ref, table):
-    rows = values_ref.shape[0] // 2
-    both = jnp.dot(values_ref[...], table, preferred_element_type=jnp.float32)
-    return both[:rows] + both[rows:]
-
-
-def spectra_kernel(relative, with_meta, *refs):
+def spectra_kernel(relative, with_meta, skip, *refs):
     f32, bf16 = jnp.float32, jnp.bfloat16
     refs = list(refs)
     here_ref = refs.pop(0) if relative else None
-    x_ref, mask_ref, owner_ref, bins_ref, source_ref = refs[:5]
-    out_refs = refs[5:-9]
-    table_ref, arrived, u, v, a, b, early, others, hold = refs[-9:]
-    target = refs[-10] if relative else out_refs[0]
-    first = pl.program_id(0) == 0
-    rows = x_ref.shape[0]
-    copies = [
-        pltpu.make_async_copy(source_ref.at[part], table_ref.at[part], arrived.at[part]) for part in range(FOLD)
+    x_any, mask_ref, owner_ref, bins_ref, table_any, band_ref = refs[:6]
+    x_ref, table_ref, x_came, table_came, spectrum, power, hold = refs[-7:]
+    out_refs = refs[6:-8] if relative else refs[6:-7]
+    target = refs[-8] if relative else out_refs[0]
+    step, steps = pl.program_id(0), pl.num_programs(0)
+    first = step == 0
+    rows = x_ref.shape[1]
+    slot = lax.rem(step, 2)
+
+    def trace_copy(block, slot):
+        at = pl.ds(pl.multiple_of((block + skip) * rows, rows), rows)
+        return pltpu.make_async_copy(x_any.at[at], x_ref.at[slot], x_came.at[slot])
+
+    table_copies = [
+        pltpu.make_async_copy(table_any.at[piece], table_ref.at[piece], table_came.at[piece])
+        for piece in range(SLICES)
     ]
 
     @pl.when(first)
     def start():
-        for copy in copies:
+        trace_copy(0, 0).start()
+        for copy in table_copies:
             copy.start()
 
-    x = [x_ref[:, m * QUARTER:(m + 1) * QUARTER].astype(f32) for m in range(FOLD)]
-    even, odd = x[0] + x[2], x[1] + x[3]
-    u[:rows], u[rows:] = two_terms(even + odd)
-    v[:rows], v[rows:] = two_terms(even - odd)
-    a[:rows], a[rows:] = two_terms(x[0] - x[2])
-    b[:rows], b[rows:] = two_terms(x[1] - x[3])
-
-    pl.when(first)(copies[0].wait)
-    early[:, :2 * CLASS] = two_term_dot(u, table_ref[0, :, :2 * CLASS])
-    early[:, 2 * CLASS:] = two_term_dot(v, table_ref[0, :, 2 * CLASS:])
-    pl.when(first)(copies[1].wait)
-    others[...] = two_term_dot(a, table_ref[1])
-    pl.when(first)(copies[2].wait)
-    others[...] += two_term_dot(b, table_ref[2])
-    pl.when(first)(copies[3].wait)
-
-    holders = [(early, 0), (others, 0), (early, 2 * CLASS), (others, 2 * CLASS)]
-    power = []
-    for ref, start in holders:
-        real, imag = ref[:, start:start + CLASS], ref[:, start + CLASS:start + 2 * CLASS]
-        power.append((real * real + imag * imag).astype(bf16))
-    power = jnp.concatenate(power, axis=1)
-    lane = lax.broadcasted_iota(jnp.int32, (1, NB), 1)
-    bin_ = (lane % CLASS) * FOLD + lane // CLASS
-    within = jnp.minimum(bin_ + HW, NB - 1) - jnp.maximum(bin_ - HW, 0) + 1
-    mean = jnp.dot(power, table_ref[3], preferred_element_type=f32) * (1.0 / within.astype(f32))
     shape = (LANES, LANES)
     diagonal = lax.broadcasted_iota(jnp.int32, shape, 0) == lax.broadcasted_iota(jnp.int32, shape, 1)
     mask = jnp.where(diagonal, jnp.broadcast_to(mask_ref[...], shape), 0).astype(f32)
-    mask = jnp.sum(mask, axis=1, keepdims=True)
-    weight = jnp.concatenate([mask] * (rows // LANES), axis=0) * lax.rsqrt(mean + EPSILON)
+    mask = jnp.concatenate([jnp.sum(mask, axis=1, keepdims=True)] * (rows // LANES), axis=0)
+    lane = lax.broadcasted_iota(jnp.int32, (1, LANES), 1)
+    place = (lane % PART) * FOLD + lane // PART
     per_group = LANES // G
-    for piece in range(SLICES):
-        ref, start = holders[piece // 2]
-        start += (piece % 2) * LANES
-        scale = weight[:, piece * LANES:(piece + 1) * LANES]
-        hold[0] = ref[:, start:start + LANES] * scale
-        hold[1] = ref[:, CLASS + start:CLASS + start + LANES] * scale
+
+    trace_copy(step, slot).wait()
+
+    @pl.when(step + 1 < steps)
+    def ahead():
+        trace_copy(step + 1, 1 - slot).start()
+
+    def whiten(piece):
+        low, high = max(piece - 1, 0), min(piece + 2, SLICES)
+        start = (low - piece + 1) * LANES
+        sums = jnp.dot(
+            power[:, low * LANES:high * LANES],
+            band_ref[start:start + (high - low) * LANES],
+            preferred_element_type=f32,
+        )
+        bin_ = place + piece * LANES
+        within = jnp.minimum(bin_ + HW, NB - 1) - jnp.maximum(bin_ - HW, 0) + 1
+        weight = mask * lax.rsqrt(sums * (1.0 / within.astype(f32)) + EPSILON)
+        hold[piece % 2, 0] = spectrum[piece, :, :LANES] * weight
+        hold[piece % 2, 1] = spectrum[piece, :, LANES:] * weight
         for seg in range(rows // LANES):
             for j in range(per_group):
                 at = seg * LANES + j * G
                 for half in range(2):
-                    taken = hold[half, pl.ds(seg * LANES + j, G, stride=per_group), :]
+                    taken = hold[piece % 2, half, pl.ds(seg * LANES + j, G, stride=per_group), :]
                     target[piece, at:at + G, half * LANES:(half + 1) * LANES] = taken.astype(bf16)
+
+    for piece in range(SLICES):
+        pl.when(first)(table_copies[piece].wait)
+        both = jnp.dot(x_ref[slot], table_ref[piece], preferred_element_type=f32)
+        real, imag = both[:, :LANES], both[:, LANES:]
+        spectrum[piece] = both
+        power[:, piece * LANES:(piece + 1) * LANES] = (real * real + imag * imag).astype(bf16)
+        if piece:
+            whiten(piece - 1)
+    whiten(SLICES - 1)
+
     if with_meta:
         tiles = owner_ref.shape[1]
         labels = (owner_ref[...] * BIN_DEV + bins_ref[...]).astype(f32)
@@ -164,25 +154,25 @@
             target[piece, at, :LANES] = jnp.broadcast_to(mask_ref[...].astype(f32), (META, LANES)).astype(bf16)
             target[piece, at, LANES:LANES + tiles] = jnp.broadcast_to(labels, (META, tiles)).astype(bf16)
     if relative:
-        for slot in range(SLICES):
-            out_refs[slot][...] = target[lax.rem(here_ref[0] + slot, SLICES)]
-
-
-def spectra(traces, mask, owners, bins, first_row, rows, here=None, with_meta=False):
-    block, relative = BLOCK, here is not None
-    skip = first_row // block
-    whole = lambda shape: pl.BlockSpec(shape, lambda i, *_: (0, 0))
-    in_specs = [
-        pl.BlockSpec((block, NT), lambda i, *_: (i + skip, 0)),
-        whole(mask.shape),
-        whole(owners.shape),
-        whole(bins.shape),
-        pl.BlockSpec(memory_space=pl.ANY),
+        for other in range(SLICES):
+            out_refs[other][...] = target[lax.rem(here_ref[0] + other, SLICES)]
+
+
+def spectra(traces, mask, owners, bins, first_row, rows, block, here=None, with_meta=False):
+    relative = here is not None
+    table, band = jnp.asarray(forward_table()), jnp.asarray(band_table())
+    whole = lambda array: pl.BlockSpec(array.shape, lambda i, *_: (0, 0))
+    in_place = pl.BlockSpec(memory_space=pl.ANY)
+    f32, bf16 = jnp.float32, jnp.bfloat16
+    scratch = [
+        pltpu.VMEM((2, block, NT), bf16),
+        pltpu.VMEM(table.shape, bf16),
+        pltpu.SemaphoreType.DMA((2,)),
+        pltpu.SemaphoreType.DMA((SLICES,)),
+        pltpu.VMEM((SLICES, block, 2 * LANES), f32),
+        pltpu.VMEM((block, NB), bf16),
+        pltpu.VMEM((2, 2, block, LANES), f32),
     ]
-    f32, bf16 = jnp.float32, jnp.bfloat16
-    scratch = [pltpu.VMEM((FOLD, QUARTER, NB), bf16), pltpu.SemaphoreType.DMA((FOLD,))]
-    scratch += [pltpu.VMEM((2 * block, QUARTER), bf16)] * 4
-    scratch += [pltpu.VMEM((block, 4 * CLASS), f32)] * 2 + [pltpu.VMEM((2, block, LANES), f32)]
     if relative:
         scratch = [pltpu.VMEM((SLICES, block, 2 * LANES), bf16)] + scratch
         out_specs = [pl.BlockSpec((block, 2 * LANES), lambda i, *_: (i, 0))] * SLICES
@@ -192,21 +182,21 @@
         out_specs = [pl.BlockSpec((SLICES, block + extra, 2 * LANES), lambda i, *_: (0, i, 0))]
         out_shape = [jax.ShapeDtypeStruct((SLICES, rows + extra, 2 * LANES), bf16)]
     result = pl.pallas_call(
-        functools.partial(spectra_kernel, relative, with_meta),
+        functools.partial(spectra_kernel, relative, with_meta, first_row // block),
         grid_spec=pltpu.PrefetchScalarGridSpec(
             num_scalar_prefetch=1 if relative else 0,
             grid=(rows // block,),
-            in_specs=in_specs,
+            in_specs=[in_place, whole(mask), whole(owners), whole(bins), in_place, whole(band)],
             out_specs=out_specs,
             scratch_shapes=scratch,
         ),
         out_shape=out_shape,
         compiler_params=pltpu.CompilerParams(vmem_limit_bytes=VMEM),
         cost_estimate=pl.CostEstimate(
-            flops=14 * rows * NB * NB, bytes_accessed=rows * NT * 3 + 8 * NB * NB, transcendentals=rows * NB
+            flops=4 * rows * NT * NB, bytes_accessed=rows * NT * 3 + 4 * NT * NB, transcendentals=rows * NB
         ),
         name="spectra",
-    )(*([here] if relative else []), traces, mask, owners, bins, jnp.asarray(forward_tables()).reshape(FOLD, QUARTER, NB))
+    )(*([here] if relative else []), traces, mask, owners, bins, table, band)
     return result if relative else result[0]
 
 
@@ -358,9 +348,14 @@
         both = jnp.dot(jnp.concatenate(two_terms(values), axis=0), table, preferred_element_type=f32)
         return both[:BIN_DEV] + both[BIN_DEV:]
 
-    zero = product(jnp.concatenate(pieces[0:2], axis=1), zero_ref[...])
-    two = product(jnp.concatenate(pieces[4:6], axis=1), two_ref[...])
-    odd = product(jnp.concatenate(pieces[2:4] + pieces[6:8], axis=1), odd_ref[...])
+    def of_class(which):
+        at = which * PART
+        parts = [piece[:, at + half:at + half + PART] for half in (0, LANES) for piece in pieces]
+        return jnp.concatenate(parts, axis=1)
+
+    zero = product(of_class(0), zero_ref[...])
+    two = product(of_class(2), two_ref[...])
+    odd = product(jnp.concatenate([of_class(1), of_class(3)], axis=1), odd_ref[...])
     plus, minus = zero + two, zero - two
     out_ref[:, :LAGQ] = plus + odd[:, :LAGQ]
     out_ref[:, LAGQ:2 * LAGQ] = minus + odd[:, LAGQ:]
@@ -388,9 +383,9 @@
     early = BLOCK
     late = x.shape[0] - early
     here = lax.axis_index("chan").astype(jnp.int32).reshape(1)
-    first = spectra(x, mask, owners, bins, 0, early, with_meta=True)
+    first = spectra(x, mask, owners, bins, 0, early, BLOCK, with_meta=True)
     first = lax.all_to_all(first, "chan", split_axis=0, concat_axis=0, tiled=True)
-    second = spectra(x, mask, owners, bins, early, late, here=here)
+    second = spectra(x, mask, owners, bins, early, late, BLOCK, here=here)
     slots = {0: second[0]}
     for shift in SENT:
         slots[shift] = lax.ppermute(second[shift], "chan", [(i, (i + shift) % count) for i in range(count)])
@@ -424,7 +419,7 @@
     every = jnp.broadcast_to(every[:, None, :], (count, META, 2 * LANES))
     fixed = fixed_pairs(count)
     weights = pair_weights(here, every, 0, total_segs, [fixed])
-    outgoing = spectra(x, mask, owners, bins, 0, rows)
+    outgoing = spectra(x, mask, owners, bins, 0, rows, BLOCK)
     outgoing = outgoing.reshape(SLICES, rows, 2, splits, narrow).transpose(0, 3, 1, 2, 4)
     outgoing = outgoing.reshape(count, rows, 2 * narrow)
     wide = lax.all_to_all(outgoing, "chan", split_axis=0, concat_axis=0, tiled=True)

time: 129 us -> 158 us (1.22)
  Pallas kernels: 41.1 us -> 70.2 us
  blocking collectives: 18.2 us -> 15.7 us
  waiting for transfers between devices: 50.8 us -> 52.6 us
    pallas_call x2, Pallas kernels: 31 us -> 61.2 us  [spectra(): pl.pallas_call(functools.partial(spectra_kernel, relative, with_meta, fir...]
    all_to_all x1, blocking collectives: 18.2 us -> 15.7 us  [per_device(): lax.all_to_all(stacks, ('seg', 'chan'), split_axis=0, concat_axis=0, tile...]
    ppermute x7, waiting for transfers between devices: 50.8 us -> 52.5 us  [sent_along(): lax.ppermute(second[shift], 'chan', [(i, (i + shift) % count) for i in ra...]
    pallas_call x4 -> x3, Pallas kernels: 8.58 us -> 7.5 us  [cross(): pl.pallas_call(functools.partial(cross_kernel, split, pairs, steps, befor...]
  transfers between devices with their start and end apart: 8 -> 8, of which waited for: 4 -> 4; matrix products, arithmetic and copies ran while one was open for 0% -> 0% of each run, Pallas kernels for 22% -> 29%
where the time goes in v5:
time: 158 us
  Pallas kernels  70.2 us (44%)
  waiting for transfers between devices  52.6 us (33%)
  starting transfers between devices  19.1 us (12%)
  blocking collectives  15.7 us (10%)
    pallas_call x2, Pallas kernels, spectra(): pl.pallas_call(functools.partial(spectra_kernel, relative, with_meta, fir...  61.2 us
    ppermute x7, waiting for transfers between devices, sent_along(): lax.ppermute(second[shift], 'chan', [(i, (i + shift) % count) for i in ra...  52.5 us
    all_to_all x1, blocking collectives, per_device(): lax.all_to_all(stacks, ('seg', 'chan'), split_axis=0, concat_axis=0, tile...  15.7 us
    ppermute x7, starting transfers between devices, sent_along(): lax.ppermute(second[shift], 'chan', [(i, (i + shift) % count) for i in ra...  11.8 us
    pallas_call x3, Pallas kernels, cross(): pl.pallas_call(functools.partial(cross_kernel, split, pairs, steps, befor...  7.5 us
    all_to_all x1, starting transfers between devices, sent_along(): lax.all_to_all(first, 'chan', split_axis=0, concat_axis=0, tiled=True)  7.29 us
  transfers between devices with their start and end apart: 8, of which 4 were waited for; matrix products, arithmetic and copies ran while one was open for 0% of the time, Pallas kernels for 29%

profile of v5, /device:TPU:0, one launch (start us, length us, event | category | flops | bytes accessed | tf_op | source)
XLA Modules:
  0.0 157.7 jit_solution(18069215816509991369)
XLA Ops:
  0.0 19.2 %spectra.3 = bf16[8,272,256]{2,1,0:T(8,128)(2,1)} custom-call(bf16[1024,4096]{1,0:T(8,128)(2,1)} %bitcast.6, s32[1,128]{1,0:T(1,128)} %bitcast.8, s32[1,64]{1,0:T(1,128)} %bitcast.10, s32[1,64]{1,0:T(1,128)} %refs_3_.1, bf16[8,4096,256]{2,1,0:T(8,128)(2,1)} %constant.20.clone.refs_5_.refs_4_, bf16[384,128]{1,0:T(8,128)(2,1)} %constant.21.clone.refs_6_.refs_5_), custom_call_target="tpu_custom_call" | custom-call | flops 4294967296 | bytes 19922944 | tf_op jit(solution)/shard_map/spectra/pallas_call | solution.py:184
  19.2 7.3 %all-to-all-start = ((bf16[8,272,256]{2,1,0:T(8,128)(2,1)}), bf16[8,272,256]{2,1,0:T(8,128)(2,1)S(1)}, u32[]{:S(2)}, u32[]{:S(2)}) async-start(bf16[8,272,256]{2,1,0:T(8,128)(2,1)} %spectra.3), calls=%async_computation | async-start | bytes 2228224 | tf_op jit(solution)/shard_map/all_to_all | solution.py:387
  26.5 0.0 copy-start.5
  26.5 0.0 copy-start.6
  26.5 42.0 %spectra.2 = (bf16[768,256]{1,0:T(8,128)(2,1)}, bf16[768,256]{1,0:T(8,128)(2,1)}, bf16[768,256]{1,0:T(8,128)(2,1)}, bf16[768,256]{1,0:T(8,128)(2,1)}, bf16[768,2...) custom-call(s32[1]{0:T(128)} %bitcast.refs_0_.here_ref, ...), custom_call_target="tpu_custom_call" | custom-call | flops 12884901888 | bytes 26214400 | tf_op jit(solution)/shard_map/spectra/pallas_call | solution.py:184
  68.5 2.1 %collective-permute-start = (bf16[768,256]{1,0:T(8,128)(2,1)}, bf16[768,256]{1,0:T(8,128)(2,1)S(1)}, u32[]{:S(2)}, u32[]{:S(2)}) collective-permute-start(bf16[768,256]{1,0:T(8,128)(2,1)} %get-tuple-element.17), channel_id=1, source_target_pairs={{0,1},{1,2},{2,3},{3,4},{4,5},{5,6},{6,7},{7,0},{8,9},{9,10},{10,1... | collective-permute-start | bytes 1179656 | tf_op jit(solution)/shard_map/ppermute | solution.py:391
  70.6 2.8 %collective-permute-start.1 = (bf16[768,256]{1,0:T(8,128)(2,1)}, bf16[768,256]{1,0:T(8,128)(2,1)S(1)}, u32[]{:S(2)}, u32[]{:S(2)}) collective-permute-start(bf16[768,256]{1,0:T(8,128)(2,1)} %get-tuple-element.18), channel_id=1, source_target_pairs={{0,7},{1,0},{2,1},{3,2},{4,3},{5,4},{6,5},{7,6},{8,15},{9,8},{10,9... | collective-permute-start | bytes 1179656 | tf_op jit(solution)/shard_map/ppermute | solution.py:391
  73.4 1.1 collective-permute-start.2
  74.4 1.5 collective-permute-start.3
  75.9 2.4 %collective-permute-start.4 = (bf16[768,256]{1,0:T(8,128)(2,1)}, bf16[768,256]{1,0:T(8,128)(2,1)S(1)}, u32[]{:S(2)}, u32[]{:S(2)}) collective-permute-start(bf16[768,256]{1,0:T(8,128)(2,1)} %get-tuple-element.21), channel_id=1, source_target_pairs={{0,5},{1,6},{2,7},{3,0},{4,1},{5,2},{6,3},{7,4},{8,13},{9,14},{10,... | collective-permute-start | bytes 1179656 | tf_op jit(solution)/shard_map/ppermute | solution.py:391
  78.3 8.9 %collective-permute-done.refs_1_ = bf16[768,256]{1,0:T(8,128)(2,1)S(1)} collective-permute-done((bf16[768,256]{1,0:T(8,128)(2,1)}, bf16[768,256]{1,0:T(8,128)(2,1)S(1)}, u32[]{:S(2)}, u32[]{:S(2)}) %collective-permute-start) | collective-permute-done | bytes 393248 | tf_op jit(solution)/shard_map/ppermute | solution.py:391
  87.2 1.0 collective-permute-start.5
  88.1 9.6 %collective-permute-done.1.refs_2_ = bf16[768,256]{1,0:T(8,128)(2,1)S(1)} collective-permute-done((bf16[768,256]{1,0:T(8,128)(2,1)}, bf16[768,256]{1,0:T(8,128)(2,1)S(1)}, u32[]{:S(2)}, u32[]{:S(2)}) %collective-permute-start.1) | collective-permute-done | bytes 393248 | tf_op jit(solution)/shard_map/ppermute | solution.py:391
  97.7 1.2 collective-permute-start.6
  98.9 0.3 weights.1
  99.1 1.3 cross.3.refs_7_
  100.5 26.4 %collective-permute-done.2.refs_3_ = bf16[768,256]{1,0:T(8,128)(2,1)S(1)} collective-permute-done((bf16[768,256]{1,0:T(8,128)(2,1)}, bf16[768,256]{1,0:T(8,128)(2,1)S(1)}, u32[]{:S(2)}, u32[]{:S(2)}) %collective-permute-start.2) | collective-permute-done | bytes 393248 | tf_op jit(solution)/shard_map/ppermute | solution.py:391
  126.9 2.4 %cross.4.refs_9_ = f32[64,256]{1,0:T(8,128)S(1)} custom-call(bf16[768,256]{1,0:T(8,128)(2,1)S(1)} %copy-done.1, bf16[768,256]{1,0:T(8,128)(2,1)S(1)} %collective-permute-done.refs_1_, bf16[768,256]{1,0:T(8,128)(2,1)S(1)} %collective-permute-done.1.refs_2_, bf16[768,256]{1,0:T(8,128)(2,1)S(1)} %collective-permute-done.2.refs_3_, ...), custom_call_target="tpu_custom_call" | custom-call | flops 11796480 | bytes 5898240 | tf_op jit(solution)/shard_map/cross/pallas_call | solution.py:275
  129.3 0.0 copy-start.2
  129.3 0.0 copy-start.3
  129.4 7.7 %collective-permute-done.6.refs_7_ = bf16[768,256]{1,0:T(8,128)(2,1)} collective-permute-done((bf16[768,256]{1,0:T(8,128)(2,1)}, bf16[768,256]{1,0:T(8,128)(2,1)}, u32[]{:S(2)}, u32[]{:S(2)}) %collective-permute-start.6) | collective-permute-done | bytes 393248 | tf_op jit(solution)/shard_map/ppermute | solution.py:391
  137.1 3.7 %cross.5 = bf16[4,64,256]{2,1,0:T(8,128)(2,1)S(1)} custom-call(bf16[768,256]{1,0:T(8,128)(2,1)S(1)} %copy-done.1, bf16[768,256]{1,0:T(8,128)(2,1)S(1)} %collective-permute-done.refs_1_, bf16[768,256]{1,0:T(8,128)(2,1)S(1)} %collective-permute-done.1.refs_2_, bf16[768,256]{1,0:T(8,128)(2,1)S(1)} %collective-permute-done.2.refs_3_, ...), custom_call_target="tpu_custom_call" | custom-call | flops 10223616 | bytes 5111808 | tf_op jit(solution)/shard_map/cross/pallas_call | solution.py:275
  140.8 15.7 %all_to_all.10.stacks_ref = bf16[32,8,256]{2,1,0:T(8,128)(2,1)S(1)} all-to-all(bf16[32,8,256]{2,1,0:T(8,128)(2,1)S(1)} %bitcast.5), channel_id=1, replica_groups=mesh['seg'=4,'chan'=8] {'seg','chan'}, dimensions={0} | all-to-all | bytes 262144 | tf_op jit(solution)/shard_map/all_to_all | solution.py:442
  156.5 1.2 lags.1
  (14 shorter events, 0.0 us)
Async XLA Ops:
  19.2 79.7 %all-to-all-start = ((bf16[8,272,256]{2,1,0:T(8,128)(2,1)}), bf16[8,272,256]{2,1,0:T(8,128)(2,1)S(1)}, u32[]{:S(2)}, u32[]{:S(2)}) async-start(bf16[8,272,256]{2,1,0:T(8,128)(2,1)} %spectra.3), calls=%async_computation | async-start | bytes 2228224 | tf_op jit(solution)/shard_map/all_to_all | solution.py:387
  26.5 72.4 %copy-start.4 = (s32[2,352]{1,0:T(2,128)S(1)}, s32[2,352]{1,0:T(2,128)}, u32[]{:S(2)}) copy-start(s32[2,352]{1,0:T(2,128)} %constant.22.clone.refs_0_) | copy-start | bytes 8452
  26.5 72.4 %copy-start.5 = (s32[2,208]{1,0:T(2,128)S(1)}, s32[2,208]{1,0:T(2,128)}, u32[]{:S(2)}) copy-start(s32[2,208]{1,0:T(2,128)} %constant.24.clone.refs_2_) | copy-start | bytes 4996
  26.5 72.4 %copy-start.6 = (s32[2,240]{1,0:T(2,128)S(1)}, s32[2,240]{1,0:T(2,128)}, u32[]{:S(2)}) copy-start(s32[2,240]{1,0:T(2,128)} %constant.23.clone.refs_1_) | copy-start | bytes 5764
  68.5 58.4 %copy-start.1 = (bf16[768,256]{1,0:T(8,128)(2,1)S(1)}, bf16[768,256]{1,0:T(8,128)(2,1)}, u32[]{:S(2)}) copy-start(bf16[768,256]{1,0:T(8,128)(2,1)} %get-tuple-element.16.refs_0_) | copy-start | bytes 1179652
  68.5 18.6 %collective-permute-start = (bf16[768,256]{1,0:T(8,128)(2,1)}, bf16[768,256]{1,0:T(8,128)(2,1)S(1)}, u32[]{:S(2)}, u32[]{:S(2)}) collective-permute-start(bf16[768,256]{1,0:T(8,128)(2,1)} %get-tuple-element.17), channel_id=1, source_target_pairs={{0,1},{1,2},{2,3},{3,4},{4,5},{5,6},{6,7},{7,0},{8,9},{9,10},{10,1... | collective-permute-start | bytes 1179656 | tf_op jit(solution)/shard_map/ppermute | solution.py:391
  70.6 27.1 %collective-permute-start.1 = (bf16[768,256]{1,0:T(8,128)(2,1)}, bf16[768,256]{1,0:T(8,128)(2,1)S(1)}, u32[]{:S(2)}, u32[]{:S(2)}) collective-permute-start(bf16[768,256]{1,0:T(8,128)(2,1)} %get-tuple-element.18), channel_id=1, source_target_pairs={{0,7},{1,0},{2,1},{3,2},{4,3},{5,4},{6,5},{7,6},{8,15},{9,8},{10,9... | collective-permute-start | bytes 1179656 | tf_op jit(solution)/shard_map/ppermute | solution.py:391
  73.4 53.5 %collective-permute-start.2 = (bf16[768,256]{1,0:T(8,128)(2,1)}, bf16[768,256]{1,0:T(8,128)(2,1)S(1)}, u32[]{:S(2)}, u32[]{:S(2)}) collective-permute-start(bf16[768,256]{1,0:T(8,128)(2,1)} %get-tuple-element.19), channel_id=1, source_target_pairs={{0,4},{1,5},{2,6},{3,7},{4,0},{5,1},{6,2},{7,3},{8,12},{9,13},{10,... | collective-permute-start | bytes 1179656 | tf_op jit(solution)/shard_map/ppermute | solution.py:391
  74.4 52.5 %collective-permute-start.3 = (bf16[768,256]{1,0:T(8,128)(2,1)}, bf16[768,256]{1,0:T(8,128)(2,1)S(1)}, u32[]{:S(2)}, u32[]{:S(2)}) collective-permute-start(bf16[768,256]{1,0:T(8,128)(2,1)} %get-tuple-element.20), channel_id=1, source_target_pairs={{0,3},{1,4},{2,5},{3,6},{4,7},{5,0},{6,1},{7,2},{8,11},{9,12},{10,... | collective-permute-start | bytes 1179656 | tf_op jit(solution)/shard_map/ppermute | solution.py:391
  75.9 51.0 %collective-permute-start.4 = (bf16[768,256]{1,0:T(8,128)(2,1)}, bf16[768,256]{1,0:T(8,128)(2,1)S(1)}, u32[]{:S(2)}, u32[]{:S(2)}) collective-permute-start(bf16[768,256]{1,0:T(8,128)(2,1)} %get-tuple-element.21), channel_id=1, source_target_pairs={{0,5},{1,6},{2,7},{3,0},{4,1},{5,2},{6,3},{7,4},{8,13},{9,14},{10,... | collective-permute-start | bytes 1179656 | tf_op jit(solution)/shard_map/ppermute | solution.py:391
  87.2 42.2 %collective-permute-start.5 = (bf16[768,256]{1,0:T(8,128)(2,1)}, bf16[768,256]{1,0:T(8,128)(2,1)}, u32[]{:S(2)}, u32[]{:S(2)}) collective-permute-start(bf16[768,256]{1,0:T(8,128)(2,1)} %get-tuple-element.22), channel_id=1, source_target_pairs={{0,2},{1,3},{2,4},{3,5},{4,6},{5,7},{6,0},{7,1},{8,10},{9,11},{10,... | collective-permute-start | bytes 1179656 | tf_op jit(solution)/shard_map/ppermute | solution.py:391
  97.7 39.4 %collective-permute-start.6 = (bf16[768,256]{1,0:T(8,128)(2,1)}, bf16[768,256]{1,0:T(8,128)(2,1)}, u32[]{:S(2)}, u32[]{:S(2)}) collective-permute-start(bf16[768,256]{1,0:T(8,128)(2,1)} %get-tuple-element.23), channel_id=1, source_target_pairs={{0,6},{1,7},{2,0},{3,1},{4,2},{5,3},{6,4},{7,5},{8,14},{9,15},{10,... | collective-permute-start | bytes 1179656 | tf_op jit(solution)/shard_map/ppermute | solution.py:391
  129.3 27.2 %copy-start = (bf16[1024,1024]{1,0:T(8,128)(2,1)S(1)}, bf16[1024,1024]{1,0:T(8,128)(2,1)}, u32[]{:S(2)}) copy-start(bf16[1024,1024]{1,0:T(8,128)(2,1)} %constant.27.clone.odd_ref) | copy-start | bytes 6291460
  129.3 27.2 %copy-start.2 = (bf16[512,512]{1,0:T(8,128)(2,1)S(1)}, bf16[512,512]{1,0:T(8,128)(2,1)}, u32[]{:S(2)}) copy-start(bf16[512,512]{1,0:T(8,128)(2,1)} %constant.26.clone.two_ref) | copy-start | bytes 1572868
  129.3 27.2 %copy-start.3 = (bf16[512,512]{1,0:T(8,128)(2,1)S(1)}, bf16[512,512]{1,0:T(8,128)(2,1)}, u32[]{:S(2)}) copy-start(bf16[512,512]{1,0:T(8,128)(2,1)} %constant.25.clone.zero_ref) | copy-start | bytes 1572868

commit v6 on v4

--- a/solution.py
+++ b/solution.py
@@ -29,11 +29,13 @@
 LAGQ = NLAG // FOLD
 VMEM = 58 * 1024 * 1024
 VMEM_SMALL = 20 * 1024 * 1024
-BLOCK = 256
 META = 16
+KEPT = 112
+EARLY_SEGS = 2
+LATE_SEGS_A_BLOCK = 2
 
 SENT = (1, 7, 4, 3, 5, 2, 6)
-STAGES = (6, 7, 8)
+STAGES = (6, 8)
 
 
 ORDER = np.arange(NB).reshape(CLASS, FOLD).T.reshape(-1)
@@ -92,25 +94,62 @@
     return both[:rows] + both[rows:]
 
 
-def spectra_kernel(relative, with_meta, *refs):
+def ranks(mask_row):
+    shape = (LANES, LANES)
+    upto = lax.broadcasted_iota(jnp.int32, shape, 0) <= lax.broadcasted_iota(jnp.int32, shape, 1)
+    row = jnp.broadcast_to(mask_row, (META, LANES)).astype(jnp.bfloat16)
+    count = jnp.dot(row, upto.astype(jnp.float32).astype(jnp.bfloat16), preferred_element_type=jnp.float32)
+    return jnp.where(mask_row > 0, count[0:1] - 1.0, -1.0)
+
+
+def channel_of_place(shape, axis):
+    place = lax.broadcasted_iota(jnp.int32, shape, axis)
+    return (place % G) * (LANES // G) + place // G
+
+
+def spectra_kernel(relative, with_meta, kept, skip, *refs):
     f32, bf16 = jnp.float32, jnp.bfloat16
     refs = list(refs)
     here_ref = refs.pop(0) if relative else None
-    x_ref, mask_ref, owner_ref, bins_ref, source_ref = refs[:5]
-    out_refs = refs[5:-9]
-    table_ref, arrived, u, v, a, b, early, others, hold = refs[-9:]
-    target = refs[-10] if relative else out_refs[0]
-    first = pl.program_id(0) == 0
-    rows = x_ref.shape[0]
+    x_any, mask_ref, owner_ref, bins_ref, source_ref = refs[:5]
+    x_refs, table_ref, x_came, arrived, u, v, a, b, early, others = refs[-10:]
+    out_refs = refs[5:-11] if relative else refs[5:-10]
+    head = refs[-11] if relative else out_refs[0]
+    rest = out_refs[-1] if kept < LANES else None
+    step, steps = pl.program_id(0), pl.num_programs(0)
+    first = step == 0
+    rows = x_refs.shape[1]
+    slot = lax.rem(step, 2)
     copies = [
         pltpu.make_async_copy(source_ref.at[part], table_ref.at[part], arrived.at[part]) for part in range(FOLD)
     ]
 
+    def trace_copy(block, slot):
+        at = pl.ds(pl.multiple_of(block * rows + skip, LANES), rows)
+        return pltpu.make_async_copy(x_any.at[at], x_refs.at[slot], x_came.at[slot])
+
     @pl.when(first)
     def start():
+        trace_copy(0, 0).start()
         for copy in copies:
             copy.start()
 
+    mask = mask_ref[...].astype(f32)
+    shape = (LANES, LANES)
+    if kept < LANES:
+        chosen = ranks(mask) == lax.broadcasted_iota(jnp.int32, shape, 0).astype(f32)
+    else:
+        chosen = channel_of_place(shape, 0) == lax.broadcasted_iota(jnp.int32, shape, 1)
+        chosen = chosen & (jnp.broadcast_to(mask, shape) > 0)
+    chosen = chosen.astype(f32).astype(bf16)
+
+    trace_copy(step, slot).wait()
+
+    @pl.when(step + 1 < steps)
+    def ahead():
+        trace_copy(step + 1, 1 - slot).start()
+
+    x_ref = x_refs.at[slot]
     x = [x_ref[:, m * QUARTER:(m + 1) * QUARTER].astype(f32) for m in range(FOLD)]
     even, odd = x[0] + x[2], x[1] + x[3]
     u[:rows], u[rows:] = two_terms(even + odd)
@@ -137,66 +176,65 @@
     bin_ = (lane % CLASS) * FOLD + lane // CLASS
     within = jnp.minimum(bin_ + HW, NB - 1) - jnp.maximum(bin_ - HW, 0) + 1
     mean = jnp.dot(power, table_ref[3], preferred_element_type=f32) * (1.0 / within.astype(f32))
-    shape = (LANES, LANES)
-    diagonal = lax.broadcasted_iota(jnp.int32, shape, 0) == lax.broadcasted_iota(jnp.int32, shape, 1)
-    mask = jnp.where(diagonal, jnp.broadcast_to(mask_ref[...], shape), 0).astype(f32)
-    mask = jnp.sum(mask, axis=1, keepdims=True)
-    weight = jnp.concatenate([mask] * (rows // LANES), axis=0) * lax.rsqrt(mean + EPSILON)
-    per_group = LANES // G
+    weight = lax.rsqrt(mean + EPSILON)
+    spare = LANES - kept
     for piece in range(SLICES):
         ref, start = holders[piece // 2]
         start += (piece % 2) * LANES
         scale = weight[:, piece * LANES:(piece + 1) * LANES]
-        hold[0] = ref[:, start:start + LANES] * scale
-        hold[1] = ref[:, CLASS + start:CLASS + start + LANES] * scale
+        real = (ref[:, start:start + LANES] * scale).astype(bf16)
+        imag = (ref[:, CLASS + start:CLASS + start + LANES] * scale).astype(bf16)
+        both = jnp.concatenate([real, imag], axis=1)
         for seg in range(rows // LANES):
-            for j in range(per_group):
-                at = seg * LANES + j * G
-                for half in range(2):
-                    taken = hold[half, pl.ds(seg * LANES + j, G, stride=per_group), :]
-                    target[piece, at:at + G, half * LANES:(half + 1) * LANES] = taken.astype(bf16)
+            sorted_ = jnp.dot(chosen, both[seg * LANES:(seg + 1) * LANES], preferred_element_type=f32).astype(bf16)
+            head[piece, seg * kept:(seg + 1) * kept, :] = sorted_[:kept]
+            if spare:
+                rest[piece, seg * spare:(seg + 1) * spare, :] = sorted_[kept:]
     if with_meta:
         tiles = owner_ref.shape[1]
         labels = (owner_ref[...] * BIN_DEV + bins_ref[...]).astype(f32)
         for piece in range(SLICES):
-            at = pl.ds(rows, META)
-            target[piece, at, :] = jnp.zeros((META, 2 * LANES), bf16)
-            target[piece, at, :LANES] = jnp.broadcast_to(mask_ref[...].astype(f32), (META, LANES)).astype(bf16)
-            target[piece, at, LANES:LANES + tiles] = jnp.broadcast_to(labels, (META, tiles)).astype(bf16)
+            at = pl.ds(rows // LANES * kept, META)
+            head[piece, at, :] = jnp.zeros((META, 2 * LANES), bf16)
+            head[piece, at, :LANES] = jnp.broadcast_to(mask, (META, LANES)).astype(bf16)
+            head[piece, at, LANES:LANES + tiles] = jnp.broadcast_to(labels, (META, tiles)).astype(bf16)
     if relative:
-        for slot in range(SLICES):
-            out_refs[slot][...] = target[lax.rem(here_ref[0] + slot, SLICES)]
-
-
-def spectra(traces, mask, owners, bins, first_row, rows, here=None, with_meta=False):
-    block, relative = BLOCK, here is not None
-    skip = first_row // block
-    whole = lambda shape: pl.BlockSpec(shape, lambda i, *_: (0, 0))
-    in_specs = [
-        pl.BlockSpec((block, NT), lambda i, *_: (i + skip, 0)),
-        whole(mask.shape),
-        whole(owners.shape),
-        whole(bins.shape),
-        pl.BlockSpec(memory_space=pl.ANY),
+        for other in range(SLICES):
+            out_refs[other][...] = head[lax.rem(here_ref[0] + other, SLICES)]
+
+
+def spectra(traces, mask, owners, bins, first_row, rows, block, kept, here=None, with_meta=False):
+    relative = here is not None
+    table = jnp.asarray(forward_tables()).reshape(FOLD, QUARTER, NB)
+    whole = lambda array: pl.BlockSpec(array.shape, lambda i, *_: (0, 0))
+    in_place = pl.BlockSpec(memory_space=pl.ANY)
+    f32, bf16 = jnp.float32, jnp.bfloat16
+    segs = block // LANES
+    scratch = [
+        pltpu.VMEM((2, block, NT), bf16),
+        pltpu.VMEM(table.shape, bf16),
+        pltpu.SemaphoreType.DMA((2,)),
+        pltpu.SemaphoreType.DMA((FOLD,)),
     ]
-    f32, bf16 = jnp.float32, jnp.bfloat16
-    scratch = [pltpu.VMEM((FOLD, QUARTER, NB), bf16), pltpu.SemaphoreType.DMA((FOLD,))]
-    scratch += [pltpu.VMEM((2 * block, QUARTER), bf16)] * 4
-    scratch += [pltpu.VMEM((block, 4 * CLASS), f32)] * 2 + [pltpu.VMEM((2, block, LANES), f32)]
+    scratch += [pltpu.VMEM((2 * block, QUARTER), bf16)] * 4 + [pltpu.VMEM((block, 4 * CLASS), f32)] * 2
     if relative:
-        scratch = [pltpu.VMEM((SLICES, block, 2 * LANES), bf16)] + scratch
-        out_specs = [pl.BlockSpec((block, 2 * LANES), lambda i, *_: (i, 0))] * SLICES
-        out_shape = [jax.ShapeDtypeStruct((rows, 2 * LANES), bf16)] * SLICES
+        scratch = [pltpu.VMEM((SLICES, segs * kept, 2 * LANES), bf16)] + scratch
+        out_specs = [pl.BlockSpec((segs * kept, 2 * LANES), lambda i, *_: (i, 0))] * SLICES
+        out_shape = [jax.ShapeDtypeStruct((rows // LANES * kept, 2 * LANES), bf16)] * SLICES
     else:
         extra = META if with_meta else 0
-        out_specs = [pl.BlockSpec((SLICES, block + extra, 2 * LANES), lambda i, *_: (0, i, 0))]
-        out_shape = [jax.ShapeDtypeStruct((SLICES, rows + extra, 2 * LANES), bf16)]
-    result = pl.pallas_call(
-        functools.partial(spectra_kernel, relative, with_meta),
+        out_specs = [pl.BlockSpec((SLICES, segs * kept + extra, 2 * LANES), lambda i, *_: (0, i, 0))]
+        out_shape = [jax.ShapeDtypeStruct((SLICES, rows // LANES * kept + extra, 2 * LANES), bf16)]
+    if kept < LANES:
+        spare = LANES - kept
+        out_specs += [pl.BlockSpec((SLICES, segs * spare, 2 * LANES), lambda i, *_: (0, i, 0))]
+        out_shape += [jax.ShapeDtypeStruct((SLICES, rows // LANES * spare, 2 * LANES), bf16)]
+    return pl.pallas_call(
+        functools.partial(spectra_kernel, relative, with_meta, kept, first_row),
         grid_spec=pltpu.PrefetchScalarGridSpec(
             num_scalar_prefetch=1 if relative else 0,
             grid=(rows // block,),
-            in_specs=in_specs,
+            in_specs=[in_place, whole(mask), whole(owners), whole(bins), in_place],
             out_specs=out_specs,
             scratch_shapes=scratch,
         ),
@@ -206,8 +244,7 @@
             flops=14 * rows * NB * NB, bytes_accessed=rows * NT * 3 + 8 * NB * NB, transcendentals=rows * NB
         ),
         name="spectra",
-    )(*([here] if relative else []), traces, mask, owners, bins, jnp.asarray(forward_tables()).reshape(FOLD, QUARTER, NB))
-    return result if relative else result[0]
+    )(*([here] if relative else []), traces, mask, owners, bins, table)
 
 
 def pair_sums(block_refs, pairs, steps, tiles):
@@ -243,14 +280,40 @@
             done += G
 
 
-def cross_kernel(split, pairs, steps, has_before, *refs):
+def place_rows(head_ref, rest_ref, rest_row, places, out_ref):
+    spare = LANES - KEPT
+    for seg in range(out_ref.shape[0] // LANES):
+        at = rest_row + seg * spare
+        rows = jnp.concatenate([head_ref[seg * KEPT:(seg + 1) * KEPT], rest_ref[at:at + spare]], axis=0)
+        placed = jnp.dot(places, rows, preferred_element_type=jnp.float32)
+        out_ref[seg * LANES:(seg + 1) * LANES, :] = placed.astype(out_ref.dtype)
+
+
+def cross_kernel(plan, here_ref, *refs):
     f32 = jnp.float32
     refs = list(refs)
-    before_ref = refs.pop(-3) if has_before else None
-    *block_refs, rows_ref, out_ref, tiles = refs
-    if split:
-        block_refs = [block_refs[0].at[m] for m in range(block_refs[0].shape[0])]
-    pair_sums(block_refs, pairs, steps, tiles)
+    take = lambda count: [refs.pop(0) for _ in range(count)]
+    ready, heads = take(plan["ready"]), take(plan["heads"])
+    rest_ref, places_ref = take(2) if heads else (None, None)
+    (rows_ref,) = take(1)
+    before_ref = refs.pop(0) if plan["before"] else None
+    out_ref = refs.pop(0)
+    placed = take(len(plan["slots"])) if plan["hand_on"] else None
+    tiles = refs.pop(0)
+    if plan["stacked"]:
+        source = heads[0] if heads else ready[0]
+        count = source.shape[0]
+        heads = [source.at[m] for m in range(count)] if heads else []
+        ready = [] if heads else [source.at[m] for m in range(count)]
+    if heads:
+        if placed is None:
+            (room,) = refs
+            placed = [room.at[i] for i in range(len(heads))]
+        for i, head in enumerate(heads):
+            block = i if plan["stacked"] else lax.rem(here_ref[0] - plan["slots"][i] + SLICES, SLICES)
+            place_rows(head, rest_ref.at[block], plan["rest_row"], places_ref[block], placed[i])
+        ready = ready + placed
+    pair_sums(ready, plan["pairs"], plan["steps"], tiles)
     bins, count = out_ref.shape[-2], tiles.shape[0]
     wanted = rows_ref[0:1, :] == lax.broadcasted_iota(jnp.int32, (bins, count), 0).astype(f32)
     high, low = two_terms(tiles[...])
@@ -263,7 +326,7 @@
         both = both[:bins] + both[bins:]
         stacked.append(both + jnp.dot(weights[:bins], low[:, at], preferred_element_type=f32))
     stacked = jnp.concatenate(stacked, axis=1)
-    if has_before:
+    if before_ref is not None:
         stacked += before_ref[...]
     if len(out_ref.shape) == 2:
         out_ref[...] = stacked
@@ -272,26 +335,44 @@
             out_ref[copy] = stacked.astype(out_ref.dtype)
 
 
-def cross(blocks, pairs, steps, bins, weights, before=None, copies=None):
+def cross(here, pairs, steps, bins, weights, ready=(), heads=(), slots=(), rest=None, rest_row=0, places=None,
+          before=None, copies=None, hand_on=False, stacked=False):
     shape = (bins, 2 * LANES)
-    split = not isinstance(blocks, (list, tuple))
-    inputs = ([blocks] if split else list(blocks)) + [weights]
+    inputs = list(ready) + list(heads) + ([rest, places] if heads else []) + [weights]
     if before is not None:
         inputs.append(before)
     if copies is None:
-        out_shape = jax.ShapeDtypeStruct(shape, jnp.float32)
+        out_shape = [jax.ShapeDtypeStruct(shape, jnp.float32)]
     else:
-        out_shape = jax.ShapeDtypeStruct((copies,) + shape, jnp.bfloat16)
-    return pl.pallas_call(
-        functools.partial(cross_kernel, split, pairs, steps, before is not None),
+        out_shape = [jax.ShapeDtypeStruct((copies,) + shape, jnp.bfloat16)]
+    scratch = [pltpu.VMEM((len(pairs) * G, 2 * LANES), jnp.float32)]
+    if hand_on:
+        out_shape += [jax.ShapeDtypeStruct((G * steps, 2 * LANES), jnp.bfloat16)] * len(heads)
+    elif heads:
+        count = heads[0].shape[0] if stacked else len(heads)
+        scratch.append(pltpu.VMEM((count, G * steps, 2 * LANES), jnp.bfloat16))
+    plan = dict(
+        ready=len(ready), heads=len(heads), slots=slots, before=before is not None, hand_on=hand_on,
+        stacked=stacked, rest_row=rest_row, pairs=pairs, steps=steps,
+    )
+    whole = lambda array: pl.BlockSpec(array.shape, lambda i, *_: (0,) * len(array.shape))
+    result = pl.pallas_call(
+        functools.partial(cross_kernel, plan),
+        grid_spec=pltpu.PrefetchScalarGridSpec(
+            num_scalar_prefetch=1,
+            grid=(1,),
+            in_specs=[whole(array) for array in inputs],
+            out_specs=[whole(array) for array in out_shape],
+            scratch_shapes=scratch,
+        ),
         out_shape=out_shape,
-        scratch_shapes=[pltpu.VMEM((len(pairs) * G, 2 * LANES), jnp.float32)],
-        compiler_params=pltpu.CompilerParams(vmem_limit_bytes=VMEM_SMALL if copies is None or not split else VMEM),
+        compiler_params=pltpu.CompilerParams(vmem_limit_bytes=VMEM if stacked and copies else VMEM_SMALL),
         cost_estimate=pl.CostEstimate(
             flops=8 * G * steps * LANES * len(pairs), bytes_accessed=4 * G * steps * LANES * len(pairs), transcendentals=0
         ),
         name="cross",
-    )(*inputs)
+    )(here, *inputs)
+    return result if hand_on else result[0]
 
 
 def weights_kernel(blocks, total_segs, here_ref, meta_ref, *refs):
@@ -301,7 +382,16 @@
     empty = jnp.zeros((R, LANES), bf16)
     padded = jnp.concatenate([masks.astype(f32), empty.astype(f32)], axis=0)
     half = len(refs) // 2
-    for ends_ref, out_ref in zip(refs[:half], refs[half:]):
+    places_ref = refs[-1]
+    shape = (LANES, LANES)
+    channel = lax.broadcasted_iota(jnp.int32, shape, 1)
+    of_place = (channel_of_place(shape, 0) == channel).astype(f32).astype(bf16)
+    for b in range(blocks):
+        rank = ranks(masks[b:b + 1].astype(f32))
+        sorted_ = (rank == lax.broadcasted_iota(jnp.int32, shape, 0).astype(f32)).astype(f32).astype(bf16)
+        places = lax.dot_general(of_place, sorted_, (((1,), (1,)), ((), ())), preferred_element_type=f32)
+        places_ref[b] = places.astype(bf16)
+    for ends_ref, out_ref in zip(refs[:half], refs[half:-1]):
         lanes = out_ref.shape[1]
         first, second = ends_ref[0:1, :], ends_ref[1:2, :]
         slots = first < 0
@@ -336,9 +426,11 @@
             grid=(1,),
             in_specs=[pl.BlockSpec((blocks, META, 2 * LANES), lambda i, *_: (0, at // META, 0))]
             + [whole(end.shape) for end in ends],
-            out_specs=[whole(shape) for shape in shapes],
+            out_specs=[whole(shape) for shape in shapes]
+            + [pl.BlockSpec((blocks, LANES, LANES), lambda i, *_: (0, 0, 0))],
         ),
-        out_shape=[jax.ShapeDtypeStruct(shape, jnp.float32) for shape in shapes],
+        out_shape=[jax.ShapeDtypeStruct(shape, jnp.float32) for shape in shapes]
+        + [jax.ShapeDtypeStruct((blocks, LANES, LANES), jnp.bfloat16)],
         compiler_params=pltpu.CompilerParams(vmem_limit_bytes=VMEM_SMALL),
         name="weights",
     )(here, meta, *ends)
@@ -385,15 +477,27 @@
 def sent_along(x, mask, owners, bins, total_segs):
     seg_count = lax.axis_size("seg")
     count = lax.axis_size("chan")
-    early = BLOCK
+    early = EARLY_SEGS * LANES
     late = x.shape[0] - early
+    spare = LANES - KEPT
     here = lax.axis_index("chan").astype(jnp.int32).reshape(1)
-    first = spectra(x, mask, owners, bins, 0, early, with_meta=True)
+    first, spare_early = spectra(x, mask, owners, bins, 0, early, early, KEPT, with_meta=True)
     first = lax.all_to_all(first, "chan", split_axis=0, concat_axis=0, tiled=True)
-    second = spectra(x, mask, owners, bins, early, late, here=here)
+    *second, spare_late = spectra(
+        x, mask, owners, bins, early, late, LATE_SEGS_A_BLOCK * LANES, KEPT, here=here
+    )
     slots = {0: second[0]}
     for shift in SENT:
         slots[shift] = lax.ppermute(second[shift], "chan", [(i, (i + shift) % count) for i in range(count)])
+
+    at = EARLY_SEGS * KEPT
+    most = jnp.max(jnp.sum(first[:, at, :LANES].astype(jnp.float32), axis=1))
+    rest = lax.cond(
+        most > KEPT,
+        lambda rows: lax.all_to_all(jnp.concatenate(rows, axis=1), "chan", split_axis=0, concat_axis=0, tiled=True),
+        lambda rows: jnp.zeros((count, (early + late) // LANES * spare, 2 * LANES), jnp.bfloat16),
+        (spare_early, spare_late),
+    )
 
     fixed = fixed_pairs(count)
     known = (0,) + SENT
@@ -401,14 +505,24 @@
         [(i, j) for j in range(start, end) for i in range(j)] for start, end in zip((1,) + STAGES, STAGES)
     ]
     as_slots = lambda pairs: [(-known[i] - count, -known[j] - count) for i, j in pairs]
-    weights = pair_weights(here, first, early, total_segs, [fixed] + [as_slots(pairs) for pairs in stages])
-    rows = count * BIN_DEV
-    stacks = cross(first, fixed, early // G, rows, weights[0])
-    held = [slots[slot] for slot in known]
+    weights = pair_weights(here, first, at, total_segs, [fixed] + [as_slots(pairs) for pairs in stages])
+    places = weights[-1]
+    bins = count * BIN_DEV
+    stacks = cross(
+        here, fixed, early // G, bins, weights[0], heads=[first], rest=rest, places=places, stacked=True
+    )
+    ready, start = [], 0
     for end, pairs, weight in zip(STAGES, stages, weights[1:]):
-        copies = seg_count if end == len(known) else None
-        stacks = cross(held[:end], pairs, late // G, rows, weight, before=stacks, copies=copies)
-    return stacks
+        final = end == len(known)
+        result = cross(
+            here, pairs, late // G, bins, weight,
+            ready=ready, heads=[slots[slot] for slot in known[start:end]], slots=known[start:end],
+            rest=rest, rest_row=EARLY_SEGS * spare, places=places, before=stacks,
+            copies=seg_count if final else None, hand_on=not final,
+        )
+        if final:
+            return result
+        stacks, ready, start = result[0], ready + list(result[1:]), end
 
 
 def sent_at_once(x, mask, owners, bins, total_segs):
@@ -423,14 +537,16 @@
     every = jnp.pad(every, ((0, 0), (0, 2 * LANES - every.shape[1])))
     every = jnp.broadcast_to(every[:, None, :], (count, META, 2 * LANES))
     fixed = fixed_pairs(count)
-    weights = pair_weights(here, every, 0, total_segs, [fixed])
-    outgoing = spectra(x, mask, owners, bins, 0, rows)
+    weights = pair_weights(here, every, 0, total_segs, [fixed])[:1]
+    (outgoing,) = spectra(x, mask, owners, bins, 0, rows, 2 * LANES, LANES)
     outgoing = outgoing.reshape(SLICES, rows, 2, splits, narrow).transpose(0, 3, 1, 2, 4)
     outgoing = outgoing.reshape(count, rows, 2 * narrow)
     wide = lax.all_to_all(outgoing, "chan", split_axis=0, concat_axis=0, tiled=True)
     wide = jnp.pad(wide.reshape(count, rows, 2, narrow), ((0, 0), (0, 0), (0, 0), (0, LANES - narrow)))
     wide = wide.reshape(count, rows, 2 * LANES)
-    stacks = cross(wide, fixed, rows // G, count * BIN_DEV, weights[0], copies=seg_count)
+    stacks = cross(
+        here, fixed, rows // G, count * BIN_DEV, weights[0], ready=[wide], copies=seg_count, stacked=True
+    )
     return stacks.reshape(-1, 2, LANES)[..., :narrow]
 
 

time: 129 us -> 125 us (0.969)
  waiting for transfers between devices: 50.8 us -> 35.3 us
  Pallas kernels: 41.1 us -> 48.6 us
  local copies, waits for them, and re-layouts: 0.06 us -> 3.6 us
  blocking collectives: 18.2 us -> 16.2 us
    ppermute x7, waiting for transfers between devices: 50.8 us -> 35.3 us  [sent_along(): lax.ppermute(second[shift], 'chan', [(i, (i + shift) % count) for i in ra...]
    pallas_call x6 -> x5, Pallas kernels: 39.6 us -> 46.5 us  [the longest x2 35 us: spectra(): pl.pallas_call(functools.partial(spectra_kernel, relative, with_meta, kep...]
    unnamed x16 -> x18, local copies, waits for them, and re-layouts: 0.06 us -> 2.76 us
    all_to_all x1, blocking collectives: 18.2 us -> 16.2 us  [per_device(): lax.all_to_all(stacks, ('seg', 'chan'), split_axis=0, concat_axis=0, tile...]
  transfers between devices with their start and end apart: 8 -> 8, of which waited for: 4 -> 4; matrix products, arithmetic and copies ran while one was open for 0% -> 1% of each run, Pallas kernels for 22% -> 26%
where the time goes in v6:
time: 125 us; the launch traced here: 124 us
  Pallas kernels  48.6 us (39%)
  waiting for transfers between devices  35.3 us (28%)
  starting transfers between devices  19.1 us (15%)
  blocking collectives  16.2 us (13%)
  local copies, waits for them, and re-layouts  3.6 us (3%)
    ppermute x7, waiting for transfers between devices, sent_along(): lax.ppermute(second[shift], 'chan', [(i, (i + shift) % count) for i in ra...  35.3 us
    pallas_call x2, Pallas kernels, spectra(): pl.pallas_call(functools.partial(spectra_kernel, relative, with_meta, kep...  35 us
    all_to_all x1, blocking collectives, per_device(): lax.all_to_all(stacks, ('seg', 'chan'), split_axis=0, concat_axis=0, tile...  16.2 us
    ppermute x7, starting transfers between devices, sent_along(): lax.ppermute(second[shift], 'chan', [(i, (i + shift) % count) for i in ra...  11.8 us
    pallas_call x3, Pallas kernels, cross(): pl.pallas_call(functools.partial(cross_kernel, plan), grid_spec=pltpu.Pre...  11.5 us
    all_to_all x1, starting transfers between devices, sent_along(): lax.all_to_all(first, 'chan', split_axis=0, concat_axis=0, tiled=True)  7.29 us
    unnamed x18, local copies, waits for them, and re-layouts  2.76 us
  transfers between devices with their start and end apart: 8, of which 4 were waited for; matrix products, arithmetic and copies ran while one was open for 1% of the time, Pallas kernels for 26%

profile of v6, /device:TPU:0, one launch (start us, length us, event | category | flops | bytes accessed | tf_op | source)
XLA Modules:
  0.0 124.5 jit_solution(8386585812579378685)
XLA Ops:
  0.0 11.5 %spectra.3 = (bf16[8,240,256]{2,1,0:T(8,128)(2,1)}, bf16[8,32,256]{2,1,0:T(8,128)(2,1)}) custom-call(bf16[1024,4096]{1,0:T(8,128)(2,1)} %bitcast.6, s32[1,128]{1,0:T(1,128)} %bitcast.8, s32[1,64]{1,0:T(1,128)} %bitcast.10, s32[1,64]{1,0:T(1,128)} %refs_3_.1, bf16[4,1024,1024]{2,1,0:T(8,128)(2,1)} %constant.35.refs_5_.refs_4_), custom_call_target="tpu_custom_call" | custom-call | flops 3758096384 | bytes 11534336 | tf_op jit(solution)/shard_map/spectra/pallas_call | solution.py:232
  11.5 7.3 %all-to-all-start.1 = ((bf16[8,240,256]{2,1,0:T(8,128)(2,1)}), bf16[8,240,256]{2,1,0:T(8,128)(2,1)S(1)}, u32[]{:S(2)}, u32[]{:S(2)}) async-start(bf16[8,240,256]{2,1,0:T(8,128)(2,1)} %get-tuple-element.42), calls=%async_computation.1 | async-start | bytes 1966080 | tf_op jit(solution)/shard_map/all_to_all | solution.py:485
  18.8 23.5 %spectra.2 = (bf16[672,256]{1,0:T(8,128)(2,1)}, bf16[672,256]{1,0:T(8,128)(2,1)}, bf16[672,256]{1,0:T(8,128)(2,1)}, bf16[672,256]{1,0:T(8,128)(2,1)}, bf16[672,2...) custom-call(s32[1]{0:T(128)} %bitcast.refs_0_.here_ref, ...), custom_call_target="tpu_custom_call" | custom-call | flops 11274289152 | bytes 17825792 | tf_op jit(solution)/shard_map/spectra/pallas_call | solution.py:232
  42.3 2.1 %collective-permute-start = (bf16[672,256]{1,0:T(8,128)(2,1)}, bf16[672,256]{1,0:T(8,128)(2,1)S(1)}, u32[]{:S(2)}, u32[]{:S(2)}) collective-permute-start(bf16[672,256]{1,0:T(8,128)(2,1)} %get-tuple-element.37), channel_id=1, source_target_pairs={{0,1},{1,2},{2,3},{3,4},{4,5},{5,6},{6,7},{7,0},{8,9},{9,10},{10,1... | collective-permute-start | bytes 1032200 | tf_op jit(solution)/shard_map/ppermute | solution.py:491
  44.4 2.8 %collective-permute-start.1 = (bf16[672,256]{1,0:T(8,128)(2,1)}, bf16[672,256]{1,0:T(8,128)(2,1)S(1)}, u32[]{:S(2)}, u32[]{:S(2)}) collective-permute-start(bf16[672,256]{1,0:T(8,128)(2,1)} %get-tuple-element.38), channel_id=1, source_target_pairs={{0,7},{1,0},{2,1},{3,2},{4,3},{5,4},{6,5},{7,6},{8,15},{9,8},{10,9... | collective-permute-start | bytes 1032200 | tf_op jit(solution)/shard_map/ppermute | solution.py:491
  47.2 1.1 collective-permute-start.2
  48.2 1.5 %collective-permute-start.3 = (bf16[672,256]{1,0:T(8,128)(2,1)}, bf16[672,256]{1,0:T(8,128)(2,1)}, u32[]{:S(2)}, u32[]{:S(2)}) collective-permute-start(bf16[672,256]{1,0:T(8,128)(2,1)} %get-tuple-element.40), channel_id=1, source_target_pairs={{0,3},{1,4},{2,5},{3,6},{4,7},{5,0},{6,1},{7,2},{8,11},{9,12},{10,... | collective-permute-start | bytes 1032200 | tf_op jit(solution)/shard_map/ppermute | solution.py:491
  49.7 2.4 %collective-permute-start.4 = (bf16[672,256]{1,0:T(8,128)(2,1)}, bf16[672,256]{1,0:T(8,128)(2,1)}, u32[]{:S(2)}, u32[]{:S(2)}) collective-permute-start(bf16[672,256]{1,0:T(8,128)(2,1)} %get-tuple-element.41), channel_id=1, source_target_pairs={{0,5},{1,6},{2,7},{3,0},{4,1},{5,2},{6,3},{7,4},{8,13},{9,14},{10,... | collective-permute-start | bytes 1032200 | tf_op jit(solution)/shard_map/ppermute | solution.py:491
  52.1 6.8 %collective-permute-done.refs_1_ = bf16[672,256]{1,0:T(8,128)(2,1)S(1)} collective-permute-done((bf16[672,256]{1,0:T(8,128)(2,1)}, bf16[672,256]{1,0:T(8,128)(2,1)S(1)}, u32[]{:S(2)}, u32[]{:S(2)}) %collective-permute-start) | collective-permute-done | bytes 344096 | tf_op jit(solution)/shard_map/ppermute | solution.py:491
  58.8 1.0 collective-permute-start.5
  59.8 8.5 %collective-permute-done.1.refs_2_ = bf16[672,256]{1,0:T(8,128)(2,1)S(1)} collective-permute-done((bf16[672,256]{1,0:T(8,128)(2,1)}, bf16[672,256]{1,0:T(8,128)(2,1)S(1)}, u32[]{:S(2)}, u32[]{:S(2)}) %collective-permute-start.1) | collective-permute-done | bytes 344096 | tf_op jit(solution)/shard_map/ppermute | solution.py:491
  69.1 1.2 collective-permute-start.6
  71.8 0.9 conditional.1
  71.8 0.8 broadcast.2
  72.7 0.9 weights.1
  73.6 2.8 %cross.3.refs_9_ = f32[64,256]{1,0:T(8,128)S(1)} custom-call(s32[1]{0:T(128)} %bitcast.refs_0_.here_ref, bf16[8,240,256]{2,1,0:T(8,128)(2,1)S(1)} %all-to-all-done.1.meta_ref.refs_0_, bf16[8,128,256]{2,1,0:T(8,128)(2,1)} %get-tuple-element.58.refs_1_.refs_6_.refs_8_, bf16[8,128,128]{2,1,0:T(8,128)(2,1)S(1)} %get-tuple-element.45.refs_2_.refs_7_.refs_9_, ...), custom_call_target="tpu_custom_call" | custom-call | flops 5767168 | bytes 2883584 | tf_op jit(solution)/shard_map/cross/pallas_call | solution.py:359
  76.4 18.0 %collective-permute-done.2.refs_3_ = bf16[672,256]{1,0:T(8,128)(2,1)} collective-permute-done((bf16[672,256]{1,0:T(8,128)(2,1)}, bf16[672,256]{1,0:T(8,128)(2,1)}, u32[]{:S(2)}, u32[]{:S(2)}) %collective-permute-start.2) | collective-permute-done | bytes 344096 | tf_op jit(solution)/shard_map/ppermute | solution.py:491
  94.5 1.0 copy-done.3
  95.4 1.0 copy-done.5
  96.4 4.5 %cross.4 = (f32[64,256]{1,0:T(8,128)S(1)}, bf16[768,256]{1,0:T(8,128)(2,1)S(1)}, bf16[768,256]{1,0:T(8,128)(2,1)S(1)}, bf16[768,256]{1,0:T(8,128)(2,1)S(1)}, bf1...) custom-call(s32[1]{0:T(128)} %bitcast.refs_0_.here_ref, ...), custom_call_target="tpu_custom_call" | custom-call | flops 11796480 | bytes 5898240 | tf_op jit(solution)/shard_map/cross/pallas_call | solution.py:359
  101.0 2.0 %collective-permute-done.6.refs_7_ = bf16[672,256]{1,0:T(8,128)(2,1)} collective-permute-done((bf16[672,256]{1,0:T(8,128)(2,1)}, bf16[672,256]{1,0:T(8,128)(2,1)}, u32[]{:S(2)}, u32[]{:S(2)}) %collective-permute-start.6) | collective-permute-done | bytes 344096 | tf_op jit(solution)/shard_map/ppermute | solution.py:491
  102.9 4.1 %cross.5 = bf16[4,64,256]{2,1,0:T(8,128)(2,1)S(1)} custom-call(s32[1]{0:T(128)} %bitcast.refs_0_.here_ref, bf16[768,256]{1,0:T(8,128)(2,1)S(1)} %get-tuple-element.48.refs_0_, bf16[768,256]{1,0:T(8,128)(2,1)S(1)} %get-tuple-element.49.refs_1_, bf16[768,256]{1,0:T(8,128)(2,1)S(1)} %get-tuple-element.50.refs_2_, ...), custom_call_target="tpu_custom_call" | custom-call | flops 10223616 | bytes 5111808 | tf_op jit(solution)/shard_map/cross/pallas_call | solution.py:359
  107.1 16.2 %all_to_all.15.stacks_ref = bf16[32,8,256]{2,1,0:T(8,128)(2,1)S(1)} all-to-all(bf16[32,8,256]{2,1,0:T(8,128)(2,1)S(1)} %bitcast.5), channel_id=1, replica_groups=mesh['seg'=4,'chan'=8] {'seg','chan'}, dimensions={0} | all-to-all | bytes 262144 | tf_op jit(solution)/shard_map/all_to_all | solution.py:563
  123.3 1.2 lags.1
  (22 shorter events, 1.6 us)
Async XLA Ops:
  11.5 58.8 %all-to-all-start.1 = ((bf16[8,240,256]{2,1,0:T(8,128)(2,1)}), bf16[8,240,256]{2,1,0:T(8,128)(2,1)S(1)}, u32[]{:S(2)}, u32[]{:S(2)}) async-start(bf16[8,240,256]{2,1,0:T(8,128)(2,1)} %get-tuple-element.42), calls=%async_computation.1 | async-start | bytes 1966080 | tf_op jit(solution)/shard_map/all_to_all | solution.py:485
  18.8 53.9 %copy-start.6 = (s32[2,352]{1,0:T(2,128)S(1)}, s32[2,352]{1,0:T(2,128)}, u32[]{:S(2)}) copy-start(s32[2,352]{1,0:T(2,128)} %constant.27.clone.refs_0_) | copy-start | bytes 8452
  18.8 53.9 %copy-start.7 = (s32[2,208]{1,0:T(2,128)S(1)}, s32[2,208]{1,0:T(2,128)}, u32[]{:S(2)}) copy-start(s32[2,208]{1,0:T(2,128)} %constant.29.clone.refs_2_) | copy-start | bytes 4996
  18.8 53.9 %copy-start.8 = (s32[2,240]{1,0:T(2,128)S(1)}, s32[2,240]{1,0:T(2,128)}, u32[]{:S(2)}) copy-start(s32[2,240]{1,0:T(2,128)} %constant.28.clone.refs_1_) | copy-start | bytes 5764
  42.3 81.0 %copy-start = (bf16[1024,1024]{1,0:T(8,128)(2,1)S(1)}, bf16[1024,1024]{1,0:T(8,128)(2,1)}, u32[]{:S(2)}) copy-start(bf16[1024,1024]{1,0:T(8,128)(2,1)} %constant.32.clone.odd_ref) | copy-start | bytes 6291460
  42.3 16.5 %collective-permute-start = (bf16[672,256]{1,0:T(8,128)(2,1)}, bf16[672,256]{1,0:T(8,128)(2,1)S(1)}, u32[]{:S(2)}, u32[]{:S(2)}) collective-permute-start(bf16[672,256]{1,0:T(8,128)(2,1)} %get-tuple-element.37), channel_id=1, source_target_pairs={{0,1},{1,2},{2,3},{3,4},{4,5},{5,6},{6,7},{7,0},{8,9},{9,10},{10,1... | collective-permute-start | bytes 1032200 | tf_op jit(solution)/shard_map/ppermute | solution.py:491
  44.4 23.9 %collective-permute-start.1 = (bf16[672,256]{1,0:T(8,128)(2,1)}, bf16[672,256]{1,0:T(8,128)(2,1)S(1)}, u32[]{:S(2)}, u32[]{:S(2)}) collective-permute-start(bf16[672,256]{1,0:T(8,128)(2,1)} %get-tuple-element.38), channel_id=1, source_target_pairs={{0,7},{1,0},{2,1},{3,2},{4,3},{5,4},{6,5},{7,6},{8,15},{9,8},{10,9... | collective-permute-start | bytes 1032200 | tf_op jit(solution)/shard_map/ppermute | solution.py:491
  47.2 47.3 %collective-permute-start.2 = (bf16[672,256]{1,0:T(8,128)(2,1)}, bf16[672,256]{1,0:T(8,128)(2,1)}, u32[]{:S(2)}, u32[]{:S(2)}) collective-permute-start(bf16[672,256]{1,0:T(8,128)(2,1)} %get-tuple-element.39), channel_id=1, source_target_pairs={{0,4},{1,5},{2,6},{3,7},{4,0},{5,1},{6,2},{7,3},{8,12},{9,13},{10,... | collective-permute-start | bytes 1032200 | tf_op jit(solution)/shard_map/ppermute | solution.py:491
  48.2 46.2 %collective-permute-start.3 = (bf16[672,256]{1,0:T(8,128)(2,1)}, bf16[672,256]{1,0:T(8,128)(2,1)}, u32[]{:S(2)}, u32[]{:S(2)}) collective-permute-start(bf16[672,256]{1,0:T(8,128)(2,1)} %get-tuple-element.40), channel_id=1, source_target_pairs={{0,3},{1,4},{2,5},{3,6},{4,7},{5,0},{6,1},{7,2},{8,11},{9,12},{10,... | collective-permute-start | bytes 1032200 | tf_op jit(solution)/shard_map/ppermute | solution.py:491
  49.7 44.8 %collective-permute-start.4 = (bf16[672,256]{1,0:T(8,128)(2,1)}, bf16[672,256]{1,0:T(8,128)(2,1)}, u32[]{:S(2)}, u32[]{:S(2)}) collective-permute-start(bf16[672,256]{1,0:T(8,128)(2,1)} %get-tuple-element.41), channel_id=1, source_target_pairs={{0,5},{1,6},{2,7},{3,0},{4,1},{5,2},{6,3},{7,4},{8,13},{9,14},{10,... | collective-permute-start | bytes 1032200 | tf_op jit(solution)/shard_map/ppermute | solution.py:491
  58.8 42.1 %collective-permute-start.5 = (bf16[672,256]{1,0:T(8,128)(2,1)}, bf16[672,256]{1,0:T(8,128)(2,1)}, u32[]{:S(2)}, u32[]{:S(2)}) collective-permute-start(bf16[672,256]{1,0:T(8,128)(2,1)} %get-tuple-element.54), channel_id=1, source_target_pairs={{0,2},{1,3},{2,4},{3,5},{4,6},{5,7},{6,0},{7,1},{8,10},{9,11},{10,... | collective-permute-start | bytes 1032200 | tf_op jit(solution)/shard_map/ppermute | solution.py:491
  68.3 0.8 copy-start.4
  69.1 33.9 %collective-permute-start.6 = (bf16[672,256]{1,0:T(8,128)(2,1)}, bf16[672,256]{1,0:T(8,128)(2,1)}, u32[]{:S(2)}, u32[]{:S(2)}) collective-permute-start(bf16[672,256]{1,0:T(8,128)(2,1)} %get-tuple-element.55), channel_id=1, source_target_pairs={{0,6},{1,7},{2,0},{3,1},{4,2},{5,3},{6,4},{7,5},{8,14},{9,15},{10,... | collective-permute-start | bytes 1032200 | tf_op jit(solution)/shard_map/ppermute | solution.py:491
  72.7 50.7 %copy-start.1 = (bf16[512,512]{1,0:T(8,128)(2,1)S(1)}, bf16[512,512]{1,0:T(8,128)(2,1)}, u32[]{:S(2)}) copy-start(bf16[512,512]{1,0:T(8,128)(2,1)} %constant.31.clone.two_ref) | copy-start | bytes 1572868
  72.7 50.7 %copy-start.2 = (bf16[512,512]{1,0:T(8,128)(2,1)S(1)}, bf16[512,512]{1,0:T(8,128)(2,1)}, u32[]{:S(2)}) copy-start(bf16[512,512]{1,0:T(8,128)(2,1)} %constant.30.clone.zero_ref) | copy-start | bytes 1572868
  94.5 1.0 copy-start.3
  95.4 1.0 copy-start.5

commit v7 on v6

--- a/solution.py
+++ b/solution.py
@@ -42,29 +42,25 @@
 
 
 def forward_tables():
-    samples = np.arange(NT // 2, dtype=np.int64)
+    samples = np.arange(QUARTER, dtype=np.int64)
     freqs = K0 + ORDER.astype(np.int64)
     phase = samples[:, None] * freqs[None, :] % NT
     angle = (phase.astype(np.float32) * np.float32(2.0 * math.pi / NT)).astype(np.float64)
     cos = np.cos(angle).astype(np.float32).astype(ml_dtypes.bfloat16)
     sin = (-np.sin(angle)).astype(np.float32).astype(ml_dtypes.bfloat16)
 
-    def part(which, rows):
+    def part(which):
         columns = slice(which * CLASS, (which + 1) * CLASS)
-        return [cos[rows, columns], sin[rows, columns]]
-
-    low, high = slice(0, QUARTER), slice(QUARTER, 2 * QUARTER)
-    band = (np.abs(ORDER[:, None] - ORDER[None, :]) <= HW).astype(ml_dtypes.bfloat16)
-    table = np.concatenate(
-        [
-            np.concatenate(part(0, low) + part(2, low), axis=1),
-            np.concatenate(part(1, low) + part(3, low), axis=1),
-            np.concatenate(part(1, high) + part(3, high), axis=1),
-            band,
-        ],
-        axis=0,
-    )
-    return table
+        return [cos[:, columns], sin[:, columns]]
+
+    return np.stack([np.concatenate(part(i) + part(i + 2), axis=1) for i in range(2)])
+
+
+def band_table():
+    near = np.arange(CLASS)
+    apart = FOLD * (near[:, None] - near[None, :])
+    blocks = [np.abs(apart + shift) <= HW for shift in (0, -1, 1)]
+    return np.concatenate(blocks, axis=0).astype(ml_dtypes.bfloat16)
 
 
 def inverse_tables():
@@ -107,28 +103,29 @@
     return (place % G) * (LANES // G) + place // G
 
 
-def spectra_kernel(relative, with_meta, kept, skip, *refs):
+def spectra_kernel(relative, with_meta, kept, skip, alone, *refs):
     f32, bf16 = jnp.float32, jnp.bfloat16
     refs = list(refs)
     here_ref = refs.pop(0) if relative else None
-    x_any, mask_ref, owner_ref, bins_ref, source_ref = refs[:5]
-    x_refs, table_ref, x_came, arrived, u, v, a, b, early, others = refs[-10:]
-    out_refs = refs[5:-11] if relative else refs[5:-10]
-    head = refs[-11] if relative else out_refs[0]
+    x_any, mask_ref, owner_ref, bins_ref, source_ref, band_any = refs[:6]
+    x_refs, table_ref, band_ref, x_came, arrived, u, v, ab, early, others, windows = refs[-11:]
+    out_refs = refs[6:-12] if relative else refs[6:-11]
+    head = refs[-12] if relative else out_refs[0]
     rest = out_refs[-1] if kept < LANES else None
     step, steps = pl.program_id(0), pl.num_programs(0)
     first = step == 0
     rows = x_refs.shape[1]
-    slot = lax.rem(step, 2)
+    slot = 0 if alone else lax.rem(step, 2)
+    at_first = (lambda act: act()) if alone else pl.when(first)
     copies = [
-        pltpu.make_async_copy(source_ref.at[part], table_ref.at[part], arrived.at[part]) for part in range(FOLD)
-    ]
+        pltpu.make_async_copy(source_ref.at[part], table_ref.at[part], arrived.at[part]) for part in range(2)
+    ] + [pltpu.make_async_copy(band_any, band_ref, arrived.at[2])]
 
     def trace_copy(block, slot):
         at = pl.ds(pl.multiple_of(block * rows + skip, LANES), rows)
         return pltpu.make_async_copy(x_any.at[at], x_refs.at[slot], x_came.at[slot])
 
-    @pl.when(first)
+    @at_first
     def start():
         trace_copy(0, 0).start()
         for copy in copies:
@@ -145,43 +142,60 @@
 
     trace_copy(step, slot).wait()
 
-    @pl.when(step + 1 < steps)
-    def ahead():
-        trace_copy(step + 1, 1 - slot).start()
+    if not alone:
+
+        @pl.when(step + 1 < steps)
+        def ahead():
+            trace_copy(step + 1, 1 - slot).start()
+
+    @at_first
+    def table_waits():
+        for copy in copies:
+            copy.wait()
 
     x_ref = x_refs.at[slot]
     x = [x_ref[:, m * QUARTER:(m + 1) * QUARTER].astype(f32) for m in range(FOLD)]
     even, odd = x[0] + x[2], x[1] + x[3]
     u[:rows], u[rows:] = two_terms(even + odd)
     v[:rows], v[rows:] = two_terms(even - odd)
-    a[:rows], a[rows:] = two_terms(x[0] - x[2])
-    b[:rows], b[rows:] = two_terms(x[1] - x[3])
-
-    pl.when(first)(copies[0].wait)
+    ab[:rows], ab[rows:2 * rows] = two_terms(x[0] - x[2])
+    ab[2 * rows:3 * rows], ab[3 * rows:] = two_terms(x[1] - x[3])
+
     early[:, :2 * CLASS] = two_term_dot(u, table_ref[0, :, :2 * CLASS])
     early[:, 2 * CLASS:] = two_term_dot(v, table_ref[0, :, 2 * CLASS:])
-    pl.when(first)(copies[1].wait)
-    others[...] = two_term_dot(a, table_ref[1])
-    pl.when(first)(copies[2].wait)
-    others[...] += two_term_dot(b, table_ref[2])
-    pl.when(first)(copies[3].wait)
+    turned = jnp.dot(ab[...], table_ref[1], preferred_element_type=f32)
+    straight = turned[:rows] + turned[rows:2 * rows]
+    turned = turned[2 * rows:3 * rows] + turned[3 * rows:]
+    columns = [slice(i * CLASS, (i + 1) * CLASS) for i in range(4)]
+    others[:, columns[0]] = straight[:, columns[0]] + turned[:, columns[1]]
+    others[:, columns[1]] = straight[:, columns[1]] - turned[:, columns[0]]
+    others[:, columns[2]] = straight[:, columns[2]] - turned[:, columns[3]]
+    others[:, columns[3]] = straight[:, columns[3]] + turned[:, columns[2]]
 
     holders = [(early, 0), (others, 0), (early, 2 * CLASS), (others, 2 * CLASS)]
     power = []
     for ref, start in holders:
         real, imag = ref[:, start:start + CLASS], ref[:, start + CLASS:start + 2 * CLASS]
-        power.append((real * real + imag * imag).astype(bf16))
-    power = jnp.concatenate(power, axis=1)
-    lane = lax.broadcasted_iota(jnp.int32, (1, NB), 1)
-    bin_ = (lane % CLASS) * FOLD + lane // CLASS
-    within = jnp.minimum(bin_ + HW, NB - 1) - jnp.maximum(bin_ - HW, 0) + 1
-    mean = jnp.dot(power, table_ref[3], preferred_element_type=f32) * (1.0 / within.astype(f32))
-    weight = lax.rsqrt(mean + EPSILON)
+        power.append(real * real + imag * imag)
+    before = [jnp.zeros_like(power[0]), power[0], power[0] + power[1], power[0] + power[1] + power[2]]
+    after = [power[1] + power[2] + power[3], power[2] + power[3], power[3], jnp.zeros_like(power[0])]
+    for which in range(FOLD):
+        at = slice(which * rows, (which + 1) * rows)
+        windows[at, :CLASS] = power[which].astype(bf16)
+        windows[at, CLASS:2 * CLASS] = before[which].astype(bf16)
+        windows[at, 2 * CLASS:] = after[which].astype(bf16)
+    sums = jnp.dot(windows[...], band_ref[...], preferred_element_type=f32)
+    weight = []
+    for which in range(FOLD):
+        bin_ = lax.broadcasted_iota(jnp.int32, (1, CLASS), 1) * FOLD + which
+        within = jnp.minimum(bin_ + HW, NB - 1) - jnp.maximum(bin_ - HW, 0) + 1
+        mean = sums[which * rows:(which + 1) * rows] * (1.0 / within.astype(f32))
+        weight.append(lax.rsqrt(mean + EPSILON))
     spare = LANES - kept
     for piece in range(SLICES):
         ref, start = holders[piece // 2]
         start += (piece % 2) * LANES
-        scale = weight[:, piece * LANES:(piece + 1) * LANES]
+        scale = weight[piece // 2][:, (piece % 2) * LANES:(piece % 2 + 1) * LANES]
         real = (ref[:, start:start + LANES] * scale).astype(bf16)
         imag = (ref[:, CLASS + start:CLASS + start + LANES] * scale).astype(bf16)
         both = jnp.concatenate([real, imag], axis=1)
@@ -205,7 +219,7 @@
 
 def spectra(traces, mask, owners, bins, first_row, rows, block, kept, here=None, with_meta=False):
     relative = here is not None
-    table = jnp.asarray(forward_tables()).reshape(FOLD, QUARTER, NB)
+    table, band = jnp.asarray(forward_tables()), jnp.asarray(band_table())
     whole = lambda array: pl.BlockSpec(array.shape, lambda i, *_: (0, 0))
     in_place = pl.BlockSpec(memory_space=pl.ANY)
     f32, bf16 = jnp.float32, jnp.bfloat16
@@ -213,10 +227,13 @@
     scratch = [
         pltpu.VMEM((2, block, NT), bf16),
         pltpu.VMEM(table.shape, bf16),
+        pltpu.VMEM(band.shape, bf16),
         pltpu.SemaphoreType.DMA((2,)),
-        pltpu.SemaphoreType.DMA((FOLD,)),
+        pltpu.SemaphoreType.DMA((3,)),
     ]
-    scratch += [pltpu.VMEM((2 * block, QUARTER), bf16)] * 4 + [pltpu.VMEM((block, 4 * CLASS), f32)] * 2
+    scratch += [pltpu.VMEM((terms * block, QUARTER), bf16) for terms in (2, 2, 4)]
+    scratch += [pltpu.VMEM((block, 4 * CLASS), f32)] * 2
+    scratch += [pltpu.VMEM((FOLD * block, 3 * CLASS), bf16)]
     if relative:
         scratch = [pltpu.VMEM((SLICES, segs * kept, 2 * LANES), bf16)] + scratch
         out_specs = [pl.BlockSpec((segs * kept, 2 * LANES), lambda i, *_: (i, 0))] * SLICES
@@ -230,11 +247,11 @@
         out_specs += [pl.BlockSpec((SLICES, segs * spare, 2 * LANES), lambda i, *_: (0, i, 0))]
         out_shape += [jax.ShapeDtypeStruct((SLICES, rows // LANES * spare, 2 * LANES), bf16)]
     return pl.pallas_call(
-        functools.partial(spectra_kernel, relative, with_meta, kept, first_row),
+        functools.partial(spectra_kernel, relative, with_meta, kept, first_row, rows == block),
         grid_spec=pltpu.PrefetchScalarGridSpec(
             num_scalar_prefetch=1 if relative else 0,
             grid=(rows // block,),
-            in_specs=[in_place, whole(mask), whole(owners), whole(bins), in_place],
+            in_specs=[in_place, whole(mask), whole(owners), whole(bins), in_place, in_place],
             out_specs=out_specs,
             scratch_shapes=scratch,
         ),
@@ -244,7 +261,7 @@
             flops=14 * rows * NB * NB, bytes_accessed=rows * NT * 3 + 8 * NB * NB, transcendentals=rows * NB
         ),
         name="spectra",
-    )(*([here] if relative else []), traces, mask, owners, bins, table)
+    )(*([here] if relative else []), traces, mask, owners, bins, table, band)
 
 
 def pair_sums(block_refs, pairs, steps, tiles):
@@ -355,17 +372,11 @@
         ready=len(ready), heads=len(heads), slots=slots, before=before is not None, hand_on=hand_on,
         stacked=stacked, rest_row=rest_row, pairs=pairs, steps=steps,
     )
-    whole = lambda array: pl.BlockSpec(array.shape, lambda i, *_: (0,) * len(array.shape))
     result = pl.pallas_call(
         functools.partial(cross_kernel, plan),
-        grid_spec=pltpu.PrefetchScalarGridSpec(
-            num_scalar_prefetch=1,
-            grid=(1,),
-            in_specs=[whole(array) for array in inputs],
-            out_specs=[whole(array) for array in out_shape],
-            scratch_shapes=scratch,
-        ),
+        in_specs=[pl.BlockSpec(memory_space=pltpu.SMEM)] + [pl.BlockSpec(memory_space=pltpu.VMEM)] * len(inputs),
         out_shape=out_shape,
+        scratch_shapes=scratch,
         compiler_params=pltpu.CompilerParams(vmem_limit_bytes=VMEM if stacked and copies else VMEM_SMALL),
         cost_estimate=pl.CostEstimate(
             flops=8 * G * steps * LANES * len(pairs), bytes_accessed=4 * G * steps * LANES * len(pairs), transcendentals=0

time: 125 us -> 117 us (0.936)
  Pallas kernels: 48.6 us -> 42.2 us
  waiting for transfers between devices: 35.3 us -> 38.8 us
  local copies, waits for them, and re-layouts: 3.6 us -> 0.87 us
    pallas_call x2, Pallas kernels: 35 us -> 29.1 us  [spectra(): pl.pallas_call(functools.partial(spectra_kernel, relative, with_meta, kep...]
    ppermute x7, waiting for transfers between devices: 35.3 us -> 38.8 us  [sent_along(): lax.ppermute(second[shift], 'chan', [(i, (i + shift) % count) for i in ra...]
    unnamed x18 -> x16, local copies, waits for them, and re-layouts: 2.76 us -> 0.05 us
  transfers between devices with their start and end apart: 8 -> 8, of which waited for: 4 -> 4; matrix products, arithmetic and copies ran while one was open for 1% -> 1% of each run, Pallas kernels for 26% -> 24%
where the time goes in v7:
time: 117 us
  Pallas kernels  42.2 us (36%)
  waiting for transfers between devices  38.8 us (33%)
  starting transfers between devices  18.8 us (16%)
  blocking collectives  15.1 us (13%)
    ppermute x7, waiting for transfers between devices, sent_along(): lax.ppermute(second[shift], 'chan', [(i, (i + shift) % count) for i in ra...  38.8 us
    pallas_call x2, Pallas kernels, spectra(): pl.pallas_call(functools.partial(spectra_kernel, relative, with_meta, kep...  29.1 us
    all_to_all x1, blocking collectives, per_device(): lax.all_to_all(stacks, ('seg', 'chan'), split_axis=0, concat_axis=0, tile...  15.1 us
    ppermute x7, starting transfers between devices, sent_along(): lax.ppermute(second[shift], 'chan', [(i, (i + shift) % count) for i in ra...  11.5 us
    pallas_call x3, Pallas kernels, cross(): pl.pallas_call(functools.partial(cross_kernel, plan), in_specs=[pl.BlockS...  11 us
    all_to_all x1, starting transfers between devices, sent_along(): lax.all_to_all(first, 'chan', split_axis=0, concat_axis=0, tiled=True)  7.28 us
  transfers between devices with their start and end apart: 8, of which 4 were waited for; matrix products, arithmetic and copies ran while one was open for 1% of the time, Pallas kernels for 24%

profile of v7, /device:TPU:0, one launch (start us, length us, event | category | flops | bytes accessed | tf_op | source)
XLA Modules:
  0.0 117.1 jit_solution(9553837675130384941)
XLA Ops:
  0.0 9.4 %spectra.3 = (bf16[8,240,256]{2,1,0:T(8,128)(2,1)}, bf16[8,32,256]{2,1,0:T(8,128)(2,1)S(1)}) custom-call(bf16[1024,4096]{1,0:T(8,128)(2,1)} %bitcast.6, s32[1,128]{1,0:T(1,128)} %bitcast.8, s32[1,64]{1,0:T(1,128)} %bitcast.10, s32[1,64]{1,0:T(1,128)} %refs_3_.1, bf16[2,1024,1024]{2,1,0:T(8,128)(2,1)} %constant.28.clone.refs_5_.refs_4_, ...), custom_call_target="tpu_custom_call" | custom-call | flops 3758096384 | bytes 11534336 | tf_op jit(solution)/shard_map/spectra/pallas_call | solution.py:249
  9.4 7.3 %all-to-all-start.1 = ((bf16[8,240,256]{2,1,0:T(8,128)(2,1)}), bf16[8,240,256]{2,1,0:T(8,128)(2,1)S(1)}, u32[]{:S(2)}, u32[]{:S(2)}) async-start(bf16[8,240,256]{2,1,0:T(8,128)(2,1)} %get-tuple-element.42), calls=%async_computation.1 | async-start | bytes 1966080 | tf_op jit(solution)/shard_map/all_to_all | solution.py:496
  16.7 19.7 %spectra.2 = (bf16[672,256]{1,0:T(8,128)(2,1)}, bf16[672,256]{1,0:T(8,128)(2,1)}, bf16[672,256]{1,0:T(8,128)(2,1)}, bf16[672,256]{1,0:T(8,128)(2,1)}, bf16[672,2...) custom-call(s32[1]{0:T(128)} %bitcast.refs_0_.here_ref, ...), custom_call_target="tpu_custom_call" | custom-call | flops 11274289152 | bytes 17825792 | tf_op jit(solution)/shard_map/spectra/pallas_call | solution.py:249
  36.4 2.0 %collective-permute-start = (bf16[672,256]{1,0:T(8,128)(2,1)}, bf16[672,256]{1,0:T(8,128)(2,1)S(1)}, u32[]{:S(2)}, u32[]{:S(2)}) collective-permute-start(bf16[672,256]{1,0:T(8,128)(2,1)} %get-tuple-element.37), channel_id=1, source_target_pairs={{0,1},{1,2},{2,3},{3,4},{4,5},{5,6},{6,7},{7,0},{8,9},{9,10},{10,1... | collective-permute-start | bytes 1032200 | tf_op jit(solution)/shard_map/ppermute | solution.py:502
  38.4 2.8 %collective-permute-start.1 = (bf16[672,256]{1,0:T(8,128)(2,1)}, bf16[672,256]{1,0:T(8,128)(2,1)S(1)}, u32[]{:S(2)}, u32[]{:S(2)}) collective-permute-start(bf16[672,256]{1,0:T(8,128)(2,1)} %get-tuple-element.38), channel_id=1, source_target_pairs={{0,7},{1,0},{2,1},{3,2},{4,3},{5,4},{6,5},{7,6},{8,15},{9,8},{10,9... | collective-permute-start | bytes 1032200 | tf_op jit(solution)/shard_map/ppermute | solution.py:502
  41.2 1.1 collective-permute-start.2
  42.3 1.5 %collective-permute-start.3 = (bf16[672,256]{1,0:T(8,128)(2,1)}, bf16[672,256]{1,0:T(8,128)(2,1)S(1)}, u32[]{:S(2)}, u32[]{:S(2)}) collective-permute-start(bf16[672,256]{1,0:T(8,128)(2,1)} %get-tuple-element.40), channel_id=1, source_target_pairs={{0,3},{1,4},{2,5},{3,6},{4,7},{5,0},{6,1},{7,2},{8,11},{9,12},{10,... | collective-permute-start | bytes 1032200 | tf_op jit(solution)/shard_map/ppermute | solution.py:502
  43.7 2.4 %collective-permute-start.4 = (bf16[672,256]{1,0:T(8,128)(2,1)}, bf16[672,256]{1,0:T(8,128)(2,1)S(1)}, u32[]{:S(2)}, u32[]{:S(2)}) collective-permute-start(bf16[672,256]{1,0:T(8,128)(2,1)} %get-tuple-element.41), channel_id=1, source_target_pairs={{0,5},{1,6},{2,7},{3,0},{4,1},{5,2},{6,3},{7,4},{8,13},{9,14},{10,... | collective-permute-start | bytes 1032200 | tf_op jit(solution)/shard_map/ppermute | solution.py:502
  46.1 7.2 %collective-permute-done.refs_1_ = bf16[672,256]{1,0:T(8,128)(2,1)S(1)} collective-permute-done((bf16[672,256]{1,0:T(8,128)(2,1)}, bf16[672,256]{1,0:T(8,128)(2,1)S(1)}, u32[]{:S(2)}, u32[]{:S(2)}) %collective-permute-start) | collective-permute-done | bytes 344096 | tf_op jit(solution)/shard_map/ppermute | solution.py:502
  53.3 0.6 collective-permute-start.5
  53.9 8.5 %collective-permute-done.1.refs_2_ = bf16[672,256]{1,0:T(8,128)(2,1)S(1)} collective-permute-done((bf16[672,256]{1,0:T(8,128)(2,1)}, bf16[672,256]{1,0:T(8,128)(2,1)S(1)}, u32[]{:S(2)}, u32[]{:S(2)}) %collective-permute-start.1) | collective-permute-done | bytes 344096 | tf_op jit(solution)/shard_map/ppermute | solution.py:502
  62.4 1.2 %collective-permute-start.6 = (bf16[672,256]{1,0:T(8,128)(2,1)}, bf16[672,256]{1,0:T(8,128)(2,1)}, u32[]{:S(2)}, u32[]{:S(2)}) collective-permute-start(bf16[672,256]{1,0:T(8,128)(2,1)} %get-tuple-element.55), channel_id=1, source_target_pairs={{0,6},{1,7},{2,0},{3,1},{4,2},{5,3},{6,4},{7,5},{8,14},{9,15},{10,... | collective-permute-start | bytes 1032200 | tf_op jit(solution)/shard_map/ppermute | solution.py:502
  63.6 0.1 fusion
  63.7 0.6 reduce_max.9
  64.8 0.8 conditional.1
  64.9 0.8 broadcast.2
  65.7 0.9 weights.1
  66.7 2.9 %cross.3.refs_9_ = f32[64,256]{1,0:T(8,128)S(1)} custom-call(s32[1]{0:T(128)} %bitcast.refs_0_.here_ref, bf16[8,240,256]{2,1,0:T(8,128)(2,1)S(1)} %all-to-all-done.1.meta_ref.refs_0_, bf16[8,128,256]{2,1,0:T(8,128)(2,1)} %get-tuple-element.58.refs_1_.refs_6_.refs_8_, bf16[8,128,128]{2,1,0:T(8,128)(2,1)S(1)} %get-tuple-element.45.refs_2_.refs_7_.refs_9_, ...), custom_call_target="tpu_custom_call" | custom-call | flops 5767168 | bytes 2883584 | tf_op jit(solution)/shard_map/cross/pallas_call | solution.py:375
  69.6 18.8 %collective-permute-done.2.refs_3_ = bf16[672,256]{1,0:T(8,128)(2,1)S(1)} collective-permute-done((bf16[672,256]{1,0:T(8,128)(2,1)}, bf16[672,256]{1,0:T(8,128)(2,1)S(1)}, u32[]{:S(2)}, u32[]{:S(2)}) %collective-permute-start.2) | collective-permute-done | bytes 344096 | tf_op jit(solution)/shard_map/ppermute | solution.py:502
  88.4 4.2 %cross.4 = (f32[64,256]{1,0:T(8,128)S(1)}, bf16[768,256]{1,0:T(8,128)(2,1)S(1)}, bf16[768,256]{1,0:T(8,128)(2,1)S(1)}, bf16[768,256]{1,0:T(8,128)(2,1)S(1)}, bf1...) custom-call(s32[1]{0:T(128)} %bitcast.refs_0_.here_ref, ...), custom_call_target="tpu_custom_call" | custom-call | flops 11796480 | bytes 5898240 | tf_op jit(solution)/shard_map/cross/pallas_call | solution.py:375
  92.7 4.3 %collective-permute-done.6.refs_7_ = bf16[672,256]{1,0:T(8,128)(2,1)} collective-permute-done((bf16[672,256]{1,0:T(8,128)(2,1)}, bf16[672,256]{1,0:T(8,128)(2,1)}, u32[]{:S(2)}, u32[]{:S(2)}) %collective-permute-start.6) | collective-permute-done | bytes 344096 | tf_op jit(solution)/shard_map/ppermute | solution.py:502
  97.0 3.9 %cross.5 = bf16[4,64,256]{2,1,0:T(8,128)(2,1)S(1)} custom-call(s32[1]{0:T(128)} %bitcast.refs_0_.here_ref, bf16[768,256]{1,0:T(8,128)(2,1)S(1)} %get-tuple-element.48.refs_0_, bf16[768,256]{1,0:T(8,128)(2,1)S(1)} %get-tuple-element.49.refs_1_, bf16[768,256]{1,0:T(8,128)(2,1)S(1)} %get-tuple-element.50.refs_2_, ...), custom_call_target="tpu_custom_call" | custom-call | flops 10223616 | bytes 5111808 | tf_op jit(solution)/shard_map/cross/pallas_call | solution.py:375
  100.9 15.1 %all_to_all.15.stacks_ref = bf16[32,8,256]{2,1,0:T(8,128)(2,1)S(1)} all-to-all(bf16[32,8,256]{2,1,0:T(8,128)(2,1)S(1)} %bitcast.5), channel_id=1, replica_groups=mesh['seg'=4,'chan'=8] {'seg','chan'}, dimensions={0} | all-to-all | bytes 262144 | tf_op jit(solution)/shard_map/all_to_all | solution.py:574
  115.9 1.2 lags.1
  (20 shorter events, 0.1 us)
Async XLA Ops:
  9.4 54.2 %all-to-all-start.1 = ((bf16[8,240,256]{2,1,0:T(8,128)(2,1)}), bf16[8,240,256]{2,1,0:T(8,128)(2,1)S(1)}, u32[]{:S(2)}, u32[]{:S(2)}) async-start(bf16[8,240,256]{2,1,0:T(8,128)(2,1)} %get-tuple-element.42), calls=%async_computation.1 | async-start | bytes 1966080 | tf_op jit(solution)/shard_map/all_to_all | solution.py:496
  16.7 49.0 %copy-start.4 = (s32[2,352]{1,0:T(2,128)S(1)}, s32[2,352]{1,0:T(2,128)}, u32[]{:S(2)}) copy-start(s32[2,352]{1,0:T(2,128)} %constant.30.clone.refs_0_) | copy-start | bytes 8452
  16.7 49.0 %copy-start.5 = (s32[2,208]{1,0:T(2,128)S(1)}, s32[2,208]{1,0:T(2,128)}, u32[]{:S(2)}) copy-start(s32[2,208]{1,0:T(2,128)} %constant.32.clone.refs_2_) | copy-start | bytes 4996
  16.7 49.0 %copy-start.6 = (s32[2,240]{1,0:T(2,128)S(1)}, s32[2,240]{1,0:T(2,128)}, u32[]{:S(2)}) copy-start(s32[2,240]{1,0:T(2,128)} %constant.31.clone.refs_1_) | copy-start | bytes 5764
  36.4 52.0 %copy-start.3 = (bf16[672,256]{1,0:T(8,128)(2,1)S(1)}, bf16[672,256]{1,0:T(8,128)(2,1)}, u32[]{:S(2)}) copy-start(bf16[672,256]{1,0:T(8,128)(2,1)} %get-tuple-element.36.refs_0_) | copy-start | bytes 1032196
  36.4 16.9 %collective-permute-start = (bf16[672,256]{1,0:T(8,128)(2,1)}, bf16[672,256]{1,0:T(8,128)(2,1)S(1)}, u32[]{:S(2)}, u32[]{:S(2)}) collective-permute-start(bf16[672,256]{1,0:T(8,128)(2,1)} %get-tuple-element.37), channel_id=1, source_target_pairs={{0,1},{1,2},{2,3},{3,4},{4,5},{5,6},{6,7},{7,0},{8,9},{9,10},{10,1... | collective-permute-start | bytes 1032200 | tf_op jit(solution)/shard_map/ppermute | solution.py:502
  38.4 23.9 %collective-permute-start.1 = (bf16[672,256]{1,0:T(8,128)(2,1)}, bf16[672,256]{1,0:T(8,128)(2,1)S(1)}, u32[]{:S(2)}, u32[]{:S(2)}) collective-permute-start(bf16[672,256]{1,0:T(8,128)(2,1)} %get-tuple-element.38), channel_id=1, source_target_pairs={{0,7},{1,0},{2,1},{3,2},{4,3},{5,4},{6,5},{7,6},{8,15},{9,8},{10,9... | collective-permute-start | bytes 1032200 | tf_op jit(solution)/shard_map/ppermute | solution.py:502
  41.2 47.2 %collective-permute-start.2 = (bf16[672,256]{1,0:T(8,128)(2,1)}, bf16[672,256]{1,0:T(8,128)(2,1)S(1)}, u32[]{:S(2)}, u32[]{:S(2)}) collective-permute-start(bf16[672,256]{1,0:T(8,128)(2,1)} %get-tuple-element.39), channel_id=1, source_target_pairs={{0,4},{1,5},{2,6},{3,7},{4,0},{5,1},{6,2},{7,3},{8,12},{9,13},{10,... | collective-permute-start | bytes 1032200 | tf_op jit(solution)/shard_map/ppermute | solution.py:502
  42.3 46.1 %collective-permute-start.3 = (bf16[672,256]{1,0:T(8,128)(2,1)}, bf16[672,256]{1,0:T(8,128)(2,1)S(1)}, u32[]{:S(2)}, u32[]{:S(2)}) collective-permute-start(bf16[672,256]{1,0:T(8,128)(2,1)} %get-tuple-element.40), channel_id=1, source_target_pairs={{0,3},{1,4},{2,5},{3,6},{4,7},{5,0},{6,1},{7,2},{8,11},{9,12},{10,... | collective-permute-start | bytes 1032200 | tf_op jit(solution)/shard_map/ppermute | solution.py:502
  43.7 44.7 %collective-permute-start.4 = (bf16[672,256]{1,0:T(8,128)(2,1)}, bf16[672,256]{1,0:T(8,128)(2,1)S(1)}, u32[]{:S(2)}, u32[]{:S(2)}) collective-permute-start(bf16[672,256]{1,0:T(8,128)(2,1)} %get-tuple-element.41), channel_id=1, source_target_pairs={{0,5},{1,6},{2,7},{3,0},{4,1},{5,2},{6,3},{7,4},{8,13},{9,14},{10,... | collective-permute-start | bytes 1032200 | tf_op jit(solution)/shard_map/ppermute | solution.py:502
  53.3 39.4 %collective-permute-start.5 = (bf16[672,256]{1,0:T(8,128)(2,1)}, bf16[672,256]{1,0:T(8,128)(2,1)S(1)}, u32[]{:S(2)}, u32[]{:S(2)}) collective-permute-start(bf16[672,256]{1,0:T(8,128)(2,1)} %get-tuple-element.54), channel_id=1, source_target_pairs={{0,2},{1,3},{2,4},{3,5},{4,6},{5,7},{6,0},{7,1},{8,10},{9,11},{10,... | collective-permute-start | bytes 1032200 | tf_op jit(solution)/shard_map/ppermute | solution.py:502
  62.4 34.6 %collective-permute-start.6 = (bf16[672,256]{1,0:T(8,128)(2,1)}, bf16[672,256]{1,0:T(8,128)(2,1)}, u32[]{:S(2)}, u32[]{:S(2)}) collective-permute-start(bf16[672,256]{1,0:T(8,128)(2,1)} %get-tuple-element.55), channel_id=1, source_target_pairs={{0,6},{1,7},{2,0},{3,1},{4,2},{5,3},{6,4},{7,5},{8,14},{9,15},{10,... | collective-permute-start | bytes 1032200 | tf_op jit(solution)/shard_map/ppermute | solution.py:502
  65.7 31.3 %copy-start.7 = (bf16[8,128,256]{2,1,0:T(8,128)(2,1)S(1)}, bf16[8,128,256]{2,1,0:T(8,128)(2,1)}, u32[]{:S(2)}) copy-start(bf16[8,128,256]{2,1,0:T(8,128)(2,1)} %get-tuple-element.58.refs_1_.refs_6_.refs_8_) | copy-start | bytes 1572868
  66.7 49.3 %copy-start = (bf16[1024,1024]{1,0:T(8,128)(2,1)S(1)}, bf16[1024,1024]{1,0:T(8,128)(2,1)}, u32[]{:S(2)}) copy-start(bf16[1024,1024]{1,0:T(8,128)(2,1)} %constant.35.clone.odd_ref) | copy-start | bytes 6291460
  66.7 49.3 %copy-start.1 = (bf16[512,512]{1,0:T(8,128)(2,1)S(1)}, bf16[512,512]{1,0:T(8,128)(2,1)}, u32[]{:S(2)}) copy-start(bf16[512,512]{1,0:T(8,128)(2,1)} %constant.34.clone.two_ref) | copy-start | bytes 1572868
  66.7 49.3 %copy-start.2 = (bf16[512,512]{1,0:T(8,128)(2,1)S(1)}, bf16[512,512]{1,0:T(8,128)(2,1)}, u32[]{:S(2)}) copy-start(bf16[512,512]{1,0:T(8,128)(2,1)} %constant.33.clone.zero_ref) | copy-start | bytes 1572868

commit v8 on v7

--- a/solution.py
+++ b/solution.py
@@ -30,11 +30,12 @@
 VMEM = 58 * 1024 * 1024
 VMEM_SMALL = 20 * 1024 * 1024
 META = 16
-KEPT = 112
+PAIR = 2 * LANES
+TIERS = (104, 8, 16)
+KEPT = 2 * TIERS[0]
 EARLY_SEGS = 2
-LATE_SEGS_A_BLOCK = 2
-
-SENT = (1, 7, 4, 3, 5, 2, 6)
+
+SENT = (4, 1, 7, 3, 5, 2, 6)
 STAGES = (6, 8)
 
 
@@ -98,9 +99,25 @@
     return jnp.where(mask_row > 0, count[0:1] - 1.0, -1.0)
 
 
-def channel_of_place(shape, axis):
-    place = lax.broadcasted_iota(jnp.int32, shape, axis)
-    return (place % G) * (LANES // G) + place // G
+def sorted_rows(mask_row):
+    rank = ranks(mask_row)
+    rows = []
+    for seg in range(2):
+        row, below, done = jnp.full_like(rank, -1.0), 0, 0
+        for tier in TIERS:
+            inside = (rank >= below) & (rank < below + tier)
+            row = jnp.where(inside, rank - below + done + seg * tier, row)
+            below, done = below + tier, done + 2 * tier
+        rows.append(row)
+    rows = jnp.concatenate(rows, axis=1)
+    return rows == lax.broadcasted_iota(jnp.int32, (PAIR, PAIR), 0).astype(jnp.float32)
+
+
+def place_order():
+    place = lax.broadcasted_iota(jnp.int32, (PAIR, PAIR), 0)
+    row = lax.broadcasted_iota(jnp.int32, (PAIR, PAIR), 1)
+    inside = place % LANES
+    return (place // LANES) * LANES + (inside % G) * (LANES // G) + inside // G == row
 
 
 def spectra_kernel(relative, with_meta, kept, skip, alone, *refs):
@@ -111,7 +128,7 @@
     x_refs, table_ref, band_ref, x_came, arrived, u, v, ab, early, others, windows = refs[-11:]
     out_refs = refs[6:-12] if relative else refs[6:-11]
     head = refs[-12] if relative else out_refs[0]
-    rest = out_refs[-1] if kept < LANES else None
+    spares = out_refs[1 - len(TIERS):] if kept < PAIR else []
     step, steps = pl.program_id(0), pl.num_programs(0)
     first = step == 0
     rows = x_refs.shape[1]
@@ -132,12 +149,10 @@
             copy.start()
 
     mask = mask_ref[...].astype(f32)
-    shape = (LANES, LANES)
-    if kept < LANES:
-        chosen = ranks(mask) == lax.broadcasted_iota(jnp.int32, shape, 0).astype(f32)
+    if kept < PAIR:
+        chosen = sorted_rows(mask)
     else:
-        chosen = channel_of_place(shape, 0) == lax.broadcasted_iota(jnp.int32, shape, 1)
-        chosen = chosen & (jnp.broadcast_to(mask, shape) > 0)
+        chosen = place_order() & (jnp.concatenate([mask, mask], axis=1) > 0)
     chosen = chosen.astype(f32).astype(bf16)
 
     trace_copy(step, slot).wait()
@@ -191,24 +206,25 @@
         within = jnp.minimum(bin_ + HW, NB - 1) - jnp.maximum(bin_ - HW, 0) + 1
         mean = sums[which * rows:(which + 1) * rows] * (1.0 / within.astype(f32))
         weight.append(lax.rsqrt(mean + EPSILON))
-    spare = LANES - kept
     for piece in range(SLICES):
-        ref, start = holders[piece // 2]
-        start += (piece % 2) * LANES
+        ref, column = holders[piece // 2]
+        column += (piece % 2) * LANES
         scale = weight[piece // 2][:, (piece % 2) * LANES:(piece % 2 + 1) * LANES]
-        real = (ref[:, start:start + LANES] * scale).astype(bf16)
-        imag = (ref[:, CLASS + start:CLASS + start + LANES] * scale).astype(bf16)
+        real = (ref[:, column:column + LANES] * scale).astype(bf16)
+        imag = (ref[:, CLASS + column:CLASS + column + LANES] * scale).astype(bf16)
         both = jnp.concatenate([real, imag], axis=1)
-        for seg in range(rows // LANES):
-            sorted_ = jnp.dot(chosen, both[seg * LANES:(seg + 1) * LANES], preferred_element_type=f32).astype(bf16)
-            head[piece, seg * kept:(seg + 1) * kept, :] = sorted_[:kept]
-            if spare:
-                rest[piece, seg * spare:(seg + 1) * spare, :] = sorted_[kept:]
+        for pair in range(rows // PAIR):
+            sorted_ = jnp.dot(chosen, both[pair * PAIR:(pair + 1) * PAIR], preferred_element_type=f32).astype(bf16)
+            head[piece, pair * kept:(pair + 1) * kept, :] = sorted_[:kept]
+            start = kept
+            for spare, tier in zip(spares, TIERS[1:]):
+                spare[piece, pair * 2 * tier:(pair + 1) * 2 * tier, :] = sorted_[start:start + 2 * tier]
+                start += 2 * tier
     if with_meta:
         tiles = owner_ref.shape[1]
         labels = (owner_ref[...] * BIN_DEV + bins_ref[...]).astype(f32)
         for piece in range(SLICES):
-            at = pl.ds(rows // LANES * kept, META)
+            at = pl.ds(rows // PAIR * kept, META)
             head[piece, at, :] = jnp.zeros((META, 2 * LANES), bf16)
             head[piece, at, :LANES] = jnp.broadcast_to(mask, (META, LANES)).astype(bf16)
             head[piece, at, LANES:LANES + tiles] = jnp.broadcast_to(labels, (META, tiles)).astype(bf16)
@@ -223,7 +239,7 @@
     whole = lambda array: pl.BlockSpec(array.shape, lambda i, *_: (0, 0))
     in_place = pl.BlockSpec(memory_space=pl.ANY)
     f32, bf16 = jnp.float32, jnp.bfloat16
-    segs = block // LANES
+    pairs = block // PAIR
     scratch = [
         pltpu.VMEM((2, block, NT), bf16),
         pltpu.VMEM(table.shape, bf16),
@@ -235,17 +251,16 @@
     scratch += [pltpu.VMEM((block, 4 * CLASS), f32)] * 2
     scratch += [pltpu.VMEM((FOLD * block, 3 * CLASS), bf16)]
     if relative:
-        scratch = [pltpu.VMEM((SLICES, segs * kept, 2 * LANES), bf16)] + scratch
-        out_specs = [pl.BlockSpec((segs * kept, 2 * LANES), lambda i, *_: (i, 0))] * SLICES
-        out_shape = [jax.ShapeDtypeStruct((rows // LANES * kept, 2 * LANES), bf16)] * SLICES
+        scratch = [pltpu.VMEM((SLICES, pairs * kept, 2 * LANES), bf16)] + scratch
+        out_specs = [pl.BlockSpec((pairs * kept, 2 * LANES), lambda i, *_: (i, 0))] * SLICES
+        out_shape = [jax.ShapeDtypeStruct((rows // PAIR * kept, 2 * LANES), bf16)] * SLICES
     else:
         extra = META if with_meta else 0
-        out_specs = [pl.BlockSpec((SLICES, segs * kept + extra, 2 * LANES), lambda i, *_: (0, i, 0))]
-        out_shape = [jax.ShapeDtypeStruct((SLICES, rows // LANES * kept + extra, 2 * LANES), bf16)]
-    if kept < LANES:
-        spare = LANES - kept
-        out_specs += [pl.BlockSpec((SLICES, segs * spare, 2 * LANES), lambda i, *_: (0, i, 0))]
-        out_shape += [jax.ShapeDtypeStruct((SLICES, rows // LANES * spare, 2 * LANES), bf16)]
+        out_specs = [pl.BlockSpec((SLICES, pairs * kept + extra, 2 * LANES), lambda i, *_: (0, i, 0))]
+        out_shape = [jax.ShapeDtypeStruct((SLICES, rows // PAIR * kept + extra, 2 * LANES), bf16)]
+    for tier in TIERS[1:] if kept < PAIR else ():
+        out_specs.append(pl.BlockSpec((SLICES, pairs * 2 * tier, 2 * LANES), lambda i, *_: (0, i, 0)))
+        out_shape.append(jax.ShapeDtypeStruct((SLICES, rows // LANES * tier, 2 * LANES), bf16))
     return pl.pallas_call(
         functools.partial(spectra_kernel, relative, with_meta, kept, first_row, rows == block),
         grid_spec=pltpu.PrefetchScalarGridSpec(
@@ -297,13 +312,14 @@
             done += G
 
 
-def place_rows(head_ref, rest_ref, rest_row, places, out_ref):
-    spare = LANES - KEPT
-    for seg in range(out_ref.shape[0] // LANES):
-        at = rest_row + seg * spare
-        rows = jnp.concatenate([head_ref[seg * KEPT:(seg + 1) * KEPT], rest_ref[at:at + spare]], axis=0)
-        placed = jnp.dot(places, rows, preferred_element_type=jnp.float32)
-        out_ref[seg * LANES:(seg + 1) * LANES, :] = placed.astype(out_ref.dtype)
+def place_rows(head_ref, spare_refs, first_pair, places, out_ref):
+    for pair in range(out_ref.shape[0] // PAIR):
+        rows = [head_ref[pair * KEPT:(pair + 1) * KEPT]]
+        for spare_ref, tier in zip(spare_refs, TIERS[1:]):
+            at = (first_pair + pair) * 2 * tier
+            rows.append(spare_ref[at:at + 2 * tier])
+        placed = jnp.dot(places, jnp.concatenate(rows, axis=0), preferred_element_type=jnp.float32)
+        out_ref[pair * PAIR:(pair + 1) * PAIR, :] = placed.astype(out_ref.dtype)
 
 
 def cross_kernel(plan, here_ref, *refs):
@@ -311,7 +327,7 @@
     refs = list(refs)
     take = lambda count: [refs.pop(0) for _ in range(count)]
     ready, heads = take(plan["ready"]), take(plan["heads"])
-    rest_ref, places_ref = take(2) if heads else (None, None)
+    *spare_refs, places_ref = take(len(TIERS)) if heads else [None]
     (rows_ref,) = take(1)
     before_ref = refs.pop(0) if plan["before"] else None
     out_ref = refs.pop(0)
@@ -328,7 +344,8 @@
             placed = [room.at[i] for i in range(len(heads))]
         for i, head in enumerate(heads):
             block = i if plan["stacked"] else lax.rem(here_ref[0] - plan["slots"][i] + SLICES, SLICES)
-            place_rows(head, rest_ref.at[block], plan["rest_row"], places_ref[block], placed[i])
+            spares = [spare_ref.at[block] for spare_ref in spare_refs]
+            place_rows(head, spares, plan["first_pair"], places_ref[block], placed[i])
         ready = ready + placed
     pair_sums(ready, plan["pairs"], plan["steps"], tiles)
     bins, count = out_ref.shape[-2], tiles.shape[0]
@@ -352,10 +369,10 @@
             out_ref[copy] = stacked.astype(out_ref.dtype)
 
 
-def cross(here, pairs, steps, bins, weights, ready=(), heads=(), slots=(), rest=None, rest_row=0, places=None,
+def cross(here, pairs, steps, bins, weights, ready=(), heads=(), slots=(), spares=(), first_pair=0, places=None,
           before=None, copies=None, hand_on=False, stacked=False):
     shape = (bins, 2 * LANES)
-    inputs = list(ready) + list(heads) + ([rest, places] if heads else []) + [weights]
+    inputs = list(ready) + list(heads) + (list(spares) + [places] if heads else []) + [weights]
     if before is not None:
         inputs.append(before)
     if copies is None:
@@ -370,7 +387,7 @@
         scratch.append(pltpu.VMEM((count, G * steps, 2 * LANES), jnp.bfloat16))
     plan = dict(
         ready=len(ready), heads=len(heads), slots=slots, before=before is not None, hand_on=hand_on,
-        stacked=stacked, rest_row=rest_row, pairs=pairs, steps=steps,
+        stacked=stacked, first_pair=first_pair, pairs=pairs, steps=steps,
     )
     result = pl.pallas_call(
         functools.partial(cross_kernel, plan),
@@ -394,13 +411,10 @@
     padded = jnp.concatenate([masks.astype(f32), empty.astype(f32)], axis=0)
     half = len(refs) // 2
     places_ref = refs[-1]
-    shape = (LANES, LANES)
-    channel = lax.broadcasted_iota(jnp.int32, shape, 1)
-    of_place = (channel_of_place(shape, 0) == channel).astype(f32).astype(bf16)
+    in_place = place_order().astype(f32).astype(bf16)
     for b in range(blocks):
-        rank = ranks(masks[b:b + 1].astype(f32))
-        sorted_ = (rank == lax.broadcasted_iota(jnp.int32, shape, 0).astype(f32)).astype(f32).astype(bf16)
-        places = lax.dot_general(of_place, sorted_, (((1,), (1,)), ((), ())), preferred_element_type=f32)
+        rows = sorted_rows(masks[b:b + 1].astype(f32)).astype(f32).astype(bf16)
+        places = lax.dot_general(in_place, rows, (((1,), (1,)), ((), ())), preferred_element_type=f32)
         places_ref[b] = places.astype(bf16)
     for ends_ref, out_ref in zip(refs[:half], refs[half:-1]):
         lanes = out_ref.shape[1]
@@ -438,10 +452,10 @@
             in_specs=[pl.BlockSpec((blocks, META, 2 * LANES), lambda i, *_: (0, at // META, 0))]
             + [whole(end.shape) for end in ends],
             out_specs=[whole(shape) for shape in shapes]
-            + [pl.BlockSpec((blocks, LANES, LANES), lambda i, *_: (0, 0, 0))],
+            + [pl.BlockSpec((blocks, PAIR, PAIR), lambda i, *_: (0, 0, 0))],
         ),
         out_shape=[jax.ShapeDtypeStruct(shape, jnp.float32) for shape in shapes]
-        + [jax.ShapeDtypeStruct((blocks, LANES, LANES), jnp.bfloat16)],
+        + [jax.ShapeDtypeStruct((blocks, PAIR, PAIR), jnp.bfloat16)],
         compiler_params=pltpu.CompilerParams(vmem_limit_bytes=VMEM_SMALL),
         name="weights",
     )(here, meta, *ends)
@@ -490,25 +504,26 @@
     count = lax.axis_size("chan")
     early = EARLY_SEGS * LANES
     late = x.shape[0] - early
-    spare = LANES - KEPT
     here = lax.axis_index("chan").astype(jnp.int32).reshape(1)
-    first, spare_early = spectra(x, mask, owners, bins, 0, early, early, KEPT, with_meta=True)
+    first, *spare_early = spectra(x, mask, owners, bins, 0, early, early, KEPT, with_meta=True)
     first = lax.all_to_all(first, "chan", split_axis=0, concat_axis=0, tiled=True)
-    *second, spare_late = spectra(
-        x, mask, owners, bins, early, late, LATE_SEGS_A_BLOCK * LANES, KEPT, here=here
-    )
+    second = spectra(x, mask, owners, bins, early, late, PAIR, KEPT, here=here)
+    spare_late = second[SLICES:]
     slots = {0: second[0]}
     for shift in SENT:
         slots[shift] = lax.ppermute(second[shift], "chan", [(i, (i + shift) % count) for i in range(count)])
 
-    at = EARLY_SEGS * KEPT
+    at = early // PAIR * KEPT
     most = jnp.max(jnp.sum(first[:, at, :LANES].astype(jnp.float32), axis=1))
-    rest = lax.cond(
-        most > KEPT,
-        lambda rows: lax.all_to_all(jnp.concatenate(rows, axis=1), "chan", split_axis=0, concat_axis=0, tiled=True),
-        lambda rows: jnp.zeros((count, (early + late) // LANES * spare, 2 * LANES), jnp.bfloat16),
-        (spare_early, spare_late),
-    )
+    spares, below = [], TIERS[0]
+    for tier, *parts in zip(TIERS[1:], spare_early, spare_late):
+        spares.append(lax.cond(
+            most > below,
+            lambda parts: lax.all_to_all(jnp.concatenate(parts, axis=1), "chan", split_axis=0, concat_axis=0, tiled=True),
+            lambda parts: jnp.zeros((count, sum(part.shape[1] for part in parts), 2 * LANES), jnp.bfloat16),
+            parts,
+        ))
+        below += tier
 
     fixed = fixed_pairs(count)
     known = (0,) + SENT
@@ -520,7 +535,7 @@
     places = weights[-1]
     bins = count * BIN_DEV
     stacks = cross(
-        here, fixed, early // G, bins, weights[0], heads=[first], rest=rest, places=places, stacked=True
+        here, fixed, early // G, bins, weights[0], heads=[first], spares=spares, places=places, stacked=True
     )
     ready, start = [], 0
     for end, pairs, weight in zip(STAGES, stages, weights[1:]):
@@ -528,7 +543,7 @@
         result = cross(
             here, pairs, late // G, bins, weight,
             ready=ready, heads=[slots[slot] for slot in known[start:end]], slots=known[start:end],
-            rest=rest, rest_row=EARLY_SEGS * spare, places=places, before=stacks,
+            spares=spares, first_pair=early // PAIR, places=places, before=stacks,
             copies=seg_count if final else None, hand_on=not final,
         )
         if final:
@@ -549,7 +564,7 @@
     every = jnp.broadcast_to(every[:, None, :], (count, META, 2 * LANES))
     fixed = fixed_pairs(count)
     weights = pair_weights(here, every, 0, total_segs, [fixed])[:1]
-    (outgoing,) = spectra(x, mask, owners, bins, 0, rows, 2 * LANES, LANES)
+    (outgoing,) = spectra(x, mask, owners, bins, 0, rows, PAIR, PAIR)
     outgoing = outgoing.reshape(SLICES, rows, 2, splits, narrow).transpose(0, 3, 1, 2, 4)
     outgoing = outgoing.reshape(count, rows, 2 * narrow)
     wide = lax.all_to_all(outgoing, "chan", split_axis=0, concat_axis=0, tiled=True)

time: 117 us -> 112 us (0.957)
  waiting for transfers between devices: 38.8 us -> 18.1 us
  starting transfers between devices: 18.8 us -> 28 us
  blocking collectives: 15.1 us -> 19.3 us
    ppermute x7, waiting for transfers between devices: 38.8 us -> 18.1 us  [sent_along(): lax.ppermute(second[shift], 'chan', [(i, (i + shift) % count) for i in ra...]
    ppermute x7, starting transfers between devices: 11.5 us -> 20.7 us  [sent_along(): lax.ppermute(second[shift], 'chan', [(i, (i + shift) % count) for i in ra...]
    all_to_all x1, blocking collectives: 15.1 us -> 19.3 us  [per_device(): lax.all_to_all(stacks, ('seg', 'chan'), split_axis=0, concat_axis=0, tile...]
  transfers between devices with their start and end apart: 8 -> 8, of which waited for: 4 -> 2; matrix products, arithmetic and copies ran while one was open for 1% -> 2% of each run, Pallas kernels for 24% -> 26%
where the time goes in v8:
time: 112 us; the launch traced here: 111 us
  Pallas kernels  42.1 us (38%)
  starting transfers between devices  28 us (25%)
  blocking collectives  19.3 us (17%)
  waiting for transfers between devices  18.1 us (16%)
  local copies, waits for them, and re-layouts  1.6 us (1%)
  between operations  1.41 us (1%)
    pallas_call x2, Pallas kernels, spectra(): pl.pallas_call(functools.partial(spectra_kernel, relative, with_meta, kep...  29.3 us
    ppermute x7, starting transfers between devices, sent_along(): lax.ppermute(second[shift], 'chan', [(i, (i + shift) % count) for i in ra...  20.7 us
    all_to_all x1, blocking collectives, per_device(): lax.all_to_all(stacks, ('seg', 'chan'), split_axis=0, concat_axis=0, tile...  19.3 us
    ppermute x7, waiting for transfers between devices, sent_along(): lax.ppermute(second[shift], 'chan', [(i, (i + shift) % count) for i in ra...  18.1 us
    pallas_call x3, Pallas kernels, cross(): pl.pallas_call(functools.partial(cross_kernel, plan), in_specs=[pl.BlockS...  10.3 us
    all_to_all x1, starting transfers between devices, sent_along(): lax.all_to_all(first, 'chan', split_axis=0, concat_axis=0, tiled=True)  7.3 us
  transfers between devices with their start and end apart: 8, of which 2 were waited for; matrix products, arithmetic and copies ran while one was open for 2% of the time, Pallas kernels for 26%

profile of v8, /device:TPU:0, one launch (start us, length us, event | category | flops | bytes accessed | tf_op | source)
XLA Modules:
  0.0 111.2 jit_solution(10108850337349733446)
XLA Ops:
  0.0 9.4 %spectra.3 = (bf16[8,224,256]{2,1,0:T(8,128)(2,1)}, bf16[8,16,256]{2,1,0:T(8,128)(2,1)S(1)}, bf16[8,32,256]{2,1,0:T(8,128)(2,1)}) custom-call(bf16[1024,4096]{1,0:T(8,128)(2,1)} %bitcast.6, s32[1,128]{1,0:T(1,128)} %bitcast.8, s32[1,64]{1,0:T(1,128)} %bitcast.10, s32[1,64]{1,0:T(1,128)} %refs_3_.1, bf16[2,1024,1024]{2,1,0:T(8,128)(2,1)} %constant.32.clone.refs_5_.refs_4_, ...), custom_call_target="tpu_custom_call" | custom-call | flops 3758096384 | bytes 11534336 | tf_op jit(solution)/shard_map/spectra/pallas_call | solution.py:264
  9.4 7.3 %all-to-all-start.2 = ((bf16[8,224,256]{2,1,0:T(8,128)(2,1)}), bf16[8,224,256]{2,1,0:T(8,128)(2,1)S(1)}, u32[]{:S(2)}, u32[]{:S(2)}) async-start(bf16[8,224,256]{2,1,0:T(8,128)(2,1)} %get-tuple-element.53), calls=%async_computation.2 | async-start | bytes 1835008 | tf_op jit(solution)/shard_map/all_to_all | solution.py:509
  16.8 0.0 copy-start.6
  16.8 19.8 %spectra.2 = (bf16[624,256]{1,0:T(8,128)(2,1)}, bf16[624,256]{1,0:T(8,128)(2,1)}, bf16[624,256]{1,0:T(8,128)(2,1)}, bf16[624,256]{1,0:T(8,128)(2,1)}, bf16[624,2...) custom-call(s32[1]{0:T(128)} %bitcast.refs_0_.here_ref, ...), custom_call_target="tpu_custom_call" | custom-call | flops 11274289152 | bytes 17825792 | tf_op jit(solution)/shard_map/spectra/pallas_call | solution.py:264
  36.6 3.0 %collective-permute-start = (bf16[624,256]{1,0:T(8,128)(2,1)}, bf16[624,256]{1,0:T(8,128)(2,1)S(1)}, u32[]{:S(2)}, u32[]{:S(2)}) collective-permute-start(bf16[624,256]{1,0:T(8,128)(2,1)} %get-tuple-element.48), channel_id=1, source_target_pairs={{0,4},{1,5},{2,6},{3,7},{4,0},{5,1},{6,2},{7,3},{8,12},{9,13},{10,... | collective-permute-start | bytes 958472 | tf_op jit(solution)/shard_map/ppermute | solution.py:514
  39.6 1.5 %collective-permute-start.1 = (bf16[624,256]{1,0:T(8,128)(2,1)}, bf16[624,256]{1,0:T(8,128)(2,1)S(1)}, u32[]{:S(2)}, u32[]{:S(2)}) collective-permute-start(bf16[624,256]{1,0:T(8,128)(2,1)} %get-tuple-element.49), channel_id=1, source_target_pairs={{0,1},{1,2},{2,3},{3,4},{4,5},{5,6},{6,7},{7,0},{8,9},{9,10},{10,1... | collective-permute-start | bytes 958472 | tf_op jit(solution)/shard_map/ppermute | solution.py:514
  41.1 3.3 %collective-permute-start.2 = (bf16[624,256]{1,0:T(8,128)(2,1)}, bf16[624,256]{1,0:T(8,128)(2,1)S(1)}, u32[]{:S(2)}, u32[]{:S(2)}) collective-permute-start(bf16[624,256]{1,0:T(8,128)(2,1)} %get-tuple-element.50), channel_id=1, source_target_pairs={{0,7},{1,0},{2,1},{3,2},{4,3},{5,4},{6,5},{7,6},{8,15},{9,8},{10,9... | collective-permute-start | bytes 958472 | tf_op jit(solution)/shard_map/ppermute | solution.py:514
  44.3 3.8 %collective-permute-start.4 = (bf16[624,256]{1,0:T(8,128)(2,1)}, bf16[624,256]{1,0:T(8,128)(2,1)S(1)}, u32[]{:S(2)}, u32[]{:S(2)}) collective-permute-start(bf16[624,256]{1,0:T(8,128)(2,1)} %get-tuple-element.52), channel_id=1, source_target_pairs={{0,5},{1,6},{2,7},{3,0},{4,1},{5,2},{6,3},{7,4},{8,13},{9,14},{10,... | collective-permute-start | bytes 958472 | tf_op jit(solution)/shard_map/ppermute | solution.py:514
  48.1 8.6 %collective-permute-done.refs_1_ = bf16[624,256]{1,0:T(8,128)(2,1)S(1)} collective-permute-done((bf16[624,256]{1,0:T(8,128)(2,1)}, bf16[624,256]{1,0:T(8,128)(2,1)S(1)}, u32[]{:S(2)}, u32[]{:S(2)}) %collective-permute-start) | collective-permute-done | bytes 319520 | tf_op jit(solution)/shard_map/ppermute | solution.py:514
  56.7 6.1 %collective-permute-start.5 = (bf16[624,256]{1,0:T(8,128)(2,1)}, bf16[624,256]{1,0:T(8,128)(2,1)S(1)}, u32[]{:S(2)}, u32[]{:S(2)}) collective-permute-start(bf16[624,256]{1,0:T(8,128)(2,1)} %get-tuple-element.67), channel_id=1, source_target_pairs={{0,2},{1,3},{2,4},{3,5},{4,6},{5,7},{6,0},{7,1},{8,10},{9,11},{10,... | collective-permute-start | bytes 958472 | tf_op jit(solution)/shard_map/ppermute | solution.py:514
  62.9 3.0 %collective-permute-start.6 = (bf16[624,256]{1,0:T(8,128)(2,1)}, bf16[624,256]{1,0:T(8,128)(2,1)S(1)}, u32[]{:S(2)}, u32[]{:S(2)}) collective-permute-start(bf16[624,256]{1,0:T(8,128)(2,1)} %get-tuple-element.68), channel_id=1, source_target_pairs={{0,6},{1,7},{2,0},{3,1},{4,2},{5,3},{6,4},{7,5},{8,14},{9,15},{10,... | collective-permute-start | bytes 958472 | tf_op jit(solution)/shard_map/ppermute | solution.py:514
  65.9 0.1 fusion
  66.0 0.7 reduce_max.9
  67.9 0.7 conditional.2
  67.9 0.7 broadcast.4
  68.7 0.8 conditional.3
  68.7 0.8 broadcast.5
  69.5 1.3 %weights.1 = (f32[8,352]{1,0:T(8,128)S(1)}, f32[8,240]{1,0:T(8,128)S(1)}, f32[8,208]{1,0:T(8,128)S(1)}, bf16[8,256,256]{2,1,0:T(8,128)(2,1)S(1)}) custom-call(s32[1]{0:T(128)} %bitcast.refs_0_.here_ref, bf16[8,224,256]{2,1,0:T(8,128)(2,1)S(1)} %all-to-all-done.2.meta_ref.refs_0_, s32[2,352]{1,0:T(2,128)S(1)} %copy-done.4, s32[2,240]{1,0:T(2,128)S(1)} %copy-done.6, ...), custom_call_target="tpu_custom_call" | custom-call | tf_op jit(solution)/shard_map/weights/pallas_call | solution.py:447
  70.9 2.9 %cross.3.refs_10_ = f32[64,256]{1,0:T(8,128)S(1)} custom-call(s32[1]{0:T(128)} %bitcast.refs_0_.here_ref, bf16[8,224,256]{2,1,0:T(8,128)(2,1)S(1)} %all-to-all-done.2.meta_ref.refs_0_, bf16[8,64,256]{2,1,0:T(8,128)(2,1)} %get-tuple-element.71.refs_1_.refs_6_.refs_8_, bf16[8,128,256]{2,1,0:T(8,128)(2,1)} %get-tuple-element.72.refs_2_.refs_7_.refs_9_, ...), custom_call_target="tpu_custom_call" | custom-call | flops 5767168 | bytes 2883584 | tf_op jit(solution)/shard_map/cross/pallas_call | solution.py:392
  73.8 9.5 %collective-permute-done.3.refs_4_ = bf16[624,256]{1,0:T(8,128)(2,1)S(1)} collective-permute-done((bf16[624,256]{1,0:T(8,128)(2,1)}, bf16[624,256]{1,0:T(8,128)(2,1)S(1)}, u32[]{:S(2)}, u32[]{:S(2)}) %collective-permute-start.3) | collective-permute-done | bytes 319520 | tf_op jit(solution)/shard_map/ppermute | solution.py:514
  83.3 4.5 %cross.4 = (f32[64,256]{1,0:T(8,128)S(1)}, bf16[768,256]{1,0:T(8,128)(2,1)S(1)}, bf16[768,256]{1,0:T(8,128)(2,1)S(1)}, bf16[768,256]{1,0:T(8,128)(2,1)S(1)}, bf1...) custom-call(s32[1]{0:T(128)} %bitcast.refs_0_.here_ref, ...), custom_call_target="tpu_custom_call" | custom-call | flops 11796480 | bytes 5898240 | tf_op jit(solution)/shard_map/cross/pallas_call | solution.py:392
  87.8 3.0 %cross.5 = bf16[4,64,256]{2,1,0:T(8,128)(2,1)S(1)} custom-call(s32[1]{0:T(128)} %bitcast.refs_0_.here_ref, bf16[768,256]{1,0:T(8,128)(2,1)S(1)} %get-tuple-element.61.refs_0_, bf16[768,256]{1,0:T(8,128)(2,1)S(1)} %get-tuple-element.62.refs_1_, bf16[768,256]{1,0:T(8,128)(2,1)S(1)} %get-tuple-element.63.refs_2_, ...), custom_call_target="tpu_custom_call" | custom-call | flops 10223616 | bytes 5111808 | tf_op jit(solution)/shard_map/cross/pallas_call | solution.py:392
  90.8 19.3 %all_to_all.20.stacks_ref = bf16[32,8,256]{2,1,0:T(8,128)(2,1)S(1)} all-to-all(bf16[32,8,256]{2,1,0:T(8,128)(2,1)S(1)} %bitcast.5), channel_id=1, replica_groups=mesh['seg'=4,'chan'=8] {'seg','chan'}, dimensions={0} | all-to-all | bytes 262144 | tf_op jit(solution)/shard_map/all_to_all | solution.py:589
  110.1 1.2 %lags.1 = f32[8,2048]{1,0:T(8,128)} custom-call(bf16[32,8,256]{2,1,0:T(8,128)(2,1)S(1)} %all_to_all.20.stacks_ref, bf16[512,512]{1,0:T(8,128)(2,1)S(1)} %copy-done.2, bf16[512,512]{1,0:T(8,128)(2,1)S(1)} %copy-done.1, bf16[1024,1024]{1,0:T(8,128)(2,1)S(1)} %copy-done), custom_call_target="tpu_custom_call" | custom-call | tf_op jit(solution)/shard_map/lags/pallas_call | solution.py:490
  (24 shorter events, 0.1 us)
Async XLA Ops:
  9.4 56.4 %all-to-all-start.2 = ((bf16[8,224,256]{2,1,0:T(8,128)(2,1)}), bf16[8,224,256]{2,1,0:T(8,128)(2,1)S(1)}, u32[]{:S(2)}, u32[]{:S(2)}) async-start(bf16[8,224,256]{2,1,0:T(8,128)(2,1)} %get-tuple-element.53), calls=%async_computation.2 | async-start | bytes 1835008 | tf_op jit(solution)/shard_map/all_to_all | solution.py:509
  16.7 52.8 %copy-start.4 = (s32[2,352]{1,0:T(2,128)S(1)}, s32[2,352]{1,0:T(2,128)}, u32[]{:S(2)}) copy-start(s32[2,352]{1,0:T(2,128)} %constant.34.clone.refs_0_) | copy-start | bytes 8452
  16.8 52.8 %copy-start.5 = (s32[2,208]{1,0:T(2,128)S(1)}, s32[2,208]{1,0:T(2,128)}, u32[]{:S(2)}) copy-start(s32[2,208]{1,0:T(2,128)} %constant.36.clone.refs_2_) | copy-start | bytes 4996
  16.8 52.7 %copy-start.6 = (s32[2,240]{1,0:T(2,128)S(1)}, s32[2,240]{1,0:T(2,128)}, u32[]{:S(2)}) copy-start(s32[2,240]{1,0:T(2,128)} %constant.35.clone.refs_1_) | copy-start | bytes 5764
  36.6 46.7 %copy-start.3 = (bf16[624,256]{1,0:T(8,128)(2,1)S(1)}, bf16[624,256]{1,0:T(8,128)(2,1)}, u32[]{:S(2)}) copy-start(bf16[624,256]{1,0:T(8,128)(2,1)} %get-tuple-element.47.refs_0_) | copy-start | bytes 958468
  36.6 20.1 %collective-permute-start = (bf16[624,256]{1,0:T(8,128)(2,1)}, bf16[624,256]{1,0:T(8,128)(2,1)S(1)}, u32[]{:S(2)}, u32[]{:S(2)}) collective-permute-start(bf16[624,256]{1,0:T(8,128)(2,1)} %get-tuple-element.48), channel_id=1, source_target_pairs={{0,4},{1,5},{2,6},{3,7},{4,0},{5,1},{6,2},{7,3},{8,12},{9,13},{10,... | collective-permute-start | bytes 958472 | tf_op jit(solution)/shard_map/ppermute | solution.py:514
  39.6 23.3 %collective-permute-start.1 = (bf16[624,256]{1,0:T(8,128)(2,1)}, bf16[624,256]{1,0:T(8,128)(2,1)S(1)}, u32[]{:S(2)}, u32[]{:S(2)}) collective-permute-start(bf16[624,256]{1,0:T(8,128)(2,1)} %get-tuple-element.49), channel_id=1, source_target_pairs={{0,1},{1,2},{2,3},{3,4},{4,5},{5,6},{6,7},{7,0},{8,9},{9,10},{10,1... | collective-permute-start | bytes 958472 | tf_op jit(solution)/shard_map/ppermute | solution.py:514
  41.1 32.7 %collective-permute-start.2 = (bf16[624,256]{1,0:T(8,128)(2,1)}, bf16[624,256]{1,0:T(8,128)(2,1)S(1)}, u32[]{:S(2)}, u32[]{:S(2)}) collective-permute-start(bf16[624,256]{1,0:T(8,128)(2,1)} %get-tuple-element.50), channel_id=1, source_target_pairs={{0,7},{1,0},{2,1},{3,2},{4,3},{5,4},{6,5},{7,6},{8,15},{9,8},{10,9... | collective-permute-start | bytes 958472 | tf_op jit(solution)/shard_map/ppermute | solution.py:514
  44.3 39.0 %collective-permute-start.3 = (bf16[624,256]{1,0:T(8,128)(2,1)}, bf16[624,256]{1,0:T(8,128)(2,1)S(1)}, u32[]{:S(2)}, u32[]{:S(2)}) collective-permute-start(bf16[624,256]{1,0:T(8,128)(2,1)} %get-tuple-element.51), channel_id=1, source_target_pairs={{0,3},{1,4},{2,5},{3,6},{4,7},{5,0},{6,1},{7,2},{8,11},{9,12},{10,... | collective-permute-start | bytes 958472 | tf_op jit(solution)/shard_map/ppermute | solution.py:514
  44.3 39.0 %collective-permute-start.4 = (bf16[624,256]{1,0:T(8,128)(2,1)}, bf16[624,256]{1,0:T(8,128)(2,1)S(1)}, u32[]{:S(2)}, u32[]{:S(2)}) collective-permute-start(bf16[624,256]{1,0:T(8,128)(2,1)} %get-tuple-element.52), channel_id=1, source_target_pairs={{0,5},{1,6},{2,7},{3,0},{4,1},{5,2},{6,3},{7,4},{8,13},{9,14},{10,... | collective-permute-start | bytes 958472 | tf_op jit(solution)/shard_map/ppermute | solution.py:514
  56.7 31.1 %collective-permute-start.5 = (bf16[624,256]{1,0:T(8,128)(2,1)}, bf16[624,256]{1,0:T(8,128)(2,1)S(1)}, u32[]{:S(2)}, u32[]{:S(2)}) collective-permute-start(bf16[624,256]{1,0:T(8,128)(2,1)} %get-tuple-element.67), channel_id=1, source_target_pairs={{0,2},{1,3},{2,4},{3,5},{4,6},{5,7},{6,0},{7,1},{8,10},{9,11},{10,... | collective-permute-start | bytes 958472 | tf_op jit(solution)/shard_map/ppermute | solution.py:514
  62.9 24.9 %collective-permute-start.6 = (bf16[624,256]{1,0:T(8,128)(2,1)}, bf16[624,256]{1,0:T(8,128)(2,1)S(1)}, u32[]{:S(2)}, u32[]{:S(2)}) collective-permute-start(bf16[624,256]{1,0:T(8,128)(2,1)} %get-tuple-element.68), channel_id=1, source_target_pairs={{0,6},{1,7},{2,0},{3,1},{4,2},{5,3},{6,4},{7,5},{8,14},{9,15},{10,... | collective-permute-start | bytes 958472 | tf_op jit(solution)/shard_map/ppermute | solution.py:514
  69.5 18.3 %copy-start.7 = (bf16[8,128,256]{2,1,0:T(8,128)(2,1)S(1)}, bf16[8,128,256]{2,1,0:T(8,128)(2,1)}, u32[]{:S(2)}) copy-start(bf16[8,128,256]{2,1,0:T(8,128)(2,1)} %get-tuple-element.72.refs_2_.refs_7_.refs_9_) | copy-start | bytes 1572868
  69.5 18.3 %copy-start.8 = (bf16[8,64,256]{2,1,0:T(8,128)(2,1)S(1)}, bf16[8,64,256]{2,1,0:T(8,128)(2,1)}, u32[]{:S(2)}) copy-start(bf16[8,64,256]{2,1,0:T(8,128)(2,1)} %get-tuple-element.71.refs_1_.refs_6_.refs_8_) | copy-start | bytes 786436
  83.3 26.8 %copy-start = (bf16[1024,1024]{1,0:T(8,128)(2,1)S(1)}, bf16[1024,1024]{1,0:T(8,128)(2,1)}, u32[]{:S(2)}) copy-start(bf16[1024,1024]{1,0:T(8,128)(2,1)} %constant.39.clone.odd_ref) | copy-start | bytes 6291460
  83.3 26.8 %copy-start.1 = (bf16[512,512]{1,0:T(8,128)(2,1)S(1)}, bf16[512,512]{1,0:T(8,128)(2,1)}, u32[]{:S(2)}) copy-start(bf16[512,512]{1,0:T(8,128)(2,1)} %constant.38.clone.two_ref) | copy-start | bytes 1572868
  83.3 26.8 %copy-start.2 = (bf16[512,512]{1,0:T(8,128)(2,1)S(1)}, bf16[512,512]{1,0:T(8,128)(2,1)}, u32[]{:S(2)}) copy-start(bf16[512,512]{1,0:T(8,128)(2,1)} %constant.37.clone.zero_ref) | copy-start | bytes 1572868
